TPU v7x, 128 devices: a whole 4x4x4 slice. The times are simulated.
128 devices in a mesh: seq: 16 (over x_hi, z, core), head: 8 (over y, x_lo).
Axes of the slice: x: 4 (x_hi: 2, x_lo: 2; x = x_hi * 2 + x_lo), y: 4, z: 4, core: 2. Of those that a mesh axis runs over, the one named last changes fastest.
Arguments:
- prompt_query: bfloat16 [1024, 8192], P('seq', 'head'), may hold values from -16 to 16
- prompt_key: bfloat16 [1024, 1024], P('seq', 'head'), may hold values from -16 to 16
- prompt_value: bfloat16 [1024, 1024], P('seq', 'head'), may hold values from -6 to 6
- reply_query: bfloat16 [8192, 8192], P('seq', 'head'), may hold values from -16 to 16
- reply_key: bfloat16 [8192, 1024], P('seq', 'head'), may hold values from -6 to 6
- reply_value: bfloat16 [8192, 1024], P('seq', 'head'), may hold values from -6 to 6
- lengths: int32 [16], P('seq'), may hold values from 128 to 512, as said below
- out_weight: bfloat16 [8192, 5120], P('head', 'seq'), may hold values from -0.25 to 0.25
- prompt_grad: bfloat16 [1024, 5120], P('seq'), may hold values from -6 to 6
- reply_grad: bfloat16 [8192, 5120], P('seq'), may hold values from -6 to 6
Outputs:
- prompt_output: bfloat16 [1024, 5120], P('seq', 'head')
- reply_output: bfloat16 [8192, 5120], P('seq', 'head')
- prompt_query_grad: bfloat16 [1024, 8192], P('seq', 'head')
- prompt_key_grad: bfloat16 [1024, 1024], P('seq', 'head')
- prompt_value_grad: bfloat16 [1024, 1024], P('seq', 'head')
- reply_query_grad: bfloat16 [8192, 8192], P('seq', 'head')
- reply_key_grad: bfloat16 [8192, 1024], P('seq', 'head')
- reply_value_grad: bfloat16 [8192, 1024], P('seq', 'head')
Inputs may be any that keep to these rules, and one draw needn't show every extreme that they name: `lengths`: multiples of 128; some response has 512 tokens and some 128.
All inputs are finite; a program needn't handle non-finite values.
Results may differ from a plain program's by a relative error of at most 0.029.
Values may be sent and summed in bfloat16 or wider, within the bound.
No kernel may reach another device: no remote copies, remote signals or barrier semaphores. Data moves between devices by JAX's collectives and lax.ppermute only.
A program may use at most 128 MiB of HBM per device.

v0:
```python
import jax
import jax.numpy as jnp
from jax import lax
from jax.sharding import PartitionSpec as P

HEADS = 64
KV_HEADS = 8
HEAD_DIM = 128


def visible_keys(index, length, prompt_rows, reply_rows, prompt_len):
    row_ids = jnp.arange(prompt_rows + reply_rows, dtype=jnp.int32)
    column = jnp.arange(prompt_len + reply_rows, dtype=jnp.int32)
    prompt_row = row_ids < prompt_rows
    position = index * prompt_rows + row_ids
    offset = row_ids - prompt_rows
    prompt_col = column < prompt_len
    own_col = column - prompt_len
    allowed = jnp.where(
        prompt_row[:, None],
        prompt_col[None, :] & (column[None, :] <= position[:, None]),
        prompt_col[None, :] | (own_col[None, :] <= offset[:, None]),
    )
    live = prompt_row | (offset < length)
    return (allowed, live)


def back_project(grads, weight_cols):
    return lax.dot_general(
        grads, weight_cols, (((1,), (1,)), ((), ())), preferred_element_type=jnp.float32
    )


def head_attention(carry, item, key_heads, value_heads, allowed, live, scale):
    key_grad, value_grad = carry
    query, grad, slot = item
    key_block = lax.dynamic_index_in_dim(key_heads, slot, 0, keepdims=False)
    value_block = lax.dynamic_index_in_dim(value_heads, slot, 0, keepdims=False)
    scores = jnp.einsum("rd,kd->rk", query, key_block, preferred_element_type=jnp.float32) * scale
    scores = jnp.where(allowed, scores, -jnp.inf)
    highest = jnp.max(scores, axis=1, keepdims=True)
    raised = jnp.where(allowed, jnp.exp(scores - highest), 0.0)
    shares = raised / jnp.sum(raised, axis=1, keepdims=True)
    weights = shares.astype(jnp.bfloat16)
    attended = jnp.einsum("rk,kd->rd", weights, value_block, preferred_element_type=jnp.float32)
    attended = jnp.where(live[:, None], attended, 0.0).astype(jnp.bfloat16)
    delta = jnp.sum(grad.astype(jnp.float32) * attended.astype(jnp.float32), axis=1, keepdims=True)
    weight_grad = jnp.einsum("rd,kd->rk", grad, value_block, preferred_element_type=jnp.float32)
    score_grad = (shares * (weight_grad - delta)).astype(jnp.bfloat16)
    query_grad = (
        jnp.einsum("rk,kd->rd", score_grad, key_block, preferred_element_type=jnp.float32) * scale
    ).astype(jnp.bfloat16)
    key_term = (
        jnp.einsum("rk,rd->kd", score_grad, query, preferred_element_type=jnp.float32) * scale
    )
    value_term = jnp.einsum("rk,rd->kd", weights, grad, preferred_element_type=jnp.float32)
    key_grad = lax.dynamic_update_index_in_dim(
        key_grad, lax.dynamic_index_in_dim(key_grad, slot, 0, keepdims=False) + key_term, slot, 0
    )
    value_grad = lax.dynamic_update_index_in_dim(
        value_grad,
        lax.dynamic_index_in_dim(value_grad, slot, 0, keepdims=False) + value_term,
        slot,
        0,
    )
    return ((key_grad, value_grad), (attended, query_grad))


def body(
    prompt_query,
    prompt_key,
    prompt_value,
    reply_query,
    reply_key,
    reply_value,
    lengths,
    out_weight,
    prompt_grad,
    reply_grad,
):
    scale = HEAD_DIM ** (-0.5)
    prompt_rows = prompt_query.shape[0]
    reply_rows = reply_query.shape[0]
    rows = prompt_rows + reply_rows
    head_cols = prompt_query.shape[1]
    head_count = head_cols // HEAD_DIM
    kv_count = prompt_key.shape[1] // HEAD_DIM
    prompt_keys, prompt_values = (
        lax.all_gather(prompt_key, "seq", axis=0, tiled=True),
        lax.all_gather(prompt_value, "seq", axis=0, tiled=True),
    )
    weight_full = lax.all_gather(out_weight, "seq", axis=1, tiled=True)
    upstream = jnp.concatenate(
        [back_project(prompt_grad, weight_full), back_project(reply_grad, weight_full)], 0
    )
    prompt_len = prompt_keys.shape[0]
    allowed, live = visible_keys(
        lax.axis_index("seq"), lengths[0], prompt_rows, reply_rows, prompt_len
    )
    upstream = jnp.where(live[:, None], upstream.astype(jnp.bfloat16), jnp.zeros((), jnp.bfloat16))
    queries = jnp.concatenate([prompt_query, reply_query], 0)
    keys = jnp.concatenate([prompt_keys, reply_key], 0)
    values = jnp.concatenate([prompt_values, reply_value], 0)
    key_count = keys.shape[0]
    key_heads = keys.reshape(key_count, kv_count, HEAD_DIM).transpose(1, 0, 2)
    value_heads = values.reshape(key_count, kv_count, HEAD_DIM).transpose(1, 0, 2)
    query_heads = queries.reshape(rows, head_count, HEAD_DIM).transpose(1, 0, 2)
    grad_heads = upstream.reshape(rows, head_count, HEAD_DIM).transpose(1, 0, 2)
    slots = jnp.arange(head_count, dtype=jnp.int32) // (HEADS // KV_HEADS)
    start_grads = (
        jnp.zeros((kv_count, key_count, HEAD_DIM), jnp.float32),
        jnp.zeros((kv_count, key_count, HEAD_DIM), jnp.float32),
    )

    def head_step(carry, item):
        return head_attention(carry, item, key_heads, value_heads, allowed, live, scale)

    (key_grad, value_grad), (attended, query_grad) = lax.scan(
        head_step, start_grads, (query_heads, grad_heads, slots)
    )
    attended = attended.transpose(1, 0, 2).reshape(rows, head_cols)
    query_grad = query_grad.transpose(1, 0, 2).reshape(rows, head_cols)
    key_grad = key_grad.transpose(1, 0, 2).reshape(key_count, kv_count * HEAD_DIM)
    value_grad = value_grad.transpose(1, 0, 2).reshape(key_count, kv_count * HEAD_DIM)
    prompt_key_grad, prompt_value_grad = (
        lax.psum_scatter(
            key_grad[:prompt_len].astype(jnp.bfloat16), "seq", scatter_dimension=0, tiled=True
        ).astype(jnp.float32),
        lax.psum_scatter(
            value_grad[:prompt_len].astype(jnp.bfloat16), "seq", scatter_dimension=0, tiled=True
        ).astype(jnp.float32),
    )
    group_term = jnp.dot(attended, weight_full, preferred_element_type=jnp.float32)
    total = lax.psum(group_term.astype(jnp.bfloat16), "head").astype(jnp.float32)
    share_width = total.shape[1] // lax.axis_size("head")
    mixed = lax.dynamic_slice_in_dim(total, lax.axis_index("head") * share_width, share_width, 1)
    mixed = mixed.astype(jnp.bfloat16)
    return (
        mixed[:prompt_rows],
        mixed[prompt_rows:],
        query_grad[:prompt_rows],
        prompt_key_grad.astype(jnp.bfloat16),
        prompt_value_grad.astype(jnp.bfloat16),
        query_grad[prompt_rows:],
        key_grad[prompt_len:].astype(jnp.bfloat16),
        value_grad[prompt_len:].astype(jnp.bfloat16),
    )


def solution(mesh):
    in_specs = (
        P("seq", "head"),
        P("seq", "head"),
        P("seq", "head"),
        P("seq", "head"),
        P("seq", "head"),
        P("seq", "head"),
        P("seq"),
        P("head", "seq"),
        P("seq", None),
        P("seq", None),
    )
    out_specs = (
        P("seq", "head"),
        P("seq", "head"),
        P("seq", "head"),
        P("seq", "head"),
        P("seq", "head"),
        P("seq", "head"),
        P("seq", "head"),
        P("seq", "head"),
    )
    return jax.shard_map(body, mesh=mesh, in_specs=in_specs, out_specs=out_specs, check_vma=False)
```

profile of v0, /device:TPU:1, one launch (start us, length us, event | category | flops | bytes accessed | tf_op | source)
XLA Modules:
  0.0 633.3 jit_solution(8613465583347035100)
XLA Ops:
  11.6 28.0 %all_gather.9 = bf16[1024,128]{1,0:T(8,128)(2,1)S(1)} all-gather(bf16[64,128]{1,0:T(8,128)(2,1)S(1)} %copy-done.5), channel_id=1, replica_groups=mesh['seq'=16,'head'=8] {'seq'}, dimensions={0}, use_global_device_ids=true | all-gather | bytes 278528 | tf_op jit(solution)/shard_map/all_gather | solution.py:89
  39.6 20.1 %all_gather.11 = bf16[1024,128]{1,0:T(8,128)(2,1)S(1)} all-gather(bf16[64,128]{1,0:T(8,128)(2,1)S(1)} %copy-done.6), channel_id=1, replica_groups=mesh['seq'=16,'head'=8] {'seq'}, dimensions={0}, use_global_device_ids=true | all-gather | bytes 278528 | tf_op jit(solution)/shard_map/all_gather | solution.py:90
  59.8 37.0 %all-gather.2.cloned.1.call-done = bf16[1024,5120]{0,1:T(8,128)(2,1)} async-done(((bf16[1024,320]{0,1:T(8,128)(2,1)}), bf16[1024,5120]{0,1:T(8,128)(2,1)}) %all-gather.2.cloned.1.call-update) | async-done | bytes 10485776 | tf_op jit(solution)/shard_map/all_gather | solution.py:92
  96.7 10.0 %fusion.34 = bf16[64,8,8,128]{3,2,1,0:T(8,128)(2,1)S(1)} fusion(bf16[512,5120]{1,0:T(8,128)(2,1)} %param.21, bf16[1024,5120]{0,1:T(8,128)(2,1)} %all-gather.2.cloned.1.call-done), kind=kOutput, calls=%fused_computation.47 | convolution fusion | flops 5369233408 | bytes 16777216 | tf_op jit(solution)/shard_map/dot_general | solution.py:29
  106.9 2.0 fusion.38
  110.4 124.2 %while.18 = (s32[]{:T(128)}, f32[1,1536,128]{2,1,0:T(8,128)S(1)}, f32[1,1536,128]{2,1,0:T(8,128)S(1)}, bf16[8,576,128]{2,1,0:T(8,128)(2,1)}, bf16[8,576,128]{2,1...) while((s32[]{:T(128)}, f32[1,1536,128]{2,1,0:T(8,128)S(1)}, ...), condition=%wide.region_4.5_spmd.clone, body=%wide.region_0.4_spmd.clone.sunk | while | flops 1385792000 | bytes 36185820 | solution.py:118
  110.4 2.6 fusion.71
  113.0 1.8 fusion.72
  114.8 2.0 fusion.73
  117.4 1.6 multiply_reduce_fusion.2
  119.0 1.6 multiply_convert_fusion.2
  121.9 1.7 fusion.75
  124.2 1.7 fusion.76
  125.9 2.6 fusion.71
  128.5 1.8 fusion.72
  130.3 2.0 fusion.73
  132.9 1.6 multiply_reduce_fusion.2
  134.6 1.6 multiply_convert_fusion.2
  137.4 1.7 fusion.75
  139.8 1.7 fusion.76
  141.5 2.6 fusion.71
  144.0 1.8 fusion.72
  145.8 2.0 fusion.73
  148.5 1.6 multiply_reduce_fusion.2
  153.0 1.7 fusion.75
  155.3 1.7 fusion.76
  157.0 2.6 fusion.71
  159.6 1.8 fusion.72
  161.4 2.0 fusion.73
  164.0 1.6 multiply_reduce_fusion.2
  165.6 1.6 multiply_convert_fusion.2
  168.5 1.7 fusion.75
  170.8 1.7 fusion.76
  172.5 2.6 fusion.71
  175.1 1.8 fusion.72
  176.9 2.0 fusion.73
  179.5 1.6 multiply_reduce_fusion.2
  181.2 1.6 multiply_convert_fusion.2
  184.0 1.7 fusion.75
  186.4 1.7 fusion.76
  188.1 2.6 fusion.71
  190.6 1.8 fusion.72
  192.4 2.0 fusion.73
  195.0 1.6 multiply_reduce_fusion.2
  196.7 1.6 multiply_convert_fusion.2
  199.5 1.7 fusion.75
  201.9 1.7 fusion.76
  203.6 2.6 fusion.71
  206.1 1.8 fusion.72
  207.9 2.0 fusion.73
  210.6 1.6 multiply_reduce_fusion.2
  212.2 1.6 multiply_convert_fusion.2
  215.0 1.7 fusion.75
  217.4 1.7 fusion.76
  219.1 2.6 fusion.71
  221.7 1.8 fusion.72
  223.4 2.0 fusion.73
  226.1 1.6 multiply_reduce_fusion.2
  230.6 1.7 fusion.75
  232.9 1.7 fusion.76
  234.6 11.2 %convolution_convert_fusion = bf16[576,5120]{1,0:T(8,128)(2,1)} fusion(bf16[1024,5120]{0,1:T(8,128)(2,1)} %all-gather.2.cloned.1.call-done, bf16[8,576,128]{2,1,0:T(8,128)(2,1)} %get-tuple-element.94), kind=kOutput, calls=%fused_computation.44 | convolution fusion | flops 6042746880 | bytes 17563648 | tf_op jit(solution)/shard_map/dot_general | solution.py:133
  250.6 238.5 %all-reduce.2.cloned.1.call-done = bf16[576,5120]{1,0:T(8,128)(2,1)} async-done(((bf16[576,5120]{1,0:T(8,128)(2,1)}), bf16[576,5120]{1,0:T(8,128)(2,1)}) %all-reduce.2.cloned.1.call-update) | async-done | bytes 5898256 | tf_op jit(solution)/shard_map/psum | solution.py:134
  491.9 66.2 %reduce-scatter.3.cloned.1.call-done = bf16[64,128]{1,0:T(8,128)(2,1)} async-done(((bf16[1024,128]{1,0:T(8,128)(2,1)}), bf16[64,128]{1,0:T(8,128)(2,1)}) %reduce-scatter.3.cloned.1.call-update) | async-done | bytes 16400 | tf_op jit(solution)/shard_map/reduce_scatter | solution.py:126
  558.1 68.7 %reduce-scatter.5.cloned.1.call-done = bf16[64,128]{1,0:T(8,128)(2,1)} async-done(((bf16[1024,128]{1,0:T(8,128)(2,1)}), bf16[64,128]{1,0:T(8,128)(2,1)}) %reduce-scatter.5.cloned.1.call-update) | async-done | bytes 16400 | tf_op jit(solution)/shard_map/reduce_scatter | solution.py:129
  (76 shorter events, 36.9 us)
Async XLA Ops:
  7.2 99.7 %copy-start = (bf16[64,5120]{1,0:T(8,128)(2,1)S(1)}, bf16[64,5120]{1,0:T(8,128)(2,1)}, u32[]{:S(2)}) copy-start(bf16[64,5120]{1,0:T(8,128)(2,1)} %param.20) | copy-start | bytes 1966084
  7.2 89.5 %all-gather.2.cloned.1.call-start = ((), (), s32[]{:S(2)}) async-start(), calls=%async_computation.2 | async-start | bytes 11141120 | tf_op jit(solution)/shard_map/all_gather | solution.py:92
  7.9 481.3 %all-reduce.2.cloned.1.call-start = ((), (), s32[]{:S(2)}) async-start(), calls=%async_computation.3 | async-start | bytes 11796480 | tf_op jit(solution)/shard_map/psum | solution.py:134
  10.0 1.6 copy-start.5
  10.0 29.6 %copy-start.6 = (bf16[64,128]{1,0:T(8,128)(2,1)S(1)}, bf16[64,128]{1,0:T(8,128)(2,1)}, u32[]{:S(2)}) copy-start(bf16[64,128]{1,0:T(8,128)(2,1)} %param.14) | copy-start | bytes 49156
  10.0 49.7 %copy-start.3 = (bf16[512,128]{1,0:T(8,128)(2,1)S(1)}, bf16[512,128]{1,0:T(8,128)(2,1)}, u32[]{:S(2)}) copy-start(bf16[512,128]{1,0:T(8,128)(2,1)} %param.16) | copy-start | bytes 393220
  10.3 49.4 %copy-start.4 = (bf16[512,128]{1,0:T(8,128)(2,1)S(1)}, bf16[512,128]{1,0:T(8,128)(2,1)}, u32[]{:S(2)}) copy-start(bf16[512,128]{1,0:T(8,128)(2,1)} %param.17) | copy-start | bytes 393220
  96.7 10.2 %copy-start.1 = (bf16[1024,5120]{0,1:T(8,128)(2,1)S(1)}, bf16[1024,5120]{0,1:T(8,128)(2,1)}, u32[]{:S(2)}) copy-start(bf16[1024,5120]{0,1:T(8,128)(2,1)} %all-gather.2.cloned.1.call-done) | copy-start | bytes 31457284
  245.8 2.3 copy-start.2
  245.8 312.3 %reduce-scatter.3.cloned.1.call-start = ((), (), s32[]{:S(2)}) async-start(), calls=%async_computation.4 | async-start | bytes 278528 | tf_op jit(solution)/shard_map/reduce_scatter | solution.py:126
  248.0 378.8 %reduce-scatter.5.cloned.1.call-start = ((), (), s32[]{:S(2)}) async-start(), calls=%async_computation.5 | async-start | bytes 278528 | tf_op jit(solution)/shard_map/reduce_scatter | solution.py:129
Sparse Core Ops, SparseCore 0:
  10.5 86.1 all-gather.1
  245.9 243.2 all-reduce.1
  493.9 64.1 reduce-scatter.2
  562.6 64.1 reduce-scatter.4
where the time goes:
time: 635 us; the launch traced here: 633 us
  waiting for transfers between devices  411 us (65%)
  matrix products  106 us (17%)
  blocking collectives  48.1 us (8%)
  other arithmetic  39.3 us (6%)
  between operations  14.6 us (2%)
  local copies, waits for them, and re-layouts  13.4 us (2%)
    psum x1, waiting for transfers between devices, body(): lax.psum(group_term.astype(jnp.bfloat16), 'head').astype(jnp.float32)  239 us
    reduce_scatter x1, waiting for transfers between devices, body(): lax.psum_scatter(value_grad[:prompt_len].astype(jnp.bfloat16), 'seq', sca...  68.7 us
    reduce_scatter x1, waiting for transfers between devices, body(): lax.psum_scatter(key_grad[:prompt_len].astype(jnp.bfloat16), 'seq', scatt...  66.2 us
    all_gather x1, waiting for transfers between devices, body(): weight_full = lax.all_gather(out_weight, 'seq', axis=1, tiled=True)  37 us
    all_gather x1, blocking collectives, body(): lax.all_gather(prompt_key, 'seq', axis=0, tiled=True)  28 us
    dot_general x8, matrix products, head_attention(): jnp.einsum('rd,kd->rk', query, key_block, preferred_element_type=jnp.floa...  20.6 us
    all_gather x1, blocking collectives, body(): lax.all_gather(prompt_value, 'seq', axis=0, tiled=True)  20.1 us
    div x8, other arithmetic, head_attention(): shares = raised / jnp.sum(raised, axis=1, keepdims=True)  15.7 us
  transfers between devices with their start and end apart: 4, of which 4 were waited for; matrix products, arithmetic and copies ran while one was open for 2% of the time, Pallas kernels for 0%

commit v1 on v0

v1 whole, which is shorter than its diff:
```python
import jax
import jax.numpy as jnp
from jax import lax
from jax.experimental import pallas as pl
from jax.experimental.pallas import tpu as pltpu
from jax.sharding import PartitionSpec as P

DIM = 128
BF = jnp.bfloat16
F32 = jnp.float32
SCALE = DIM**-0.5
EXP_SCALE = SCALE * 1.4426950408889634
VMEM_LIMIT = 44 * 1024 * 1024


def dot_nn(a, b):
    return lax.dot_general(a, b, (((1,), (0,)), ((), ())), preferred_element_type=F32)


def dot_nt(a, b):
    return lax.dot_general(a, b, (((1,), (1,)), ((), ())), preferred_element_type=F32)


def forward_kernel(
    index_ref, length_ref, query_ref, prompt_query_ref, key_ref, value_ref, reply_key_ref, reply_value_ref,
    weight_ref, prompt_weight_ref, out_ref, prompt_out_ref, value_t, scores, stack,
):
    step = pl.program_id(0)
    heads = pl.num_programs(0) - 1
    prompt = key_ref.shape[0]
    rows = query_ref.shape[0]
    keys = prompt + rows
    prompt_rows = prompt_query_ref.shape[0]

    @pl.when(step == 0)
    def _():
        value_t[:, :prompt] = value_ref[...].T
        value_t[:, prompt:] = reply_value_ref[...].T

    @pl.when(step < heads)
    def _():
        query = query_ref[...]
        half = rows // 2
        scores[:prompt, :] = dot_nt(key_ref[...], query)
        scores[prompt : prompt + half, :] = dot_nt(reply_key_ref[:half], query)
        scores[prompt + half :, half:] = dot_nt(reply_key_ref[half:], query[half:])
        seen = lax.broadcasted_iota(jnp.int32, (DIM, DIM), 0) <= lax.broadcasted_iota(jnp.int32, (DIM, DIM), 1)
        for tile in range(rows // DIM):
            lanes = slice(tile * DIM, (tile + 1) * DIM)
            full = prompt + tile * DIM
            wide = scores[:full, lanes]
            diag = jnp.where(seen, scores[full : full + DIM, lanes], -jnp.inf)
            top = jnp.maximum(jnp.max(wide, axis=0, keepdims=True), jnp.max(diag, axis=0, keepdims=True))
            wide = jnp.exp2((wide - top) * EXP_SCALE)
            diag = jnp.exp2((diag - top) * EXP_SCALE)
            total = jnp.sum(wide, axis=0, keepdims=True) + jnp.sum(diag, axis=0, keepdims=True)
            inverse = 1.0 / total
            weight_ref[0, :full, lanes] = (wide * inverse).astype(BF)
            weight_ref[0, full : full + DIM, lanes] = (diag * inverse).astype(BF)
            if full + DIM < keys:
                weight_ref[0, full + DIM :, lanes] = jnp.zeros((keys - full - DIM, DIM), BF)
        out = dot_nn(value_t[...], weight_ref[0]).T
        live = lax.broadcasted_iota(jnp.int32, (rows, DIM), 0) < length_ref[0]
        out_ref[...] = jnp.where(live, out, 0.0).astype(BF)

    @pl.when(step == heads)
    def _():
        for head in range(rows // prompt_rows):
            stack[head * prompt_rows : (head + 1) * prompt_rows, :] = prompt_query_ref[:, head * DIM : (head + 1) * DIM]
        scores[:prompt, :] = dot_nt(key_ref[...], stack[...])
        first = index_ref[0] * prompt_rows
        for tile in range(rows // DIM):
            lanes = slice(tile * DIM, (tile + 1) * DIM)
            place = lax.broadcasted_iota(jnp.int32, (prompt, DIM), 1) % prompt_rows + first
            seen = lax.broadcasted_iota(jnp.int32, (prompt, DIM), 0) <= place
            part = jnp.where(seen, scores[:prompt, lanes], -jnp.inf)
            top = jnp.max(part, axis=0, keepdims=True)
            part = jnp.exp2((part - top) * EXP_SCALE)
            inverse = 1.0 / jnp.sum(part, axis=0, keepdims=True)
            prompt_weight_ref[:, lanes] = (part * inverse).astype(BF)
        out = dot_nn(value_t[:, :prompt], prompt_weight_ref[...]).T.astype(BF)
        for head in range(rows // prompt_rows):
            prompt_out_ref[:, head * DIM : (head + 1) * DIM] = out[head * prompt_rows : (head + 1) * prompt_rows, :]


def attention_forward(index, length, reply_query, prompt_query, kv, reply_key, reply_value):
    rows, columns = reply_query.shape
    prompt_rows = prompt_query.shape[0]
    heads = columns // DIM
    prompt = kv.shape[0]
    keys = prompt + rows
    last = heads - 1
    whole = lambda shape: pl.BlockSpec(shape, lambda g: (0, 0))
    return pl.pallas_call(
        forward_kernel,
        grid=(heads + 1,),
        in_specs=[
            pl.BlockSpec(memory_space=pltpu.SMEM),
            pl.BlockSpec(memory_space=pltpu.SMEM),
            pl.BlockSpec((rows, DIM), lambda g: (0, jnp.minimum(g, last))),
            whole((prompt_rows, columns)),
            pl.BlockSpec((prompt, DIM), lambda g: (0, 0)),
            pl.BlockSpec((prompt, DIM), lambda g: (0, 1)),
            whole((rows, DIM)),
            whole((rows, DIM)),
        ],
        out_specs=[
            pl.BlockSpec((1, keys, rows), lambda g: (jnp.minimum(g, last), 0, 0)),
            whole((prompt, rows)),
            pl.BlockSpec((rows, DIM), lambda g: (0, jnp.minimum(g, last))),
            whole((prompt_rows, columns)),
        ],
        out_shape=[
            jax.ShapeDtypeStruct((heads, keys, rows), BF),
            jax.ShapeDtypeStruct((prompt, rows), BF),
            jax.ShapeDtypeStruct((rows, columns), BF),
            jax.ShapeDtypeStruct((prompt_rows, columns), BF),
        ],
        scratch_shapes=[
            pltpu.VMEM((DIM, keys), BF),
            pltpu.VMEM((keys, rows), F32),
            pltpu.VMEM((rows, DIM), BF),
        ],
        compiler_params=pltpu.CompilerParams(vmem_limit_bytes=VMEM_LIMIT),
        cost_estimate=pl.CostEstimate(flops=4 * heads * keys * rows * DIM, bytes_accessed=18 * 2**20, transcendentals=heads * keys * rows),
        name="attention_forward",
    )(index, length, reply_query, prompt_query, kv, kv, reply_key, reply_value)


def backward_kernel(
    weight_ref, prompt_weight_ref, query_ref, grad_ref, out_ref, prompt_query_ref, prompt_grad_ref, prompt_out_ref,
    key_ref, value_ref, reply_key_ref, reply_value_ref,
    query_grad_ref, prompt_query_grad_ref, kv_grad_ref, reply_key_grad_ref, reply_value_grad_ref,
    key_t, score_grad, key_grad, value_grad, stack,
):
    step = pl.program_id(0)
    heads = pl.num_programs(0) - 1
    prompt = key_ref.shape[0]
    rows = query_ref.shape[0]
    keys = prompt + rows
    half = rows // 2
    prompt_rows = prompt_query_ref.shape[0]

    @pl.when(step == 0)
    def _():
        key_t[:, :prompt] = key_ref[...].T
        key_t[:, prompt:] = reply_key_ref[...].T
        key_grad[...] = jnp.zeros_like(key_grad)
        value_grad[...] = jnp.zeros_like(value_grad)
        score_grad[prompt + half :, :half] = jnp.zeros((half, half), BF)

    def row_delta(grad, out):
        return jnp.sum((grad.astype(F32) * out.astype(F32)).T, axis=0, keepdims=True)

    def key_block(weight, value, grad, query, delta, start, size, low):
        block = slice(start, start + size)
        slope = dot_nt(value, grad)
        part = (weight.astype(F32) * (slope - delta)).astype(BF)
        score_grad[block, low:] = part
        key_grad[block, :] += dot_nn(part, query)
        value_grad[block, :] += dot_nn(weight, grad)

    @pl.when(step < heads)
    def _():
        query, grad = query_ref[...], grad_ref[...]
        delta = row_delta(grad, out_ref[...])
        for start in range(0, prompt, 256):
            key_block(weight_ref[0, start : start + 256, :], value_ref[start : start + 256, :], grad, query, delta, start, 256, 0)
        key_block(weight_ref[0, prompt : prompt + half, :], reply_value_ref[:half], grad, query, delta, prompt, half, 0)
        key_block(
            weight_ref[0, prompt + half :, half:], reply_value_ref[half:], grad[half:], query[half:], delta[:, half:], prompt + half, half, half
        )
        query_grad_ref[...] = (dot_nn(key_t[...], score_grad[...]).T * SCALE).astype(BF)

    @pl.when(step == heads)
    def _():
        count = rows // prompt_rows
        for head in range(count):
            place, lanes = slice(head * prompt_rows, (head + 1) * prompt_rows), slice(head * DIM, (head + 1) * DIM)
            stack[0, place, :] = prompt_query_ref[:, lanes]
            stack[1, place, :] = prompt_grad_ref[:, lanes]
            stack[2, place, :] = prompt_out_ref[:, lanes]
        query, grad = stack[0], stack[1]
        delta = row_delta(grad, stack[2])
        for start in range(0, prompt, 256):
            key_block(prompt_weight_ref[start : start + 256, :], value_ref[start : start + 256, :], grad, query, delta, start, 256, 0)
        result = (dot_nn(key_t[:, :prompt], score_grad[:prompt, :]).T * SCALE).astype(BF)
        for head in range(count):
            prompt_query_grad_ref[:, head * DIM : (head + 1) * DIM] = result[head * prompt_rows : (head + 1) * prompt_rows, :]
        kv_grad_ref[:, :DIM] = (key_grad[:prompt, :] * SCALE).astype(BF)
        kv_grad_ref[:, DIM:] = value_grad[:prompt, :].astype(BF)
        reply_key_grad_ref[...] = (key_grad[prompt:, :] * SCALE).astype(BF)
        reply_value_grad_ref[...] = value_grad[prompt:, :].astype(BF)


def attention_backward(weights, prompt_weights, reply_query, reply_up, reply_att, prompt_query, prompt_up, prompt_att, kv, reply_key, reply_value):
    rows, columns = reply_query.shape
    prompt_rows = prompt_query.shape[0]
    heads = columns // DIM
    prompt = kv.shape[0]
    keys = prompt + rows
    last = heads - 1
    whole = lambda shape: pl.BlockSpec(shape, lambda g: (0, 0))
    column = pl.BlockSpec((rows, DIM), lambda g: (0, jnp.minimum(g, last)))
    return pl.pallas_call(
        backward_kernel,
        grid=(heads + 1,),
        in_specs=[
            pl.BlockSpec((1, keys, rows), lambda g: (jnp.minimum(g, last), 0, 0)),
            whole((prompt, rows)),
            column,
            column,
            column,
            whole((prompt_rows, columns)),
            whole((prompt_rows, columns)),
            whole((prompt_rows, columns)),
            pl.BlockSpec((prompt, DIM), lambda g: (0, 0)),
            pl.BlockSpec((prompt, DIM), lambda g: (0, 1)),
            whole((rows, DIM)),
            whole((rows, DIM)),
        ],
        out_specs=[
            column,
            whole((prompt_rows, columns)),
            whole((prompt, 2 * DIM)),
            whole((rows, DIM)),
            whole((rows, DIM)),
        ],
        out_shape=[
            jax.ShapeDtypeStruct((rows, columns), BF),
            jax.ShapeDtypeStruct((prompt_rows, columns), BF),
            jax.ShapeDtypeStruct((prompt, 2 * DIM), BF),
            jax.ShapeDtypeStruct((rows, DIM), BF),
            jax.ShapeDtypeStruct((rows, DIM), BF),
        ],
        scratch_shapes=[
            pltpu.VMEM((DIM, keys), BF),
            pltpu.VMEM((keys, rows), BF),
            pltpu.VMEM((keys, DIM), F32),
            pltpu.VMEM((keys, DIM), F32),
            pltpu.VMEM((3, rows, DIM), BF),
        ],
        compiler_params=pltpu.CompilerParams(vmem_limit_bytes=VMEM_LIMIT),
        cost_estimate=pl.CostEstimate(flops=8 * heads * keys * rows * DIM, bytes_accessed=18 * 2**20, transcendentals=0),
        name="attention_backward",
    )(weights, prompt_weights, reply_query, reply_up, reply_att, prompt_query, prompt_up, prompt_att, kv, kv, reply_key, reply_value)


def body(prompt_query, prompt_key, prompt_value, reply_query, reply_key, reply_value, lengths, out_weight, prompt_grad, reply_grad):
    prompt_rows = prompt_query.shape[0]
    reply_rows = reply_query.shape[0]
    n_seq, n_head = lax.axis_size("seq"), lax.axis_size("head")
    seq, head = lax.axis_index("seq"), lax.axis_index("head")
    weight = lax.all_gather(out_weight.T, "seq", axis=0, tiled=True)
    own = jnp.concatenate([prompt_key, prompt_value], 1)
    kv = lax.all_to_all(jnp.broadcast_to(own[None], (n_seq,) + own.shape), "seq", 0, 0).reshape(n_seq * prompt_rows, 2 * DIM)
    weights, prompt_weights, reply_att, prompt_att = attention_forward(
        seq.reshape(1).astype(jnp.int32), lengths, reply_query, prompt_query, kv, reply_key, reply_value
    )
    attended = jnp.concatenate([prompt_att, reply_att], 0)
    width = weight.shape[0] // n_head
    mixed = None
    for hop in [7, 6, 5, 4, 3, 2, 1, 0]:
        target = head ^ hop
        block = lax.dynamic_slice_in_dim(weight, target * width, width, 0)
        term = dot_nt(attended, block).astype(BF)
        if hop:
            term = lax.ppermute(term, "head", [(i, i ^ hop) for i in range(n_head)])
        mixed = term.astype(F32) if mixed is None else mixed + term.astype(F32)
    mixed = mixed.astype(BF)
    prompt_up = dot_nn(prompt_grad, weight).astype(BF)
    live = jnp.arange(reply_rows, dtype=jnp.int32) < lengths[0]
    reply_up = jnp.where(live[:, None], dot_nn(reply_grad, weight).astype(BF), jnp.zeros((), BF))
    query_grad, prompt_query_grad, kv_grad, reply_key_grad, reply_value_grad = attention_backward(
        weights, prompt_weights, reply_query, reply_up, reply_att, prompt_query, prompt_up, prompt_att, kv, reply_key, reply_value
    )
    terms = lax.all_to_all(kv_grad.reshape(n_seq, prompt_rows, 2 * DIM), "seq", 0, 0)
    kv_total = jnp.sum(terms.astype(F32), axis=0).astype(BF)
    return (
        mixed[:prompt_rows],
        mixed[prompt_rows:],
        prompt_query_grad,
        kv_total[:, :DIM],
        kv_total[:, DIM:],
        query_grad,
        reply_key_grad,
        reply_value_grad,
    )


def solution(mesh):
    cut = P("seq", "head")
    in_specs = (cut, cut, cut, cut, cut, cut, P("seq"), P("head", "seq"), P("seq", None), P("seq", None))
    return jax.shard_map(body, mesh=mesh, in_specs=in_specs, out_specs=(cut,) * 8, check_vma=False)
```

time: 635 us -> 205 us (0.32)
  waiting for transfers between devices: 411 us -> 85.8 us
  matrix products: 106 us -> 34.7 us
  blocking collectives: 48.1 us -> 0 us
  other arithmetic: 39.3 us -> 0.83 us
  Pallas kernels: 0 us -> 37.4 us
  starting transfers between devices: 0.16 us -> 23.3 us
    psum x1 -> x0, waiting for transfers between devices: 239 us -> none  [body(): lax.psum(group_term.astype(jnp.bfloat16), 'head').astype(jnp.float32)]
    reduce_scatter x2 -> x0, waiting for transfers between devices: 135 us -> none  [the longest x1 68.7 us: body(): lax.psum_scatter(value_grad[:prompt_len].astype(jnp.bfloat16), 'seq', sca...]
    dot_general x51 -> x10, matrix products: 106 us -> 34.7 us  [the longest x8 27 us: dot_nt(): lax.dot_general(a, b, (((1,), (1,)), ((), ())), preferred_element_type=F32)]
    all_gather x2 -> x0, blocking collectives: 48.1 us -> none  [the longest x1 28 us: body(): lax.all_gather(prompt_key, 'seq', axis=0, tiled=True)]
    pallas_call x0 -> x2, Pallas kernels: none -> 37.4 us  [the longest x1 21.4 us: attention_backward(): pl.pallas_call(backward_kernel, grid=(heads + 1,), in_specs=[pl.BlockSpec...]
    all_to_all x0 -> x2, waiting for transfers between devices: none -> 21.9 us  [the longest x1 11.3 us: body(): lax.all_to_all(kv_grad.reshape(n_seq, prompt_rows, 2 * DIM), 'seq', 0, 0)]
    ppermute x0 -> x7, waiting for transfers between devices: none -> 17.6 us  [body(): term = lax.ppermute(term, 'head', [(i, i ^ hop) for i in range(n_head)])]
    div x8 -> x0, other arithmetic: 15.7 us -> none  [head_attention(): shares = raised / jnp.sum(raised, axis=1, keepdims=True)]
  transfers between devices with their start and end apart: 4 -> 10, of which waited for: 4 -> 4; matrix products, arithmetic and copies ran while one was open for 2% -> 15% of each run, Pallas kernels for 0% -> 18%
where the time goes in v1:
time: 205 us; the launch traced here: 204 us
  waiting for transfers between devices  85.8 us (42%)
  Pallas kernels  37.4 us (18%)
  matrix products  34.7 us (17%)
  starting transfers between devices  23.3 us (11%)
  between operations  14.8 us (7%)
  local copies, waits for them, and re-layouts  7.51 us (4%)
    all_gather x1, waiting for transfers between devices, body(): weight = lax.all_gather(out_weight.T, 'seq', axis=0, tiled=True)  45.6 us
    dot_general x8, matrix products, dot_nt(): lax.dot_general(a, b, (((1,), (1,)), ((), ())), preferred_element_type=F32)  27 us
    pallas_call x1, Pallas kernels, attention_backward(): pl.pallas_call(backward_kernel, grid=(heads + 1,), in_specs=[pl.BlockSpec...  21.4 us
    ppermute x7, waiting for transfers between devices, body(): term = lax.ppermute(term, 'head', [(i, i ^ hop) for i in range(n_head)])  17.6 us
    pallas_call x1, Pallas kernels, attention_forward(): pl.pallas_call(forward_kernel, grid=(heads + 1,), in_specs=[pl.BlockSpec(...  16 us
    all_to_all x1, waiting for transfers between devices, body(): lax.all_to_all(kv_grad.reshape(n_seq, prompt_rows, 2 * DIM), 'seq', 0, 0)  11.3 us
    all_to_all x1, waiting for transfers between devices, body(): lax.all_to_all(jnp.broadcast_to(own[None], (n_seq,) + own.shape), 'seq',...  10.6 us
    all_to_all x1, starting transfers between devices, body(): lax.all_to_all(jnp.broadcast_to(own[None], (n_seq,) + own.shape), 'seq',...  9.29 us
  transfers between devices with their start and end apart: 10, of which 4 were waited for; matrix products, arithmetic and copies ran while one was open for 15% of the time, Pallas kernels for 18%

profile of v1, /device:TPU:1, one launch (start us, length us, event | category | flops | bytes accessed | tf_op | source)
XLA Modules:
  0.0 204.3 jit_solution(8439985247472044837)
XLA Ops:
  7.2 0.0 copy-start
  7.2 0.0 copy-start.1
  7.2 0.0 copy-start.2
  7.2 0.0 all-gather.2.cloned.1.call-start
  7.2 0.7 all-gather.2.cloned.1.call-update
  7.9 0.7 pad_maximum_fusion
  8.7 0.8 broadcast_in_dim.19
  9.5 9.3 %all-to-all-start = ((bf16[16,64,256]{2,1,0:T(8,128)(2,1)}), bf16[16,64,256]{2,1,0:T(8,128)(2,1)S(1)}, u32[]{:S(2)}, u32[]{:S(2)}) async-start(bf16[16,64,256]{2,1,0:T(8,128)(2,1)} %broadcast_in_dim.19), calls=%async_computation | async-start | bytes 1048576 | tf_op jit(solution)/shard_map/all_to_all | solution.py:256
  19.5 10.6 %all-to-all-done = bf16[16,64,256]{2,1,0:T(8,128)(2,1)S(1)} async-done(((bf16[16,64,256]{2,1,0:T(8,128)(2,1)}), bf16[16,64,256]{2,1,0:T(8,128)(2,1)S(1)}, u32[]{:S(2)}, u32[]{:S(2)}) %all-to-all-start) | async-done | bytes 524320 | tf_op jit(solution)/shard_map/all_to_all | solution.py:256
  30.1 0.0 copy-done.1
  30.1 0.0 copy-done.2
  30.1 0.0 copy-start.3
  30.1 0.9 copy-done.3
  31.0 0.0 copy-start.5
  31.0 0.9 copy-done.5
  31.9 16.0 %attention_forward.1 = (bf16[8,1536,512]{2,1,0:T(8,128)(2,1)}, bf16[1024,512]{1,0:T(8,128)(2,1)S(1)}, bf16[512,1024]{1,0:T(8,128)(2,1)S(1)}, bf16[64,1024]{1,0:T(8,128)(2,1)S(1)}) custom-call(s32[1]{0:T(128)} %bitcast.index_ref, s32[1]{0:T(128)} %copy.19.length_ref, bf16[512,1024]{1,0:T(8,128)(2,1)S(1)} %copy-done.1, bf16[64,1024]{1,0:T(8,128)(2,1)S(1)} %copy-done.2, ...), custom_call_target="tpu_custom_call" | custom-call | flops 3221225472 | bytes 18874368 | tf_op jit(solution)/shard_map/attention_forward/pallas_call | solution.py:94
  48.0 0.0 copy-start.7
  48.0 1.0 copy-done.7
  48.9 0.7 constant_dynamic-update-slice_fusion.1
  49.6 1.0 constant_dynamic-update-slice_fusion
  50.6 45.6 %all-gather.2.cloned.1.call-done = bf16[5120,1024]{1,0:T(8,128)(2,1)} async-done(((bf16[320,1024]{1,0:T(8,128)(2,1)}), bf16[5120,1024]{1,0:T(8,128)(2,1)}) %all-gather.2.cloned.1.call-update) | async-done | bytes 10485776 | tf_op jit(solution)/shard_map/all_gather | solution.py:254
  96.2 0.0 copy-start.9
  96.2 2.9 %convolution_convert_fusion.8 = bf16[576,640]{1,0:T(8,128)(2,1)S(1)} fusion(bf16[576,1024]{1,0:T(8,128)(2,1)} %constant_dynamic-update-slice_fusion, bf16[5120,1024]{1,0:T(8,128)(2,1)} %all-gather.2.cloned.1.call-done, s32[]{:T(128)S(6)} %select_n.28), kind=kOutput, calls=%fused_computation.9 | convolution fusion | flops 755343360 | bytes 3227652 | tf_op jit(solution)/shard_map/dot_general | solution.py:21
  99.2 2.5 %collective-permute-start = (bf16[576,640]{1,0:T(8,128)(2,1)S(1)}, bf16[576,640]{1,0:T(8,128)(2,1)}, u32[]{:S(2)}, u32[]{:S(2)}) collective-permute-start(bf16[576,640]{1,0:T(8,128)(2,1)S(1)} %convolution_convert_fusion.8), channel_id=1, source_target_pairs={{0,7},{1,6},{2,5},{3,4},{4,3},{5,2},{6,1},{7,0},{8,15},{9,14},{10,... | collective-permute-start | bytes 2211848 | tf_op jit(solution)/shard_map/ppermute | solution.py:268
  101.7 2.8 %convolution_convert_fusion.7 = bf16[576,640]{1,0:T(8,128)(2,1)S(1)} fusion(bf16[576,1024]{1,0:T(8,128)(2,1)} %constant_dynamic-update-slice_fusion, bf16[5120,1024]{1,0:T(8,128)(2,1)} %all-gather.2.cloned.1.call-done, s32[]{:T(128)S(6)} %select_n.29), kind=kOutput, calls=%fused_computation.8 | convolution fusion | flops 755343360 | bytes 3227652 | tf_op jit(solution)/shard_map/dot_general | solution.py:21
  104.5 0.8 collective-permute-start.1
  105.3 0.0 copy-done.9
  105.3 3.3 %convolution_convert_fusion.6 = bf16[576,640]{1,0:T(8,128)(2,1)} fusion(bf16[576,1024]{1,0:T(8,128)(2,1)} %constant_dynamic-update-slice_fusion, bf16[5120,1024]{1,0:T(8,128)(2,1)S(1)} %copy-done.9, s32[]{:T(128)S(6)} %select_n.30), kind=kOutput, calls=%fused_computation.7 | convolution fusion | flops 755343360 | bytes 3227652 | tf_op jit(solution)/shard_map/dot_general | solution.py:21
  108.6 1.9 collective-permute-start.2
  110.6 0.0 slice-start
  110.6 3.4 %convolution_convert_fusion.5 = bf16[576,640]{1,0:T(8,128)(2,1)} fusion(bf16[576,1024]{1,0:T(8,128)(2,1)} %constant_dynamic-update-slice_fusion, bf16[5120,1024]{1,0:T(8,128)(2,1)S(1)} %copy-done.9, s32[]{:T(128)S(6)} %select_n.31), kind=kOutput, calls=%fused_computation.6 | convolution fusion | flops 755343360 | bytes 3227652 | tf_op jit(solution)/shard_map/dot_general | solution.py:21
  114.0 0.0 slice-start.1
  114.0 1.4 collective-permute-start.3
  115.5 3.3 %convolution_convert_fusion.4 = bf16[576,640]{1,0:T(8,128)(2,1)} fusion(bf16[576,1024]{1,0:T(8,128)(2,1)} %constant_dynamic-update-slice_fusion, bf16[5120,1024]{1,0:T(8,128)(2,1)S(1)} %copy-done.9, s32[]{:T(128)S(6)} %select_n.32), kind=kOutput, calls=%fused_computation.5 | convolution fusion | flops 755343360 | bytes 3227652 | tf_op jit(solution)/shard_map/dot_general | solution.py:21
  118.7 0.4 collective-permute-start.4
  119.2 3.3 %convolution_convert_fusion.2 = bf16[576,640]{1,0:T(8,128)(2,1)} fusion(bf16[576,1024]{1,0:T(8,128)(2,1)} %constant_dynamic-update-slice_fusion, bf16[5120,1024]{1,0:T(8,128)(2,1)S(1)} %copy-done.9, s32[]{:T(128)S(6)} %select_n.34), kind=kOutput, calls=%fused_computation.3 | convolution fusion | flops 755343360 | bytes 3227652 | tf_op jit(solution)/shard_map/dot_general | solution.py:21
  122.5 0.0 slice-done
  122.5 0.0 slice-done.1
  122.5 5.7 %fusion.8.grad_ref = bf16[512,1024]{1,0:T(8,128)(2,1)S(1)} fusion(bf16[512,5120]{1,0:T(8,128)(2,1)S(1)} %bitcast.24, bf16[5120,1024]{1,0:T(8,128)(2,1)S(1)} %copy-done.9, pred[512]{0:T(512)(128)(4,1)S(1)} %iota_compare_fusion), kind=kOutput, calls=%fused_computation.18 | convolution fusion | flops 5369757696 | bytes 16777728 | tf_op jit(solution)/shard_map/dot_general | solution.py:17
  128.2 3.3 %convolution_convert_fusion.3 = bf16[576,640]{1,0:T(8,128)(2,1)} fusion(bf16[576,1024]{1,0:T(8,128)(2,1)} %constant_dynamic-update-slice_fusion, bf16[5120,1024]{1,0:T(8,128)(2,1)S(1)} %copy-done.9, s32[]{:T(128)S(6)} %select_n.33), kind=kOutput, calls=%fused_computation.4 | convolution fusion | flops 755343360 | bytes 3227652 | tf_op jit(solution)/shard_map/dot_general | solution.py:21
  131.5 0.0 copy-done
  131.5 0.0 copy-start.4
  131.5 0.0 copy-start.6
  131.5 2.0 convolution_convert_fusion.9.prompt_grad_ref
  133.5 0.0 collective-permute-done
  133.5 1.6 collective-permute-start.5
  135.1 17.5 %collective-permute-done.1 = bf16[576,640]{1,0:T(8,128)(2,1)} collective-permute-done((bf16[576,640]{1,0:T(8,128)(2,1)S(1)}, bf16[576,640]{1,0:T(8,128)(2,1)}, u32[]{:S(2)}, u32[]{:S(2)}) %collective-permute-start.1) | collective-permute-done | bytes 737312 | tf_op jit(solution)/shard_map/ppermute | solution.py:268
  152.6 0.3 collective-permute-start.6
  152.9 0.0 copy-done.4
  152.9 0.0 copy-done.6
  152.9 0.0 copy-done.8
  152.9 21.4 %attention_backward.1 = (bf16[512,1024]{1,0:T(8,128)(2,1)}, bf16[64,1024]{1,0:T(8,128)(2,1)}, bf16[1024,256]{1,0:T(8,128)(2,1)}, bf16[512,128]{1,0:T(8,128)(2,1)}, bf16[512,128]{1,0:T(8,128)(2,1)}) custom-call(bf16[8,1536,512]{2,1,0:T(8,128)(2,1)} %get-tuple-element.19.weight_ref, bf16[1024,512]{1,0:T(8,128)(2,1)S(1)} %copy-done.8, ...), custom_call_target="tpu_custom_call" | custom-call | flops 6442450944 | bytes 18874368 | tf_op jit(solution)/shard_map/attention_backward/pallas_call | solution.py:205
  174.3 4.9 %all-to-all-start.1 = ((bf16[16,64,256]{2,1,0:T(8,128)(2,1)}), bf16[16,64,256]{2,1,0:T(8,128)(2,1)S(1)}, u32[]{:S(2)}, u32[]{:S(2)}) async-start(bf16[16,64,256]{2,1,0:T(8,128)(2,1)} %bitcast.4), calls=%async_computation.1 | async-start | bytes 1048576 | tf_op jit(solution)/shard_map/all_to_all | solution.py:277
  179.2 11.3 %all-to-all-done.1 = bf16[16,64,256]{2,1,0:T(8,128)(2,1)S(1)} async-done(((bf16[16,64,256]{2,1,0:T(8,128)(2,1)}), bf16[16,64,256]{2,1,0:T(8,128)(2,1)S(1)}, u32[]{:S(2)}, u32[]{:S(2)}) %all-to-all-start.1) | async-done | bytes 524320 | tf_op jit(solution)/shard_map/all_to_all | solution.py:277
  190.5 0.1 reduce_sum.12
  190.6 0.6 fusion.19
  191.2 0.0 collective-permute-done.2
  191.2 0.0 collective-permute-done.3
  191.2 0.0 collective-permute-done.4
  191.2 0.0 collective-permute-done.5
  191.2 0.0 collective-permute-done.6
  191.2 4.7 %add_convert_fusion = bf16[576,640]{1,0:T(8,128)(2,1)S(1)} fusion(bf16[576,640]{1,0:T(8,128)(2,1)} %collective-permute-done.6, bf16[576,640]{1,0:T(8,128)(2,1)} %collective-permute-done.5, bf16[576,640]{1,0:T(8,128)(2,1)} %collective-permute-done.4, bf16[576,640]{1,0:T(8,128)(2,1)} %collective-permute-done.3, bf16[576,640]{1,0:T(8,128)(2,1)} %collective-permute-done.2, ...), kind=kOutput, calls=%fused_computation.1 | convolution fusion | flops 761241600 | bytes 8388612 | tf_op jit(solution)/shard_map/dot_general | solution.py:21
  195.9 0.6 slice.16
  196.5 0.9 slice.17
  (3 shorter events, 0.0 us)
Async XLA Ops:
  7.2 124.3 %copy-start = (bf16[64,5120]{1,0:T(8,128)(2,1)S(1)}, bf16[64,5120]{1,0:T(8,128)(2,1)}, u32[]{:S(2)}) copy-start(bf16[64,5120]{1,0:T(8,128)(2,1)} %param.18) | copy-start | bytes 1966084
  7.2 22.9 %copy-start.1 = (bf16[512,1024]{1,0:T(8,128)(2,1)S(1)}, bf16[512,1024]{1,0:T(8,128)(2,1)}, u32[]{:S(2)}) copy-start(bf16[512,1024]{1,0:T(8,128)(2,1)} %query_ref.3) | copy-start | bytes 3145732
  7.2 22.9 %copy-start.2 = (bf16[64,1024]{1,0:T(8,128)(2,1)S(1)}, bf16[64,1024]{1,0:T(8,128)(2,1)}, u32[]{:S(2)}) copy-start(bf16[64,1024]{1,0:T(8,128)(2,1)} %prompt_query_ref.3) | copy-start | bytes 393220
  7.2 89.0 %all-gather.2.cloned.1.call-start = ((), (), s32[]{:S(2)}) async-start(), calls=%async_computation.2 | async-start | bytes 11141120 | tf_op jit(solution)/shard_map/all_gather | solution.py:254
  9.5 20.6 %all-to-all-start = ((bf16[16,64,256]{2,1,0:T(8,128)(2,1)}), bf16[16,64,256]{2,1,0:T(8,128)(2,1)S(1)}, u32[]{:S(2)}, u32[]{:S(2)}) async-start(bf16[16,64,256]{2,1,0:T(8,128)(2,1)} %broadcast_in_dim.19), calls=%async_computation | async-start | bytes 1048576 | tf_op jit(solution)/shard_map/all_to_all | solution.py:256
  30.1 0.9 copy-start.3
  31.0 0.9 copy-start.5
  48.0 1.0 copy-start.7
  96.2 9.1 %copy-start.9 = (bf16[5120,1024]{1,0:T(8,128)(2,1)S(1)}, bf16[5120,1024]{1,0:T(8,128)(2,1)}, u32[]{:S(2)}) copy-start(bf16[5120,1024]{1,0:T(8,128)(2,1)} %all-gather.2.cloned.1.call-done) | copy-start | bytes 31457284
  99.2 34.3 %collective-permute-start = (bf16[576,640]{1,0:T(8,128)(2,1)S(1)}, bf16[576,640]{1,0:T(8,128)(2,1)}, u32[]{:S(2)}, u32[]{:S(2)}) collective-permute-start(bf16[576,640]{1,0:T(8,128)(2,1)S(1)} %convolution_convert_fusion.8), channel_id=1, source_target_pairs={{0,7},{1,6},{2,5},{3,4},{4,3},{5,2},{6,1},{7,0},{8,15},{9,14},{10,... | collective-permute-start | bytes 2211848 | tf_op jit(solution)/shard_map/ppermute | solution.py:268
  104.5 48.1 %collective-permute-start.1 = (bf16[576,640]{1,0:T(8,128)(2,1)S(1)}, bf16[576,640]{1,0:T(8,128)(2,1)}, u32[]{:S(2)}, u32[]{:S(2)}) collective-permute-start(bf16[576,640]{1,0:T(8,128)(2,1)S(1)} %convolution_convert_fusion.7), channel_id=1, source_target_pairs={{0,6},{1,7},{2,4},{3,5},{4,2},{5,3},{6,0},{7,1},{8,14},{9,15},{10,... | collective-permute-start | bytes 2211848 | tf_op jit(solution)/shard_map/ppermute | solution.py:268
  108.6 82.5 %collective-permute-start.2 = (bf16[576,640]{1,0:T(8,128)(2,1)}, bf16[576,640]{1,0:T(8,128)(2,1)}, u32[]{:S(2)}, u32[]{:S(2)}) collective-permute-start(bf16[576,640]{1,0:T(8,128)(2,1)} %convolution_convert_fusion.6), channel_id=1, source_target_pairs={{0,5},{1,4},{2,7},{3,6},{4,1},{5,0},{6,3},{7,2},{8,13},{9,12},{10,... | collective-permute-start | bytes 2211848 | tf_op jit(solution)/shard_map/ppermute | solution.py:268
  110.6 11.9 %slice-start = ((s8[5242880]{0:T(1024)(128)(4,1)}), s8[4194304]{0:T(1024)(128)(4,1)S(1)}, s32[]{:S(2)}) async-start(s8[5242880]{0:T(1024)(128)(4,1)} %bitcast.23), calls=%async_computation.3 | async-start | bytes 8388608
  114.0 8.5 %slice-start.1 = ((s8[5242880]{0:T(1024)(128)(4,1)}), s8[1048576]{0:T(1024)(128)(4,1)S(1)}, s32[]{:S(2)}) async-start(s8[5242880]{0:T(1024)(128)(4,1)} %bitcast.23), calls=%async_computation.4 | async-start | bytes 2097152
  114.0 77.2 %collective-permute-start.3 = (bf16[576,640]{1,0:T(8,128)(2,1)}, bf16[576,640]{1,0:T(8,128)(2,1)}, u32[]{:S(2)}, u32[]{:S(2)}) collective-permute-start(bf16[576,640]{1,0:T(8,128)(2,1)} %convolution_convert_fusion.5), channel_id=1, source_target_pairs={{0,4},{1,5},{2,6},{3,7},{4,0},{5,1},{6,2},{7,3},{8,12},{9,13},{10,... | collective-permute-start | bytes 2211848 | tf_op jit(solution)/shard_map/ppermute | solution.py:268
  118.7 72.5 %collective-permute-start.4 = (bf16[576,640]{1,0:T(8,128)(2,1)}, bf16[576,640]{1,0:T(8,128)(2,1)}, u32[]{:S(2)}, u32[]{:S(2)}) collective-permute-start(bf16[576,640]{1,0:T(8,128)(2,1)} %convolution_convert_fusion.4), channel_id=1, source_target_pairs={{0,3},{1,2},{2,1},{3,0},{4,7},{5,6},{6,5},{7,4},{8,11},{9,10},{10,... | collective-permute-start | bytes 2211848 | tf_op jit(solution)/shard_map/ppermute | solution.py:268
  131.5 21.5 %copy-start.4 = (bf16[512,128]{1,0:T(8,128)(2,1)S(1)}, bf16[512,128]{1,0:T(8,128)(2,1)}, u32[]{:S(2)}) copy-start(bf16[512,128]{1,0:T(8,128)(2,1)} %reply_key_ref.3) | copy-start | bytes 393220
  131.5 21.5 %copy-start.6 = (bf16[512,128]{1,0:T(8,128)(2,1)S(1)}, bf16[512,128]{1,0:T(8,128)(2,1)}, u32[]{:S(2)}) copy-start(bf16[512,128]{1,0:T(8,128)(2,1)} %reply_value_ref.3) | copy-start | bytes 393220
  131.5 21.5 %copy-start.8 = (bf16[1024,512]{1,0:T(8,128)(2,1)S(1)}, bf16[1024,512]{1,0:T(8,128)(2,1)}, u32[]{:S(2)}) copy-start(bf16[1024,512]{1,0:T(8,128)(2,1)} %copy-done.7) | copy-start | bytes 3145732
  133.5 57.7 %collective-permute-start.5 = (bf16[576,640]{1,0:T(8,128)(2,1)}, bf16[576,640]{1,0:T(8,128)(2,1)}, u32[]{:S(2)}, u32[]{:S(2)}) collective-permute-start(bf16[576,640]{1,0:T(8,128)(2,1)} %convolution_convert_fusion.3), channel_id=1, source_target_pairs={{0,2},{1,3},{2,0},{3,1},{4,6},{5,7},{6,4},{7,5},{8,10},{9,11},{10,... | collective-permute-start | bytes 2211848 | tf_op jit(solution)/shard_map/ppermute | solution.py:268
  152.6 38.6 %collective-permute-start.6 = (bf16[576,640]{1,0:T(8,128)(2,1)}, bf16[576,640]{1,0:T(8,128)(2,1)}, u32[]{:S(2)}, u32[]{:S(2)}) collective-permute-start(bf16[576,640]{1,0:T(8,128)(2,1)} %convolution_convert_fusion.2), channel_id=1, source_target_pairs={{0,1},{1,0},{2,3},{3,2},{4,5},{5,4},{6,7},{7,6},{8,9},{9,8},{10,11... | collective-permute-start | bytes 2211848 | tf_op jit(solution)/shard_map/ppermute | solution.py:268
  174.3 16.2 %all-to-all-start.1 = ((bf16[16,64,256]{2,1,0:T(8,128)(2,1)}), bf16[16,64,256]{2,1,0:T(8,128)(2,1)S(1)}, u32[]{:S(2)}, u32[]{:S(2)}) async-start(bf16[16,64,256]{2,1,0:T(8,128)(2,1)} %bitcast.4), calls=%async_computation.1 | async-start | bytes 1048576 | tf_op jit(solution)/shard_map/all_to_all | solution.py:277
Sparse Core Ops, SparseCore 0:
  10.5 85.6 all-gather.1

commit v2 on v1

--- a/solution.py
+++ b/solution.py
@@ -10,7 +10,7 @@
 F32 = jnp.float32
 SCALE = DIM**-0.5
 EXP_SCALE = SCALE * 1.4426950408889634
-VMEM_LIMIT = 44 * 1024 * 1024
+VMEM_LIMIT = 60 * 1024 * 1024
 
 
 def dot_nn(a, b):
@@ -246,39 +246,233 @@
     )(weights, prompt_weights, reply_query, reply_up, reply_att, prompt_query, prompt_up, prompt_att, kv, kv, reply_key, reply_value)
 
 
+def half_copies(chunks, order_ref, core_ref, gathered, sems):
+    size = chunks[0].shape[0]
+    core = core_ref[0]
+    copies = []
+    for slot in range(4):
+        for side in range(2):
+            place = order_ref[slot if side == 0 else SWAPPED[slot]]
+            row = place * (2 * size) + (core if side == 0 else 1 - core) * size
+            copies.append(
+                pltpu.make_async_copy(
+                    chunks[side * 4 + slot],
+                    gathered.at[pl.ds(pl.multiple_of(row, size), size), :],
+                    sems.at[place, side],
+                )
+            )
+    return copies
+
+
+def products_kernel(order_ref, core_ref, head_ref, half_ref, *refs):
+    chunks = refs[:8]
+    prompt_ref, reply_ref = refs[8:10]
+    outs, (gathered, rows, held, sems, out_sems) = refs[-11:-5], refs[-5:]
+    size = chunks[0].shape[0]
+    for copy in half_copies(chunks, order_ref, core_ref, gathered, sems):
+        copy.start()
+    count = prompt_ref.shape[0]
+    half = rows.shape[0] // 2
+    rows[:count, :] = prompt_ref[...]
+    rows[count:, :] = reply_ref[...]
+    across, along = head_ref[0] % 2, head_ref[0] // 2
+
+    def flush(slot, dy, dx):
+        upper = [
+            pltpu.make_async_copy(held.at[slot, pl.ds(0, half), :], outs[side].at[dy], out_sems.at[slot, 0]) for side in range(2)
+        ]
+        lower = [
+            pltpu.make_async_copy(held.at[slot, pl.ds(half, half), :], outs[2 + turn].at[dx], out_sems.at[slot, 1]) for turn in range(4)
+        ]
+        return upper, lower
+
+    for place in range(4):
+        slot = place % 2
+        if place >= 2:
+            upper, lower = flush(slot, 0, 0)
+            upper[0].wait()
+            lower[0].wait()
+        for side in range(2):
+            pltpu.make_async_copy(chunks[side * 4], gathered.at[pl.ds(0, size), :], sems.at[place, side]).wait()
+        block = gathered[2 * size * place : 2 * size * (place + 1), :]
+        held[slot] = dot_nt(rows[...], block).astype(BF)
+        target = half_ref[0] * 4 + place
+        dy, dx = (target // 2 - along + 4) % 4, (target % 2 - across + 2) % 2
+        upper, lower = flush(slot, dy, dx)
+        for side in range(2):
+            pl.when(dx == side)(upper[side].start)
+        for turn in range(4):
+            pl.when(dy == turn)(lower[turn].start)
+    for slot in range(2):
+        upper, lower = flush(slot, 0, 0)
+        upper[0].wait()
+        lower[0].wait()
+
+
+def head_products(order, core, head, half, chunks, prompt_att, reply_att, earlier):
+    total = prompt_att.shape[0] + reply_att.shape[0]
+    size, depth = chunks[0].shape
+    width = 2 * size
+    anywhere = pl.BlockSpec(memory_space=pl.ANY)
+    scalar = pl.BlockSpec(memory_space=pltpu.SMEM)
+    return pl.pallas_call(
+        products_kernel,
+        in_specs=[scalar] * 4 + [anywhere] * 8 + [pl.BlockSpec(memory_space=pltpu.VMEM)] * 2 + [anywhere] * len(earlier),
+        out_specs=[anywhere] * 6,
+        out_shape=[jax.ShapeDtypeStruct((4, total // 2, width), BF)] * 2 + [jax.ShapeDtypeStruct((2, total // 2, width), BF)] * 4,
+        input_output_aliases={14 + place: place for place in range(len(earlier))},
+        scratch_shapes=[
+            pltpu.VMEM((8 * size, depth), BF),
+            pltpu.VMEM((total, depth), BF),
+            pltpu.VMEM((2, total, width), BF),
+            pltpu.SemaphoreType.DMA((4, 2)),
+            pltpu.SemaphoreType.DMA((2, 2)),
+        ],
+        compiler_params=pltpu.CompilerParams(vmem_limit_bytes=VMEM_LIMIT),
+        cost_estimate=pl.CostEstimate(flops=2 * total * depth * 8 * size, bytes_accessed=9 * 2**20, transcendentals=0),
+        name="head_products",
+    )(order, core, head, half, *chunks, prompt_att, reply_att, *earlier)
+
+
+def upstream_kernel(order_ref, core_ref, half_ref, length_ref, *refs):
+    chunks = refs[:8]
+    prompt_ref, reply_ref = refs[8:10]
+    last = len(refs) == 17
+    earlier, outs, (gathered, rows, sems, row_sems) = (refs[10:11], refs[11:13], refs[13:]) if last else ((), refs[10:11], refs[11:])
+    step = pl.program_id(0)
+    count = prompt_ref.shape[0]
+
+    @pl.when(step == 0)
+    def _():
+        columns = pl.ds(pl.multiple_of(half_ref[0] * rows.shape[1], rows.shape[1]), rows.shape[1])
+        copies = half_copies(chunks, order_ref, core_ref, gathered, sems)
+        copies.append(pltpu.make_async_copy(prompt_ref.at[:, columns], rows.at[pl.ds(0, count), :], row_sems.at[0]))
+        copies.append(pltpu.make_async_copy(reply_ref.at[:, columns], rows.at[pl.ds(count, rows.shape[0] - count), :], row_sems.at[1]))
+        for copy in copies:
+            copy.start()
+        for copy in copies:
+            copy.wait()
+
+    width = outs[0].shape[1]
+    total = dot_nn(rows[...], gathered[:, pl.ds(pl.multiple_of(step * width, width), width)])
+    if not last:
+        outs[0][...] = total
+    else:
+        total = total + earlier[0][...]
+        outs[0][...] = total[:count].astype(BF)
+        live = lax.broadcasted_iota(jnp.int32, (total.shape[0] - count, width), 0) < length_ref[0]
+        outs[1][...] = jnp.where(live, total[count:], 0.0).astype(BF)
+
+
+def upstream(order, core, half, lengths, chunks, prompt_grad, reply_grad, earlier):
+    size, depth = chunks[0].shape
+    prompt_rows, reply_rows = prompt_grad.shape[0], reply_grad.shape[0]
+    total = prompt_rows + reply_rows
+    parts = 2
+    anywhere = pl.BlockSpec(memory_space=pl.ANY)
+    scalar = pl.BlockSpec(memory_space=pltpu.SMEM)
+    column = lambda rows: pl.BlockSpec((rows, depth // parts), lambda k: (0, k))
+    if earlier is None:
+        out_specs, out_shape = [column(total)], [jax.ShapeDtypeStruct((total, depth), F32)]
+    else:
+        out_specs = [column(prompt_rows), column(reply_rows)]
+        out_shape = [jax.ShapeDtypeStruct((prompt_rows, depth), BF), jax.ShapeDtypeStruct((reply_rows, depth), BF)]
+    return pl.pallas_call(
+        upstream_kernel,
+        grid=(parts,),
+        in_specs=[scalar] * 4 + [anywhere] * 10 + ([] if earlier is None else [column(total)]),
+        out_specs=out_specs,
+        out_shape=out_shape,
+        scratch_shapes=[
+            pltpu.VMEM((8 * size, depth), BF),
+            pltpu.VMEM((total, 8 * size), BF),
+            pltpu.SemaphoreType.DMA((4, 2)),
+            pltpu.SemaphoreType.DMA((2,)),
+        ],
+        compiler_params=pltpu.CompilerParams(vmem_limit_bytes=VMEM_LIMIT),
+        cost_estimate=pl.CostEstimate(flops=2 * total * depth * 8 * size, bytes_accessed=9 * 2**20, transcendentals=0),
+        name="upstream",
+    )(order, core, half, lengths, *chunks, prompt_grad, reply_grad, *([] if earlier is None else [earlier]))
+
+
+SWAPPED = (0, 2, 1, 3)
+
+
+def seq_perm(move):
+    pairs = []
+    for x in range(2):
+        for z in range(4):
+            for core in range(2):
+                to_x, to_z, to_core = move(x, z, core)
+                pairs.append((x * 8 + z * 2 + core, (to_x % 2) * 8 + (to_z % 4) * 2 + to_core % 2))
+    return pairs
+
+
+ALONG = seq_perm(lambda x, z, core: (x, z + 1 - 2 * core, core))
+AGAINST = seq_perm(lambda x, z, core: (x, z - 1 + 2 * core, core))
+PEER = seq_perm(lambda x, z, core: (x + 1, z, core))
+SIBLING = seq_perm(lambda x, z, core: (x, z, core + 1))
+
+
+def head_perm(dy, dx):
+    return [(y * 2 + x, ((y + dy) % 4) * 2 + (x + dx) % 2) for y in range(4) for x in range(2)]
+
+
+def gather_first(own):
+    return [own] + [lax.ppermute(own, "seq", perm) for perm in (ALONG, AGAINST, PEER)]
+
+
+def gather_second(along, peer):
+    return [lax.ppermute(along, "seq", ALONG), lax.ppermute(peer, "seq", ALONG), lax.ppermute(peer, "seq", AGAINST)]
+
+
+def sibling(chunk):
+    return lax.ppermute(chunk, "seq", SIBLING)
+
+
 def body(prompt_query, prompt_key, prompt_value, reply_query, reply_key, reply_value, lengths, out_weight, prompt_grad, reply_grad):
     prompt_rows = prompt_query.shape[0]
-    reply_rows = reply_query.shape[0]
-    n_seq, n_head = lax.axis_size("seq"), lax.axis_size("head")
+    n_seq = lax.axis_size("seq")
     seq, head = lax.axis_index("seq"), lax.axis_index("head")
-    weight = lax.all_gather(out_weight.T, "seq", axis=0, tiled=True)
+    scalar = lambda value: value.reshape(1).astype(jnp.int32)
+    x, z, core = seq // 8, (seq // 2) % 4, seq % 2
+    order = jnp.stack([(z - (1 - 2 * core) * hop) % 4 for hop in (0, 1, -1, 2)]).astype(jnp.int32)
+    core, near, other, head = scalar(core), scalar(x), scalar(1 - x), scalar(head)
     own = jnp.concatenate([prompt_key, prompt_value], 1)
     kv = lax.all_to_all(jnp.broadcast_to(own[None], (n_seq,) + own.shape), "seq", 0, 0).reshape(n_seq * prompt_rows, 2 * DIM)
-    weights, prompt_weights, reply_att, prompt_att = attention_forward(
-        seq.reshape(1).astype(jnp.int32), lengths, reply_query, prompt_query, kv, reply_key, reply_value
-    )
-    attended = jnp.concatenate([prompt_att, reply_att], 0)
-    width = weight.shape[0] // n_head
-    mixed = None
-    for hop in [7, 6, 5, 4, 3, 2, 1, 0]:
-        target = head ^ hop
-        block = lax.dynamic_slice_in_dim(weight, target * width, width, 0)
-        term = dot_nt(attended, block).astype(BF)
-        if hop:
-            term = lax.ppermute(term, "head", [(i, i ^ hop) for i in range(n_head)])
-        mixed = term.astype(F32) if mixed is None else mixed + term.astype(F32)
-    mixed = mixed.astype(BF)
-    prompt_up = dot_nn(prompt_grad, weight).astype(BF)
-    live = jnp.arange(reply_rows, dtype=jnp.int32) < lengths[0]
-    reply_up = jnp.where(live[:, None], dot_nn(reply_grad, weight).astype(BF), jnp.zeros((), BF))
+    mine, along, against, peer = gather_first(out_weight.T)
+    mine_twin = sibling(mine)
+    along, against, peer, mine_twin, kv = lax.optimization_barrier((along, against, peer, mine_twin, kv))
+    far, peer_along, peer_against = gather_second(along, peer)
+    weights, prompt_weights, reply_att, prompt_att = attention_forward(scalar(seq), lengths, reply_query, prompt_query, kv, reply_key, reply_value)
+    along, against, peer, peer_along, reply_att = lax.optimization_barrier((along, against, peer, peer_along, reply_att))
+    peer_far = lax.ppermute(peer_along, "seq", ALONG)
+    near_chunks = [mine, along, against, far, mine_twin] + [sibling(chunk) for chunk in (along, against, far)]
+    far_chunks = [peer, peer_along, peer_against, peer_far]
+    far_chunks = far_chunks + [sibling(chunk) for chunk in far_chunks]
+    (partial,) = upstream(order, core, near, lengths, near_chunks, prompt_grad, reply_grad, None)
+    products = head_products(order, core, head, near, near_chunks, prompt_att, reply_att, ())
+    partial, products, far_chunks = lax.optimization_barrier((partial, products, far_chunks))
+    kept, sent, *turns = head_products(order, core, head, other, far_chunks, prompt_att, reply_att, products)
+    came = lax.ppermute(sent, "head", head_perm(0, 1))
+    turned = [lax.ppermute(turns[dy], "head", head_perm(dy, 0)) for dy in (1, 2, 3)]
+    prompt_up, reply_up = upstream(order, core, other, lengths, far_chunks, prompt_grad, reply_grad, partial)
     query_grad, prompt_query_grad, kv_grad, reply_key_grad, reply_value_grad = attention_backward(
         weights, prompt_weights, reply_query, reply_up, reply_att, prompt_query, prompt_up, prompt_att, kv, reply_key, reply_value
     )
+    first = [(kept[dy].astype(F32) + came[dy].astype(F32)).astype(BF) for dy in range(4)]
+    second = turns[0].astype(F32) + turned[0].astype(F32) + turned[1].astype(F32) + turned[2].astype(F32)
+    second = second.astype(BF)
+    first, second, kv_grad = lax.optimization_barrier((first, (second[0], second[1]), kv_grad))
+    first = [first[0]] + [lax.ppermute(first[dy], "head", head_perm(dy, 0)) for dy in (1, 2, 3)]
+    second = second[0].astype(F32) + lax.ppermute(second[1], "head", head_perm(0, 1)).astype(F32)
+    first = first[0].astype(F32) + first[1].astype(F32) + first[2].astype(F32) + first[3].astype(F32)
+    first, second = first.astype(BF), second.astype(BF)
     terms = lax.all_to_all(kv_grad.reshape(n_seq, prompt_rows, 2 * DIM), "seq", 0, 0)
     kv_total = jnp.sum(terms.astype(F32), axis=0).astype(BF)
     return (
-        mixed[:prompt_rows],
-        mixed[prompt_rows:],
+        first[:prompt_rows],
+        jnp.concatenate([first[prompt_rows:], second], 0),
         prompt_query_grad,
         kv_total[:, :DIM],
         kv_total[:, DIM:],

time: 205 us -> 163 us (0.80)
  waiting for transfers between devices: 85.8 us -> 14.5 us
  Pallas kernels: 37.4 us -> 75.2 us
  matrix products: 34.7 us -> 0 us
  blocking collectives: 0 us -> 21 us
  starting transfers between devices: 23.3 us -> 40.5 us
  between operations: 14.8 us -> 1.52 us
  other arithmetic: 0.83 us -> 5.49 us
  local copies, waits for them, and re-layouts: 7.51 us -> 4.41 us
    all_gather x1 -> x0, waiting for transfers between devices: 45.6 us -> none  [body(): weight = lax.all_gather(out_weight.T, 'seq', axis=0, tiled=True)]
    pallas_call x0 -> x4, Pallas kernels: none -> 36.1 us  [the longest x2 18.5 us: head_products(): pl.pallas_call(products_kernel, in_specs=[scalar] * 4 + [anywhere] * 8 +...]
    dot_general x10 -> x0, matrix products: 34.7 us -> none  [the longest x8 27 us: dot_nt(): lax.dot_general(a, b, (((1,), (1,)), ((), ())), preferred_element_type=F32)]
    ppermute x7 -> x23, starting transfers between devices: 9.04 us -> 31.6 us  [the longest x8 9.9 us: sibling(): return lax.ppermute(chunk, 'seq', SIBLING)]
    all_to_all x0 -> x1, blocking collectives: none -> 21 us  [body(): lax.all_to_all(jnp.broadcast_to(own[None], (n_seq,) + own.shape), 'seq',...]
    all_to_all x1 -> x0, waiting for transfers between devices: 10.6 us -> none  [body(): lax.all_to_all(jnp.broadcast_to(own[None], (n_seq,) + own.shape), 'seq',...]
    all_to_all x1 -> x0, starting transfers between devices: 9.29 us -> none  [body(): lax.all_to_all(jnp.broadcast_to(own[None], (n_seq,) + own.shape), 'seq',...]
    all_to_all x1, waiting for transfers between devices: 11.3 us -> 2.81 us  [body(): lax.all_to_all(kv_grad.reshape(n_seq, prompt_rows, 2 * DIM), 'seq', 0, 0)]
  transfers between devices with their start and end apart: 10 -> 24, of which waited for: 4 -> 4; matrix products, arithmetic and copies ran while one was open for 15% -> 3% of each run, Pallas kernels for 18% -> 41%
where the time goes in v2:
time: 163 us
  Pallas kernels  75.2 us (46%)
  starting transfers between devices  40.5 us (25%)
  blocking collectives  21 us (13%)
  waiting for transfers between devices  14.5 us (9%)
  other arithmetic  5.49 us (3%)
  local copies, waits for them, and re-layouts  4.41 us (3%)
    pallas_call x1, Pallas kernels, attention_backward(): pl.pallas_call(backward_kernel, grid=(heads + 1,), in_specs=[pl.BlockSpec...  21.8 us
    all_to_all x1, blocking collectives, body(): lax.all_to_all(jnp.broadcast_to(own[None], (n_seq,) + own.shape), 'seq',...  21 us
    pallas_call x2, Pallas kernels, head_products(): pl.pallas_call(products_kernel, in_specs=[scalar] * 4 + [anywhere] * 8 +...  18.5 us
    pallas_call x2, Pallas kernels, upstream(): pl.pallas_call(upstream_kernel, grid=(parts,), in_specs=[scalar] * 4 + [a...  17.6 us
    pallas_call x1, Pallas kernels, attention_forward(): pl.pallas_call(forward_kernel, grid=(heads + 1,), in_specs=[pl.BlockSpec(...  17.2 us
    ppermute x8, starting transfers between devices, sibling(): return lax.ppermute(chunk, 'seq', SIBLING)  9.9 us
    all_to_all x1, starting transfers between devices, body(): lax.all_to_all(kv_grad.reshape(n_seq, prompt_rows, 2 * DIM), 'seq', 0, 0)  9 us
    ppermute x3, starting transfers between devices, gather_first(): lax.ppermute(own, 'seq', perm)  7.4 us
  transfers between devices with their start and end apart: 24, of which 4 were waited for; matrix products, arithmetic and copies ran while one was open for 3% of the time, Pallas kernels for 41%

profile of v2, /device:TPU:1, one launch (start us, length us, event | category | flops | bytes accessed | tf_op | source)
XLA Modules:
  0.0 162.6 jit_solution(4172783110717401131)
XLA Ops:
  0.6 4.7 %collective-permute-start = (bf16[320,1024]{1,0:T(8,128)(2,1)}, bf16[320,1024]{1,0:T(8,128)(2,1)}, u32[]{:S(2)}, u32[]{:S(2)}) collective-permute-start(bf16[320,1024]{1,0:T(8,128)(2,1)} %bitcast.24), channel_id=1, source_target_pairs={{0,16},{8,56},{16,32},{24,8},{32,48},{40,24},{48,0},{56,40},{64,80... | collective-permute-start | bytes 1966088 | tf_op jit(solution)/shard_map/ppermute | solution.py:422
  5.3 0.0 collective-permute-start.1
  5.3 2.7 %collective-permute-start.2 = (bf16[320,1024]{1,0:T(8,128)(2,1)}, bf16[320,1024]{1,0:T(8,128)(2,1)S(1)}, u32[]{:S(2)}, u32[]{:S(2)}) collective-permute-start(bf16[320,1024]{1,0:T(8,128)(2,1)} %bitcast.26), channel_id=1, source_target_pairs={{0,64},{8,72},{16,80},{24,88},{32,96},{40,104},{48,112},{56,120},{... | collective-permute-start | bytes 1966088 | tf_op jit(solution)/shard_map/ppermute | solution.py:422
  8.0 1.3 collective-permute-start.3
  9.4 0.7 pad_maximum_fusion.1
  10.1 21.0 %all_to_all.10 = bf16[16,64,256]{2,1,0:T(8,128)(2,1)} all-to-all(bf16[16,64,256]{2,1,0:T(8,128)(2,1)S(1)} %broadcast_in_dim.2), channel_id=1, replica_groups=mesh['seq'=16,'head'=8] {'seq'}, dimensions={0} | all-to-all | bytes 1048576 | tf_op jit(solution)/shard_map/all_to_all | solution.py:442
  31.2 0.0 collective-permute-done.refs_1_
  31.2 0.0 collective-permute-done.1.refs_2_
  31.2 0.0 collective-permute-done.2.refs_0_
  31.2 0.0 copy-start.2
  31.2 0.0 collective-permute-done.3.refs_4_
  31.2 0.9 copy-done.7
  32.1 0.4 collective-permute-start.4
  32.5 0.5 collective-permute-start.5
  33.7 1.1 collective-permute-start.9
  34.7 17.2 %attention_forward.1 = (bf16[8,1536,512]{2,1,0:T(8,128)(2,1)}, bf16[1024,512]{1,0:T(8,128)(2,1)}, bf16[512,1024]{1,0:T(8,128)(2,1)}, bf16[64,1024]{1,0:T(8,128)(2,1)}) custom-call(s32[1]{0:T(128)} %bitcast.10.index_ref, s32[1]{0:T(128)S(6)} %copy.30.length_ref, bf16[512,1024]{1,0:T(8,128)(2,1)} %query_ref.3, bf16[64,1024]{1,0:T(8,128)(2,1)} %prompt_query_ref.3, ...), custom_call_target="tpu_custom_call" | custom-call | flops 3221225472 | bytes 18874368 | tf_op jit(solution)/shard_map/attention_forward/pallas_call | solution.py:94
  51.9 0.0 collective-permute-done.4.refs_1_
  52.0 0.0 copy-start.3
  52.0 2.6 %collective-permute-start.6 = (bf16[320,1024]{1,0:T(8,128)(2,1)}, bf16[320,1024]{1,0:T(8,128)(2,1)}, u32[]{:S(2)}, u32[]{:S(2)}) collective-permute-start(bf16[320,1024]{1,0:T(8,128)(2,1)} %collective-permute-done.refs_1_), channel_id=1, source_target_pairs={{0,8},{8,0},{16,24},{24,16},{32,40},{40,32},{48,56},{56,48},{64,72... | collective-permute-start | bytes 1966088 | tf_op jit(solution)/shard_map/ppermute | solution.py:430
  54.5 0.1 collective-permute-start.7
  54.6 1.7 %collective-permute-start.10 = (bf16[320,1024]{1,0:T(8,128)(2,1)S(1)}, bf16[320,1024]{1,0:T(8,128)(2,1)S(1)}, u32[]{:S(2)}, u32[]{:S(2)}) collective-permute-start(bf16[320,1024]{1,0:T(8,128)(2,1)S(1)} %collective-permute-done.4.refs_1_), channel_id=1, source_target_pairs={{0,16},{8,56},{16,32},{24,8},{32,48},{40,24},{48,0},{56,40},{64,80... | collective-permute-start | bytes 1966088 | tf_op jit(solution)/shard_map/ppermute | solution.py:449
  56.3 0.0 collective-permute-done.5.refs_3_
  56.3 2.8 %collective-permute-start.8 = (bf16[320,1024]{1,0:T(8,128)(2,1)}, bf16[320,1024]{1,0:T(8,128)(2,1)}, u32[]{:S(2)}, u32[]{:S(2)}) collective-permute-start(bf16[320,1024]{1,0:T(8,128)(2,1)} %collective-permute-done.5.refs_3_), channel_id=1, source_target_pairs={{0,8},{8,0},{16,24},{24,16},{32,40},{40,32},{48,56},{56,48},{64,72... | collective-permute-start | bytes 1966088 | tf_op jit(solution)/shard_map/ppermute | solution.py:430
  59.2 0.0 collective-permute-done.9.refs_2_
  59.2 0.1 collective-permute-start.12
  59.3 0.0 collective-permute-done.6.refs_5_
  59.3 0.4 collective-permute-start.11
  59.7 0.0 collective-permute-done.7.refs_6_
  59.7 0.1 collective-permute-start.13
  59.8 4.6 %collective-permute-done.10.refs_3_ = bf16[320,1024]{1,0:T(8,128)(2,1)S(1)} collective-permute-done((bf16[320,1024]{1,0:T(8,128)(2,1)S(1)}, bf16[320,1024]{1,0:T(8,128)(2,1)S(1)}, u32[]{:S(2)}, u32[]{:S(2)}) %collective-permute-start.10) | collective-permute-done | bytes 655392 | tf_op jit(solution)/shard_map/ppermute | solution.py:449
  64.4 2.5 %collective-permute-start.14 = (bf16[320,1024]{1,0:T(8,128)(2,1)S(1)}, bf16[320,1024]{1,0:T(8,128)(2,1)}, u32[]{:S(2)}, u32[]{:S(2)}) collective-permute-start(bf16[320,1024]{1,0:T(8,128)(2,1)S(1)} %collective-permute-done.10.refs_3_), channel_id=1, source_target_pairs={{0,8},{8,0},{16,24},{24,16},{32,40},{40,32},{48,56},{56,48},{64,72... | collective-permute-start | bytes 1966088 | tf_op jit(solution)/shard_map/ppermute | solution.py:430
  66.8 0.6 pad_add_fusion.order_ref
  67.4 0.0 collective-permute-done.8.refs_7_
  67.4 8.6 %upstream.2.refs_10_ = f32[576,1024]{1,0:T(8,128)} custom-call(s32[4]{0:T(128)} %pad_add_fusion.order_ref, s32[1]{0:T(128)} %bitcast.4.core_ref, s32[1]{0:T(128)} %bitcast.7.half_ref, s32[1]{0:T(128)S(6)} %copy.30.length_ref, bf16[320,1024]{1,0:T(8,128)(2,1)} %bitcast.28, bf16[320,1024]{1,0:T(8,128)(2,1)} %collective-permute-done.refs_1_, ...), custom_call_target="tpu_custom_call" | custom-call | flops 3019898880 | bytes 9437184 | tf_op jit(solution)/shard_map/upstream/pallas_call | solution.py:380
  76.1 9.2 %head_products.2 = (bf16[4,288,640]{2,1,0:T(8,128)(2,1)}, bf16[4,288,640]{2,1,0:T(8,128)(2,1)}, bf16[2,288,640]{2,1,0:T(8,128)(2,1)}, bf16[2,288,640]{2,1,0:T(8,...) custom-call(s32[4]{0:T(128)} %pad_add_fusion.order_ref, s32[1]{0:T(128)} %bitcast.4.core_ref, ...), custom_call_target="tpu_custom_call" | custom-call | flops 3019898880 | bytes 9437184 | tf_op jit(solution)/shard_map/head_products/pallas_call | solution.py:318
  85.3 0.0 collective-permute-done.11.refs_4_
  85.4 0.8 copy-done.6
  86.2 9.3 %head_products.3 = (bf16[4,288,640]{2,1,0:T(8,128)(2,1)}, bf16[4,288,640]{2,1,0:T(8,128)(2,1)}, bf16[2,288,640]{2,1,0:T(8,128)(2,1)}, bf16[2,288,640]{2,1,0:T(8,...) custom-call(s32[4]{0:T(128)} %pad_add_fusion.order_ref, ...), custom_call_target="tpu_custom_call", output_to_operand_aliasing={{0}: (14, {}), {1}: (15, {}), {2}: (16, {}), {3}: (17, {}),... | custom-call | flops 3019898880 | bytes 9437184 | tf_op jit(solution)/shard_map/head_products/pallas_call | solution.py:318
  95.4 1.2 collective-permute-start.15
  96.7 1.3 collective-permute-start.16
  98.0 2.6 %collective-permute-start.17 = (bf16[2,288,640]{2,1,0:T(8,128)(2,1)}, bf16[2,288,640]{2,1,0:T(8,128)(2,1)}, u32[]{:S(2)}, u32[]{:S(2)}) collective-permute-start(bf16[2,288,640]{2,1,0:T(8,128)(2,1)} %get-tuple-element.99), channel_id=1, source_target_pairs={{0,4},{1,5},{2,6},{3,7},{4,0},{5,1},{6,2},{7,3},{8,12},{9,13},{10,... | collective-permute-start | bytes 2211848 | tf_op jit(solution)/shard_map/ppermute | solution.py:458
  100.6 1.0 collective-permute-start.18
  101.7 9.1 %upstream.3 = (bf16[64,1024]{1,0:T(8,128)(2,1)}, bf16[512,1024]{1,0:T(8,128)(2,1)}) custom-call(s32[4]{0:T(128)} %pad_add_fusion.order_ref, s32[1]{0:T(128)} %bitcast.4.core_ref, s32[1]{0:T(128)} %bitcast.6.half_ref, s32[1]{0:T(128)S(6)} %copy.30.length_ref, bf16[320,1024]{1,0:T(8,128)(2,1)} %copy-done.2, bf16[320,1024]{1,0:T(8,128)(2,1)} %copy-done.3, ...), custom_call_target="tpu_custom_call" | custom-call | flops 3019898880 | bytes 9437184 | tf_op jit(solution)/shard_map/upstream/pallas_call | solution.py:380
  110.7 21.8 %attention_backward.1 = (bf16[512,1024]{1,0:T(8,128)(2,1)}, bf16[64,1024]{1,0:T(8,128)(2,1)}, bf16[1024,256]{1,0:T(8,128)(2,1)}, bf16[512,128]{1,0:T(8,128)(2,1)}, bf16[512,128]{1,0:T(8,128)(2,1)}) custom-call(bf16[8,1536,512]{2,1,0:T(8,128)(2,1)} %get-tuple-element.101.weight_ref, bf16[1024,512]{1,0:T(8,128)(2,1)} %get-tuple-element.102.prompt_weight_ref, ...), custom_call_target="tpu_custom_call" | custom-call | flops 6442450944 | bytes 18874368 | tf_op jit(solution)/shard_map/attention_backward/pallas_call | solution.py:205
  132.5 0.5 collective-permute-done.17
  133.0 0.0 collective-permute-done.18
  133.0 1.7 %add_convert_fusion = bf16[2,288,640]{2,1,0:T(8,128)(2,1)S(1)} fusion(bf16[2,288,640]{2,1,0:T(8,128)(2,1)} %collective-permute-done.18, bf16[2,288,640]{2,1,0:T(8,128)(2,1)} %collective-permute-done.17, bf16[2,288,640]{2,1,0:T(8,128)(2,1)S(1)} %collective-permute-done.16, bf16[2,288,640]{2,1,0:T(8,128)(2,1)S(1)} %copy-done.1), kind=kLoop, calls=%fused_computation | loop fusion | flops 2949120 | bytes 3686400 | tf_op jit(solution)/shard_map/convert_element_type | solution.py:465
  134.7 0.1 slice_bitcast_fusion
  134.8 1.3 copy-done
  136.1 1.2 fusion.3
  137.3 0.8 collective-permute-start.19
  138.1 2.9 %collective-permute-start.20 = (bf16[288,640]{1,0:T(8,128)(2,1)}, bf16[288,640]{1,0:T(8,128)(2,1)S(1)}, u32[]{:S(2)}, u32[]{:S(2)}) collective-permute-start(bf16[288,640]{1,0:T(8,128)(2,1)} %get-tuple-element.109), channel_id=1, source_target_pairs={{0,4},{1,5},{2,6},{3,7},{4,0},{5,1},{6,2},{7,3},{8,12},{9,13},{10,... | collective-permute-start | bytes 1105928 | tf_op jit(solution)/shard_map/ppermute | solution.py:467
  141.0 0.4 collective-permute-start.21
  141.4 0.3 collective-permute-start.22
  141.7 9.0 %all-to-all-start.1 = ((bf16[16,64,256]{2,1,0:T(8,128)(2,1)}), bf16[16,64,256]{2,1,0:T(8,128)(2,1)S(1)}, u32[]{:S(2)}, u32[]{:S(2)}) async-start(bf16[16,64,256]{2,1,0:T(8,128)(2,1)} %bitcast.17), calls=%async_computation.1 | async-start | bytes 1048576 | tf_op jit(solution)/shard_map/all_to_all | solution.py:471
  150.7 6.6 %collective-permute-done.20 = bf16[288,640]{1,0:T(8,128)(2,1)S(1)} collective-permute-done((bf16[288,640]{1,0:T(8,128)(2,1)}, bf16[288,640]{1,0:T(8,128)(2,1)S(1)}, u32[]{:S(2)}, u32[]{:S(2)}) %collective-permute-start.20) | collective-permute-done | bytes 368672 | tf_op jit(solution)/shard_map/ppermute | solution.py:467
  157.3 0.2 add_convert_fusion.2
  157.5 0.6 slice.62
  158.1 0.0 collective-permute-done.22
  158.1 0.1 add_convert_fusion.1
  158.2 0.9 pad_maximum_fusion
  159.1 2.8 %all-to-all-done.1 = bf16[16,64,256]{2,1,0:T(8,128)(2,1)S(1)} async-done(((bf16[16,64,256]{2,1,0:T(8,128)(2,1)}), bf16[16,64,256]{2,1,0:T(8,128)(2,1)S(1)}, u32[]{:S(2)}, u32[]{:S(2)}) %all-to-all-start.1) | async-done | bytes 524320 | tf_op jit(solution)/shard_map/all_to_all | solution.py:471
  162.0 0.1 reduce_sum.12
  162.0 0.6 fusion.4
  (20 shorter events, 0.1 us)
Async XLA Ops:
  0.6 30.5 %collective-permute-start = (bf16[320,1024]{1,0:T(8,128)(2,1)}, bf16[320,1024]{1,0:T(8,128)(2,1)}, u32[]{:S(2)}, u32[]{:S(2)}) collective-permute-start(bf16[320,1024]{1,0:T(8,128)(2,1)} %bitcast.24), channel_id=1, source_target_pairs={{0,16},{8,56},{16,32},{24,8},{32,48},{40,24},{48,0},{56,40},{64,80... | collective-permute-start | bytes 1966088 | tf_op jit(solution)/shard_map/ppermute | solution.py:422
  5.3 25.9 %collective-permute-start.1 = (bf16[320,1024]{1,0:T(8,128)(2,1)}, bf16[320,1024]{1,0:T(8,128)(2,1)}, u32[]{:S(2)}, u32[]{:S(2)}) collective-permute-start(bf16[320,1024]{1,0:T(8,128)(2,1)} %bitcast.25), channel_id=1, source_target_pairs={{0,48},{8,24},{16,0},{24,40},{32,16},{40,56},{48,32},{56,8},{64,11... | collective-permute-start | bytes 1966088 | tf_op jit(solution)/shard_map/ppermute | solution.py:422
  5.3 25.9 %collective-permute-start.2 = (bf16[320,1024]{1,0:T(8,128)(2,1)}, bf16[320,1024]{1,0:T(8,128)(2,1)S(1)}, u32[]{:S(2)}, u32[]{:S(2)}) collective-permute-start(bf16[320,1024]{1,0:T(8,128)(2,1)} %bitcast.26), channel_id=1, source_target_pairs={{0,64},{8,72},{16,80},{24,88},{32,96},{40,104},{48,112},{56,120},{... | collective-permute-start | bytes 1966088 | tf_op jit(solution)/shard_map/ppermute | solution.py:422
  8.0 23.2 %collective-permute-start.3 = (bf16[320,1024]{1,0:T(8,128)(2,1)}, bf16[320,1024]{1,0:T(8,128)(2,1)S(1)}, u32[]{:S(2)}, u32[]{:S(2)}) collective-permute-start(bf16[320,1024]{1,0:T(8,128)(2,1)} %bitcast.27), channel_id=1, source_target_pairs={{0,8},{8,0},{16,24},{24,16},{32,40},{40,32},{48,56},{56,48},{64,72... | collective-permute-start | bytes 1966088 | tf_op jit(solution)/shard_map/ppermute | solution.py:430
  31.2 28.1 %copy-start.2 = (bf16[320,1024]{1,0:T(8,128)(2,1)}, bf16[320,1024]{1,0:T(8,128)(2,1)S(1)}, u32[]{:S(2)}) copy-start(bf16[320,1024]{1,0:T(8,128)(2,1)S(1)} %collective-permute-done.2.refs_0_) | copy-start | bytes 1966084
  31.2 0.9 copy-start.7
  32.1 19.8 %collective-permute-start.4 = (bf16[320,1024]{1,0:T(8,128)(2,1)S(1)}, bf16[320,1024]{1,0:T(8,128)(2,1)S(1)}, u32[]{:S(2)}, u32[]{:S(2)}) collective-permute-start(bf16[320,1024]{1,0:T(8,128)(2,1)S(1)} %collective-permute-done.2.refs_0_), channel_id=1, source_target_pairs={{0,16},{8,56},{16,32},{24,8},{32,48},{40,24},{48,0},{56,40},{64,80... | collective-permute-start | bytes 1966088 | tf_op jit(solution)/shard_map/ppermute | solution.py:426
  32.5 23.8 %collective-permute-start.5 = (bf16[320,1024]{1,0:T(8,128)(2,1)}, bf16[320,1024]{1,0:T(8,128)(2,1)}, u32[]{:S(2)}, u32[]{:S(2)}) collective-permute-start(bf16[320,1024]{1,0:T(8,128)(2,1)} %collective-permute-done.refs_1_), channel_id=1, source_target_pairs={{0,16},{8,56},{16,32},{24,8},{32,48},{40,24},{48,0},{56,40},{64,80... | collective-permute-start | bytes 1966088 | tf_op jit(solution)/shard_map/ppermute | solution.py:426
  33.7 25.5 %collective-permute-start.9 = (bf16[320,1024]{1,0:T(8,128)(2,1)S(1)}, bf16[320,1024]{1,0:T(8,128)(2,1)S(1)}, u32[]{:S(2)}, u32[]{:S(2)}) collective-permute-start(bf16[320,1024]{1,0:T(8,128)(2,1)S(1)} %collective-permute-done.2.refs_0_), channel_id=1, source_target_pairs={{0,48},{8,24},{16,0},{24,40},{32,16},{40,56},{48,32},{56,8},{64,11... | collective-permute-start | bytes 1966088 | tf_op jit(solution)/shard_map/ppermute | solution.py:426
  52.0 24.1 %copy-start.3 = (bf16[320,1024]{1,0:T(8,128)(2,1)}, bf16[320,1024]{1,0:T(8,128)(2,1)S(1)}, u32[]{:S(2)}) copy-start(bf16[320,1024]{1,0:T(8,128)(2,1)S(1)} %collective-permute-done.4.refs_1_) | copy-start | bytes 1966084
  52.0 7.3 %collective-permute-start.6 = (bf16[320,1024]{1,0:T(8,128)(2,1)}, bf16[320,1024]{1,0:T(8,128)(2,1)}, u32[]{:S(2)}, u32[]{:S(2)}) collective-permute-start(bf16[320,1024]{1,0:T(8,128)(2,1)} %collective-permute-done.refs_1_), channel_id=1, source_target_pairs={{0,8},{8,0},{16,24},{24,16},{32,40},{40,32},{48,56},{56,48},{64,72... | collective-permute-start | bytes 1966088 | tf_op jit(solution)/shard_map/ppermute | solution.py:430
  54.5 5.2 %collective-permute-start.7 = (bf16[320,1024]{1,0:T(8,128)(2,1)}, bf16[320,1024]{1,0:T(8,128)(2,1)}, u32[]{:S(2)}, u32[]{:S(2)}) collective-permute-start(bf16[320,1024]{1,0:T(8,128)(2,1)} %collective-permute-done.1.refs_2_), channel_id=1, source_target_pairs={{0,8},{8,0},{16,24},{24,16},{32,40},{40,32},{48,56},{56,48},{64,72... | collective-permute-start | bytes 1966088 | tf_op jit(solution)/shard_map/ppermute | solution.py:430
  54.6 9.7 %collective-permute-start.10 = (bf16[320,1024]{1,0:T(8,128)(2,1)S(1)}, bf16[320,1024]{1,0:T(8,128)(2,1)S(1)}, u32[]{:S(2)}, u32[]{:S(2)}) collective-permute-start(bf16[320,1024]{1,0:T(8,128)(2,1)S(1)} %collective-permute-done.4.refs_1_), channel_id=1, source_target_pairs={{0,16},{8,56},{16,32},{24,8},{32,48},{40,24},{48,0},{56,40},{64,80... | collective-permute-start | bytes 1966088 | tf_op jit(solution)/shard_map/ppermute | solution.py:449
  56.3 11.1 %collective-permute-start.8 = (bf16[320,1024]{1,0:T(8,128)(2,1)}, bf16[320,1024]{1,0:T(8,128)(2,1)}, u32[]{:S(2)}, u32[]{:S(2)}) collective-permute-start(bf16[320,1024]{1,0:T(8,128)(2,1)} %collective-permute-done.5.refs_3_), channel_id=1, source_target_pairs={{0,8},{8,0},{16,24},{24,16},{32,40},{40,32},{48,56},{56,48},{64,72... | collective-permute-start | bytes 1966088 | tf_op jit(solution)/shard_map/ppermute | solution.py:430
  59.2 16.9 %copy-start.4 = (bf16[320,1024]{1,0:T(8,128)(2,1)}, bf16[320,1024]{1,0:T(8,128)(2,1)S(1)}, u32[]{:S(2)}) copy-start(bf16[320,1024]{1,0:T(8,128)(2,1)S(1)} %collective-permute-done.9.refs_2_) | copy-start | bytes 1966084
  59.2 26.1 %collective-permute-start.12 = (bf16[320,1024]{1,0:T(8,128)(2,1)S(1)}, bf16[320,1024]{1,0:T(8,128)(2,1)S(1)}, u32[]{:S(2)}, u32[]{:S(2)}) collective-permute-start(bf16[320,1024]{1,0:T(8,128)(2,1)S(1)} %collective-permute-done.4.refs_1_), channel_id=1, source_target_pairs={{0,8},{8,0},{16,24},{24,16},{32,40},{40,32},{48,56},{56,48},{64,72... | collective-permute-start | bytes 1966088 | tf_op jit(solution)/shard_map/ppermute | solution.py:430
  59.3 26.1 %collective-permute-start.11 = (bf16[320,1024]{1,0:T(8,128)(2,1)S(1)}, bf16[320,1024]{1,0:T(8,128)(2,1)}, u32[]{:S(2)}, u32[]{:S(2)}) collective-permute-start(bf16[320,1024]{1,0:T(8,128)(2,1)S(1)} %collective-permute-done.2.refs_0_), channel_id=1, source_target_pairs={{0,8},{8,0},{16,24},{24,16},{32,40},{40,32},{48,56},{56,48},{64,72... | collective-permute-start | bytes 1966088 | tf_op jit(solution)/shard_map/ppermute | solution.py:430
  59.7 25.7 %collective-permute-start.13 = (bf16[320,1024]{1,0:T(8,128)(2,1)S(1)}, bf16[320,1024]{1,0:T(8,128)(2,1)}, u32[]{:S(2)}, u32[]{:S(2)}) collective-permute-start(bf16[320,1024]{1,0:T(8,128)(2,1)S(1)} %collective-permute-done.9.refs_2_), channel_id=1, source_target_pairs={{0,8},{8,0},{16,24},{24,16},{32,40},{40,32},{48,56},{56,48},{64,72... | collective-permute-start | bytes 1966088 | tf_op jit(solution)/shard_map/ppermute | solution.py:430
  64.4 11.7 %copy-start.5 = (bf16[320,1024]{1,0:T(8,128)(2,1)}, bf16[320,1024]{1,0:T(8,128)(2,1)S(1)}, u32[]{:S(2)}) copy-start(bf16[320,1024]{1,0:T(8,128)(2,1)S(1)} %collective-permute-done.10.refs_3_) | copy-start | bytes 1966084
  64.4 21.0 %collective-permute-start.14 = (bf16[320,1024]{1,0:T(8,128)(2,1)S(1)}, bf16[320,1024]{1,0:T(8,128)(2,1)}, u32[]{:S(2)}, u32[]{:S(2)}) collective-permute-start(bf16[320,1024]{1,0:T(8,128)(2,1)S(1)} %collective-permute-done.10.refs_3_), channel_id=1, source_target_pairs={{0,8},{8,0},{16,24},{24,16},{32,40},{40,32},{48,56},{56,48},{64,72... | collective-permute-start | bytes 1966088 | tf_op jit(solution)/shard_map/ppermute | solution.py:430
  85.3 0.8 copy-start.6
  95.4 39.4 %collective-permute-start.15 = (bf16[4,288,640]{2,1,0:T(8,128)(2,1)}, bf16[4,288,640]{2,1,0:T(8,128)(2,1)S(1)}, u32[]{:S(2)}, u32[]{:S(2)}) collective-permute-start(bf16[4,288,640]{2,1,0:T(8,128)(2,1)} %get-tuple-element.96), channel_id=1, source_target_pairs={{0,1},{1,0},{2,3},{3,2},{4,5},{5,4},{6,7},{7,6},{8,9},{9,8},{10,11... | collective-permute-start | bytes 4423688 | tf_op jit(solution)/shard_map/ppermute | solution.py:457
  96.7 35.9 %collective-permute-start.16 = (bf16[2,288,640]{2,1,0:T(8,128)(2,1)}, bf16[2,288,640]{2,1,0:T(8,128)(2,1)S(1)}, u32[]{:S(2)}, u32[]{:S(2)}) collective-permute-start(bf16[2,288,640]{2,1,0:T(8,128)(2,1)} %get-tuple-element.98), channel_id=1, source_target_pairs={{0,2},{1,3},{2,4},{3,5},{4,6},{5,7},{6,0},{7,1},{8,10},{9,11},{10,... | collective-permute-start | bytes 2211848 | tf_op jit(solution)/shard_map/ppermute | solution.py:458
  98.0 35.0 %collective-permute-start.17 = (bf16[2,288,640]{2,1,0:T(8,128)(2,1)}, bf16[2,288,640]{2,1,0:T(8,128)(2,1)}, u32[]{:S(2)}, u32[]{:S(2)}) collective-permute-start(bf16[2,288,640]{2,1,0:T(8,128)(2,1)} %get-tuple-element.99), channel_id=1, source_target_pairs={{0,4},{1,5},{2,6},{3,7},{4,0},{5,1},{6,2},{7,3},{8,12},{9,13},{10,... | collective-permute-start | bytes 2211848 | tf_op jit(solution)/shard_map/ppermute | solution.py:458
  100.6 32.4 %collective-permute-start.18 = (bf16[2,288,640]{2,1,0:T(8,128)(2,1)}, bf16[2,288,640]{2,1,0:T(8,128)(2,1)}, u32[]{:S(2)}, u32[]{:S(2)}) collective-permute-start(bf16[2,288,640]{2,1,0:T(8,128)(2,1)} %get-tuple-element.100), channel_id=1, source_target_pairs={{0,6},{1,7},{2,0},{3,1},{4,2},{5,3},{6,4},{7,5},{8,14},{9,15},{10,... | collective-permute-start | bytes 2211848 | tf_op jit(solution)/shard_map/ppermute | solution.py:458
  110.7 22.3 %copy-start.1 = (bf16[2,288,640]{2,1,0:T(8,128)(2,1)S(1)}, bf16[2,288,640]{2,1,0:T(8,128)(2,1)}, u32[]{:S(2)}) copy-start(bf16[2,288,640]{2,1,0:T(8,128)(2,1)} %get-tuple-element.97) | copy-start | bytes 2211844
  134.7 1.4 copy-start
  137.3 13.4 %collective-permute-start.19 = (bf16[288,640]{1,0:T(8,128)(2,1)}, bf16[288,640]{1,0:T(8,128)(2,1)S(1)}, u32[]{:S(2)}, u32[]{:S(2)}) collective-permute-start(bf16[288,640]{1,0:T(8,128)(2,1)} %get-tuple-element.108), channel_id=1, source_target_pairs={{0,2},{1,3},{2,4},{3,5},{4,6},{5,7},{6,0},{7,1},{8,10},{9,11},{10,... | collective-permute-start | bytes 1105928 | tf_op jit(solution)/shard_map/ppermute | solution.py:467
  138.1 19.2 %collective-permute-start.20 = (bf16[288,640]{1,0:T(8,128)(2,1)}, bf16[288,640]{1,0:T(8,128)(2,1)S(1)}, u32[]{:S(2)}, u32[]{:S(2)}) collective-permute-start(bf16[288,640]{1,0:T(8,128)(2,1)} %get-tuple-element.109), channel_id=1, source_target_pairs={{0,4},{1,5},{2,6},{3,7},{4,0},{5,1},{6,2},{7,3},{8,12},{9,13},{10,... | collective-permute-start | bytes 1105928 | tf_op jit(solution)/shard_map/ppermute | solution.py:467
  141.0 16.3 %collective-permute-start.21 = (bf16[288,640]{1,0:T(8,128)(2,1)S(1)}, bf16[288,640]{1,0:T(8,128)(2,1)S(1)}, u32[]{:S(2)}, u32[]{:S(2)}) collective-permute-start(bf16[288,640]{1,0:T(8,128)(2,1)S(1)} %get-tuple-element.110), channel_id=1, source_target_pairs={{0,6},{1,7},{2,0},{3,1},{4,2},{5,3},{6,4},{7,5},{8,14},{9,15},{10,... | collective-permute-start | bytes 1105928 | tf_op jit(solution)/shard_map/ppermute | solution.py:467
  141.4 16.8 %collective-permute-start.22 = (bf16[288,640]{1,0:T(8,128)(2,1)S(1)}, bf16[288,640]{1,0:T(8,128)(2,1)S(1)}, u32[]{:S(2)}, u32[]{:S(2)}) collective-permute-start(bf16[288,640]{1,0:T(8,128)(2,1)S(1)} %get-tuple-element.112), channel_id=1, source_target_pairs={{0,1},{1,0},{2,3},{3,2},{4,5},{5,4},{6,7},{7,6},{8,9},{9,8},{10,11... | collective-permute-start | bytes 1105928 | tf_op jit(solution)/shard_map/ppermute | solution.py:468
  141.7 20.3 %all-to-all-start.1 = ((bf16[16,64,256]{2,1,0:T(8,128)(2,1)}), bf16[16,64,256]{2,1,0:T(8,128)(2,1)S(1)}, u32[]{:S(2)}, u32[]{:S(2)}) async-start(bf16[16,64,256]{2,1,0:T(8,128)(2,1)} %bitcast.17), calls=%async_computation.1 | async-start | bytes 1048576 | tf_op jit(solution)/shard_map/all_to_all | solution.py:471

commit v3 on v2

--- a/solution.py
+++ b/solution.py
@@ -10,6 +10,7 @@
 F32 = jnp.float32
 SCALE = DIM**-0.5
 EXP_SCALE = SCALE * 1.4426950408889634
+PER = 2
 VMEM_LIMIT = 60 * 1024 * 1024
 
 
@@ -21,9 +22,16 @@
     return lax.dot_general(a, b, (((1,), (1,)), ((), ())), preferred_element_type=F32)
 
 
+def fold(part):
+    while part.shape[0] > 8:
+        half = part.shape[0] // 2
+        part = jnp.maximum(part[:half], part[half:])
+    return part
+
+
 def forward_kernel(
     index_ref, length_ref, query_ref, prompt_query_ref, key_ref, value_ref, reply_key_ref, reply_value_ref,
-    weight_ref, prompt_weight_ref, out_ref, prompt_out_ref, value_t, scores, stack,
+    weight_ref, prompt_weight_ref, out_ref, prompt_out_ref, inverse_ref, prompt_inverse_ref, value_t, scores, stack,
 ):
     step = pl.program_id(0)
     heads = pl.num_programs(0) - 1
@@ -34,51 +42,85 @@
 
     @pl.when(step == 0)
     def _():
-        value_t[:, :prompt] = value_ref[...].T
-        value_t[:, prompt:] = reply_value_ref[...].T
-
-    @pl.when(step < heads)
-    def _():
-        query = query_ref[...]
+        value_t[:DIM, :prompt] = value_ref[...].T
+        value_t[:DIM, prompt:] = reply_value_ref[...].T
+        value_t[DIM:, :] = jnp.ones((value_t.shape[0] - DIM, keys), BF)
+
+    def raise_block(slot, block, lanes, shift, seen=None):
+        part = scores[slot, block, lanes]
+        if seen is not None:
+            part = jnp.where(seen, part, -jnp.inf)
+        return jnp.exp2(part * EXP_SCALE - shift).astype(BF)
+
+    def divide(total):
+        inverse = 1.0 / total[DIM : DIM + 1, :]
+        return (total[:DIM, :] * inverse).T, jnp.broadcast_to(inverse, (DIM, rows)).T
+
+    def score(slot):
+        query = query_ref[:, slot * DIM : (slot + 1) * DIM]
         half = rows // 2
-        scores[:prompt, :] = dot_nt(key_ref[...], query)
-        scores[prompt : prompt + half, :] = dot_nt(reply_key_ref[:half], query)
-        scores[prompt + half :, half:] = dot_nt(reply_key_ref[half:], query[half:])
+        upper = None
+        for start in range(0, prompt, 256):
+            part = dot_nt(key_ref[start : start + 256, :], query)
+            scores[slot, start : start + 256, :] = part
+            upper = fold(part) if upper is None else jnp.maximum(upper, fold(part))
+        scores[slot, prompt : prompt + half, :] = dot_nt(reply_key_ref[:half], query)
+        scores[slot, prompt + half :, half:] = dot_nt(reply_key_ref[half:], query[half:])
+        return upper
+
+    def weigh(slot, upper):
         seen = lax.broadcasted_iota(jnp.int32, (DIM, DIM), 0) <= lax.broadcasted_iota(jnp.int32, (DIM, DIM), 1)
         for tile in range(rows // DIM):
             lanes = slice(tile * DIM, (tile + 1) * DIM)
             full = prompt + tile * DIM
-            wide = scores[:full, lanes]
-            diag = jnp.where(seen, scores[full : full + DIM, lanes], -jnp.inf)
-            top = jnp.maximum(jnp.max(wide, axis=0, keepdims=True), jnp.max(diag, axis=0, keepdims=True))
-            wide = jnp.exp2((wide - top) * EXP_SCALE)
-            diag = jnp.exp2((diag - top) * EXP_SCALE)
-            total = jnp.sum(wide, axis=0, keepdims=True) + jnp.sum(diag, axis=0, keepdims=True)
-            inverse = 1.0 / total
-            weight_ref[0, :full, lanes] = (wide * inverse).astype(BF)
-            weight_ref[0, full : full + DIM, lanes] = (diag * inverse).astype(BF)
+            top = jnp.maximum(upper[:, lanes], fold(jnp.where(seen, scores[slot, full : full + DIM, lanes], -jnp.inf)))
+            for start in range(prompt, full, DIM):
+                top = jnp.maximum(top, fold(scores[slot, start : start + DIM, lanes]))
+            shift = jnp.max(top, axis=0, keepdims=True) * EXP_SCALE
+            for start in range(0, full, DIM):
+                block = slice(start, start + DIM)
+                weight_ref[slot, block, lanes] = raise_block(slot, block, lanes, shift)
+            block = slice(full, full + DIM)
+            weight_ref[slot, block, lanes] = raise_block(slot, block, lanes, shift, seen)
             if full + DIM < keys:
-                weight_ref[0, full + DIM :, lanes] = jnp.zeros((keys - full - DIM, DIM), BF)
-        out = dot_nn(value_t[...], weight_ref[0]).T
+                weight_ref[slot, full + DIM :, lanes] = jnp.zeros((keys - full - DIM, DIM), BF)
+
+    def attend(slot):
+        lanes = slice(slot * DIM, (slot + 1) * DIM)
+        out, inverse = divide(dot_nn(value_t[...], weight_ref[slot]))
         live = lax.broadcasted_iota(jnp.int32, (rows, DIM), 0) < length_ref[0]
-        out_ref[...] = jnp.where(live, out, 0.0).astype(BF)
+        out_ref[:, lanes] = jnp.where(live, out, 0.0).astype(BF)
+        inverse_ref[:, lanes] = inverse
+
+    @pl.when(step < heads)
+    def _():
+        upper = score(0)
+        for slot in range(PER):
+            following = score(slot + 1) if slot + 1 < PER else None
+            weigh(slot, upper)
+            attend(slot)
+            upper = following
 
     @pl.when(step == heads)
     def _():
         for head in range(rows // prompt_rows):
             stack[head * prompt_rows : (head + 1) * prompt_rows, :] = prompt_query_ref[:, head * DIM : (head + 1) * DIM]
-        scores[:prompt, :] = dot_nt(key_ref[...], stack[...])
-        first = index_ref[0] * prompt_rows
+        scores[0, :prompt, :] = dot_nt(key_ref[...], stack[...])
+        place = lax.broadcasted_iota(jnp.int32, (DIM, DIM), 1) % prompt_rows + index_ref[0] * prompt_rows
         for tile in range(rows // DIM):
             lanes = slice(tile * DIM, (tile + 1) * DIM)
-            place = lax.broadcasted_iota(jnp.int32, (prompt, DIM), 1) % prompt_rows + first
-            seen = lax.broadcasted_iota(jnp.int32, (prompt, DIM), 0) <= place
-            part = jnp.where(seen, scores[:prompt, lanes], -jnp.inf)
-            top = jnp.max(part, axis=0, keepdims=True)
-            part = jnp.exp2((part - top) * EXP_SCALE)
-            inverse = 1.0 / jnp.sum(part, axis=0, keepdims=True)
-            prompt_weight_ref[:, lanes] = (part * inverse).astype(BF)
-        out = dot_nn(value_t[:, :prompt], prompt_weight_ref[...]).T.astype(BF)
+            masks = [lax.broadcasted_iota(jnp.int32, (DIM, DIM), 0) + start <= place for start in range(0, prompt, DIM)]
+            top = None
+            for start, seen in zip(range(0, prompt, DIM), masks):
+                part = fold(jnp.where(seen, scores[0, start : start + DIM, lanes], -jnp.inf))
+                top = part if top is None else jnp.maximum(top, part)
+            top = jnp.max(top, axis=0, keepdims=True)
+            for start, seen in zip(range(0, prompt, DIM), masks):
+                block = slice(start, start + DIM)
+                prompt_weight_ref[block, lanes] = raise_block(0, block, lanes, top * EXP_SCALE, seen)
+        out, inverse = divide(dot_nn(value_t[:, :prompt], prompt_weight_ref[...]))
+        prompt_inverse_ref[...] = inverse
+        out = out.astype(BF)
         for head in range(rows // prompt_rows):
             prompt_out_ref[:, head * DIM : (head + 1) * DIM] = out[head * prompt_rows : (head + 1) * prompt_rows, :]
 
@@ -89,15 +131,16 @@
     heads = columns // DIM
     prompt = kv.shape[0]
     keys = prompt + rows
-    last = heads - 1
+    steps = heads // PER
+    last = steps - 1
     whole = lambda shape: pl.BlockSpec(shape, lambda g: (0, 0))
     return pl.pallas_call(
         forward_kernel,
-        grid=(heads + 1,),
+        grid=(steps + 1,),
         in_specs=[
             pl.BlockSpec(memory_space=pltpu.SMEM),
             pl.BlockSpec(memory_space=pltpu.SMEM),
-            pl.BlockSpec((rows, DIM), lambda g: (0, jnp.minimum(g, last))),
+            pl.BlockSpec((rows, PER * DIM), lambda g: (0, jnp.minimum(g, last))),
             whole((prompt_rows, columns)),
             pl.BlockSpec((prompt, DIM), lambda g: (0, 0)),
             pl.BlockSpec((prompt, DIM), lambda g: (0, 1)),
@@ -105,20 +148,24 @@
             whole((rows, DIM)),
         ],
         out_specs=[
-            pl.BlockSpec((1, keys, rows), lambda g: (jnp.minimum(g, last), 0, 0)),
+            pl.BlockSpec((PER, keys, rows), lambda g: (jnp.minimum(g, last), 0, 0)),
             whole((prompt, rows)),
-            pl.BlockSpec((rows, DIM), lambda g: (0, jnp.minimum(g, last))),
+            pl.BlockSpec((rows, PER * DIM), lambda g: (0, jnp.minimum(g, last))),
             whole((prompt_rows, columns)),
+            pl.BlockSpec((rows, PER * DIM), lambda g: (0, jnp.minimum(g, last))),
+            whole((rows, DIM)),
         ],
         out_shape=[
             jax.ShapeDtypeStruct((heads, keys, rows), BF),
             jax.ShapeDtypeStruct((prompt, rows), BF),
             jax.ShapeDtypeStruct((rows, columns), BF),
             jax.ShapeDtypeStruct((prompt_rows, columns), BF),
+            jax.ShapeDtypeStruct((rows, columns), F32),
+            jax.ShapeDtypeStruct((rows, DIM), F32),
         ],
         scratch_shapes=[
-            pltpu.VMEM((DIM, keys), BF),
-            pltpu.VMEM((keys, rows), F32),
+            pltpu.VMEM((DIM + 16, keys), BF),
+            pltpu.VMEM((PER, keys, rows), F32),
             pltpu.VMEM((rows, DIM), BF),
         ],
         compiler_params=pltpu.CompilerParams(vmem_limit_bytes=VMEM_LIMIT),
@@ -129,7 +176,7 @@
 
 def backward_kernel(
     weight_ref, prompt_weight_ref, query_ref, grad_ref, out_ref, prompt_query_ref, prompt_grad_ref, prompt_out_ref,
-    key_ref, value_ref, reply_key_ref, reply_value_ref,
+    inverse_ref, prompt_inverse_ref, key_ref, value_ref, reply_key_ref, reply_value_ref,
     query_grad_ref, prompt_query_grad_ref, kv_grad_ref, reply_key_grad_ref, reply_value_grad_ref,
     key_t, score_grad, key_grad, value_grad, stack,
 ):
@@ -147,30 +194,33 @@
         key_t[:, prompt:] = reply_key_ref[...].T
         key_grad[...] = jnp.zeros_like(key_grad)
         value_grad[...] = jnp.zeros_like(value_grad)
-        score_grad[prompt + half :, :half] = jnp.zeros((half, half), BF)
+        score_grad[:, prompt + half :, :half] = jnp.zeros((PER, half, half), BF)
 
     def row_delta(grad, out):
         return jnp.sum((grad.astype(F32) * out.astype(F32)).T, axis=0, keepdims=True)
 
-    def key_block(weight, value, grad, query, delta, start, size, low):
+    def key_block(slot, weight, value, grad, query, delta, start, size, low):
         block = slice(start, start + size)
         slope = dot_nt(value, grad)
         part = (weight.astype(F32) * (slope - delta)).astype(BF)
-        score_grad[block, low:] = part
+        score_grad[slot, block, low:] = part
         key_grad[block, :] += dot_nn(part, query)
         value_grad[block, :] += dot_nn(weight, grad)
 
     @pl.when(step < heads)
     def _():
-        query, grad = query_ref[...], grad_ref[...]
-        delta = row_delta(grad, out_ref[...])
-        for start in range(0, prompt, 256):
-            key_block(weight_ref[0, start : start + 256, :], value_ref[start : start + 256, :], grad, query, delta, start, 256, 0)
-        key_block(weight_ref[0, prompt : prompt + half, :], reply_value_ref[:half], grad, query, delta, prompt, half, 0)
-        key_block(
-            weight_ref[0, prompt + half :, half:], reply_value_ref[half:], grad[half:], query[half:], delta[:, half:], prompt + half, half, half
-        )
-        query_grad_ref[...] = (dot_nn(key_t[...], score_grad[...]).T * SCALE).astype(BF)
+        for slot in range(PER):
+            lanes = slice(slot * DIM, (slot + 1) * DIM)
+            query, grad = query_ref[:, lanes], (grad_ref[:, lanes].astype(F32) * inverse_ref[:, lanes]).astype(BF)
+            delta = row_delta(grad, out_ref[:, lanes])
+            for start in range(0, prompt, 512):
+                key_block(slot, weight_ref[slot, start : start + 512, :], value_ref[start : start + 512, :], grad, query, delta, start, 512, 0)
+            key_block(slot, weight_ref[slot, prompt : prompt + half, :], reply_value_ref[:half], grad, query, delta, prompt, half, 0)
+            key_block(
+                slot, weight_ref[slot, prompt + half :, half:], reply_value_ref[half:], grad[half:], query[half:], delta[:, half:],
+                prompt + half, half, half,
+            )
+            query_grad_ref[:, lanes] = (dot_nn(key_t[...], score_grad[slot]).T * SCALE).astype(BF)
 
     @pl.when(step == heads)
     def _():
@@ -180,11 +230,11 @@
             stack[0, place, :] = prompt_query_ref[:, lanes]
             stack[1, place, :] = prompt_grad_ref[:, lanes]
             stack[2, place, :] = prompt_out_ref[:, lanes]
-        query, grad = stack[0], stack[1]
+        query, grad = stack[0], (stack[1].astype(F32) * prompt_inverse_ref[...]).astype(BF)
         delta = row_delta(grad, stack[2])
-        for start in range(0, prompt, 256):
-            key_block(prompt_weight_ref[start : start + 256, :], value_ref[start : start + 256, :], grad, query, delta, start, 256, 0)
-        result = (dot_nn(key_t[:, :prompt], score_grad[:prompt, :]).T * SCALE).astype(BF)
+        for start in range(0, prompt, 512):
+            key_block(0, prompt_weight_ref[start : start + 512, :], value_ref[start : start + 512, :], grad, query, delta, start, 512, 0)
+        result = (dot_nn(key_t[:, :prompt], score_grad[0, :prompt, :]).T * SCALE).astype(BF)
         for head in range(count):
             prompt_query_grad_ref[:, head * DIM : (head + 1) * DIM] = result[head * prompt_rows : (head + 1) * prompt_rows, :]
         kv_grad_ref[:, :DIM] = (key_grad[:prompt, :] * SCALE).astype(BF)
@@ -193,20 +243,21 @@
         reply_value_grad_ref[...] = value_grad[prompt:, :].astype(BF)
 
 
-def attention_backward(weights, prompt_weights, reply_query, reply_up, reply_att, prompt_query, prompt_up, prompt_att, kv, reply_key, reply_value):
+def attention_backward(weights, prompt_weights, inverse, prompt_inverse, reply_query, reply_up, reply_att, prompt_query, prompt_up, prompt_att, kv, reply_key, reply_value):
     rows, columns = reply_query.shape
     prompt_rows = prompt_query.shape[0]
     heads = columns // DIM
     prompt = kv.shape[0]
     keys = prompt + rows
-    last = heads - 1
+    steps = heads // PER
+    last = steps - 1
     whole = lambda shape: pl.BlockSpec(shape, lambda g: (0, 0))
-    column = pl.BlockSpec((rows, DIM), lambda g: (0, jnp.minimum(g, last)))
+    column = pl.BlockSpec((rows, PER * DIM), lambda g: (0, jnp.minimum(g, last)))
     return pl.pallas_call(
         backward_kernel,
-        grid=(heads + 1,),
+        grid=(steps + 1,),
         in_specs=[
-            pl.BlockSpec((1, keys, rows), lambda g: (jnp.minimum(g, last), 0, 0)),
+            pl.BlockSpec((PER, keys, rows), lambda g: (jnp.minimum(g, last), 0, 0)),
             whole((prompt, rows)),
             column,
             column,
@@ -214,6 +265,8 @@
             whole((prompt_rows, columns)),
             whole((prompt_rows, columns)),
             whole((prompt_rows, columns)),
+            column,
+            whole((rows, DIM)),
             pl.BlockSpec((prompt, DIM), lambda g: (0, 0)),
             pl.BlockSpec((prompt, DIM), lambda g: (0, 1)),
             whole((rows, DIM)),
@@ -235,7 +288,7 @@
         ],
         scratch_shapes=[
             pltpu.VMEM((DIM, keys), BF),
-            pltpu.VMEM((keys, rows), BF),
+            pltpu.VMEM((PER, keys, rows), BF),
             pltpu.VMEM((keys, DIM), F32),
             pltpu.VMEM((keys, DIM), F32),
             pltpu.VMEM((3, rows, DIM), BF),
@@ -243,7 +296,7 @@
         compiler_params=pltpu.CompilerParams(vmem_limit_bytes=VMEM_LIMIT),
         cost_estimate=pl.CostEstimate(flops=8 * heads * keys * rows * DIM, bytes_accessed=18 * 2**20, transcendentals=0),
         name="attention_backward",
-    )(weights, prompt_weights, reply_query, reply_up, reply_att, prompt_query, prompt_up, prompt_att, kv, kv, reply_key, reply_value)
+    )(weights, prompt_weights, reply_query, reply_up, reply_att, prompt_query, prompt_up, prompt_att, inverse, prompt_inverse, kv, kv, reply_key, reply_value)
 
 
 def half_copies(chunks, order_ref, core_ref, gathered, sems):
@@ -418,18 +471,6 @@
     return [(y * 2 + x, ((y + dy) % 4) * 2 + (x + dx) % 2) for y in range(4) for x in range(2)]
 
 
-def gather_first(own):
-    return [own] + [lax.ppermute(own, "seq", perm) for perm in (ALONG, AGAINST, PEER)]
-
-
-def gather_second(along, peer):
-    return [lax.ppermute(along, "seq", ALONG), lax.ppermute(peer, "seq", ALONG), lax.ppermute(peer, "seq", AGAINST)]
-
-
-def sibling(chunk):
-    return lax.ppermute(chunk, "seq", SIBLING)
-
-
 def body(prompt_query, prompt_key, prompt_value, reply_query, reply_key, reply_value, lengths, out_weight, prompt_grad, reply_grad):
     prompt_rows = prompt_query.shape[0]
     n_seq = lax.axis_size("seq")
@@ -440,25 +481,30 @@
     core, near, other, head = scalar(core), scalar(x), scalar(1 - x), scalar(head)
     own = jnp.concatenate([prompt_key, prompt_value], 1)
     kv = lax.all_to_all(jnp.broadcast_to(own[None], (n_seq,) + own.shape), "seq", 0, 0).reshape(n_seq * prompt_rows, 2 * DIM)
-    mine, along, against, peer = gather_first(out_weight.T)
-    mine_twin = sibling(mine)
-    along, against, peer, mine_twin, kv = lax.optimization_barrier((along, against, peer, mine_twin, kv))
-    far, peer_along, peer_against = gather_second(along, peer)
-    weights, prompt_weights, reply_att, prompt_att = attention_forward(scalar(seq), lengths, reply_query, prompt_query, kv, reply_key, reply_value)
-    along, against, peer, peer_along, reply_att = lax.optimization_barrier((along, against, peer, peer_along, reply_att))
-    peer_far = lax.ppermute(peer_along, "seq", ALONG)
-    near_chunks = [mine, along, against, far, mine_twin] + [sibling(chunk) for chunk in (along, against, far)]
-    far_chunks = [peer, peer_along, peer_against, peer_far]
-    far_chunks = far_chunks + [sibling(chunk) for chunk in far_chunks]
+    mine = out_weight.T
+    send = lambda chunk, perm: lax.ppermute(chunk, "seq", perm)
+    along, against, peer = [send(mine, perm) for perm in (ALONG, AGAINST, PEER)]
+    along, against, peer, kv = lax.optimization_barrier((along, against, peer, kv))
+    far, peer_along = send(along, ALONG), send(peer, ALONG)
+    near_twins = [send(chunk, SIBLING) for chunk in (mine, along, against)]
+    weights, prompt_weights, reply_att, prompt_att, inverse, prompt_inverse = attention_forward(
+        scalar(seq), lengths, reply_query, prompt_query, kv, reply_key, reply_value
+    )
+    far, peer, peer_along, near_twins, reply_att = lax.optimization_barrier((far, peer, peer_along, near_twins, reply_att))
+    near_chunks = [mine, along, against, far, *near_twins, send(far, SIBLING)]
+    peer_against, peer_far = send(peer, AGAINST), send(peer_along, ALONG)
+    peer_twins = [send(chunk, SIBLING) for chunk in (peer, peer_along)]
     (partial,) = upstream(order, core, near, lengths, near_chunks, prompt_grad, reply_grad, None)
     products = head_products(order, core, head, near, near_chunks, prompt_att, reply_att, ())
-    partial, products, far_chunks = lax.optimization_barrier((partial, products, far_chunks))
+    partial, products, peer_against, peer_far = lax.optimization_barrier((partial, products, peer_against, peer_far))
+    peer_twins = peer_twins + [send(chunk, SIBLING) for chunk in (peer_against, peer_far)]
+    far_chunks = [peer, peer_along, peer_against, peer_far, *peer_twins]
     kept, sent, *turns = head_products(order, core, head, other, far_chunks, prompt_att, reply_att, products)
     came = lax.ppermute(sent, "head", head_perm(0, 1))
     turned = [lax.ppermute(turns[dy], "head", head_perm(dy, 0)) for dy in (1, 2, 3)]
     prompt_up, reply_up = upstream(order, core, other, lengths, far_chunks, prompt_grad, reply_grad, partial)
     query_grad, prompt_query_grad, kv_grad, reply_key_grad, reply_value_grad = attention_backward(
-        weights, prompt_weights, reply_query, reply_up, reply_att, prompt_query, prompt_up, prompt_att, kv, reply_key, reply_value
+        weights, prompt_weights, inverse, prompt_inverse, reply_query, reply_up, reply_att, prompt_query, prompt_up, prompt_att, kv, reply_key, reply_value
     )
     first = [(kept[dy].astype(F32) + came[dy].astype(F32)).astype(BF) for dy in range(4)]
     second = turns[0].astype(F32) + turned[0].astype(F32) + turned[1].astype(F32) + turned[2].astype(F32)

time: 163 us -> 155 us (0.951)
  blocking collectives: 21 us -> 0 us
  waiting for transfers between devices: 14.5 us -> 31 us
  Pallas kernels: 75.2 us -> 71.6 us
    all_to_all x1 -> x0, blocking collectives: 21 us -> none  [body(): lax.all_to_all(jnp.broadcast_to(own[None], (n_seq,) + own.shape), 'seq',...]
    all_to_all x0 -> x1, waiting for transfers between devices: none -> 16.5 us  [body(): lax.all_to_all(jnp.broadcast_to(own[None], (n_seq,) + own.shape), 'seq',...]
    ppermute x15, starting transfers between devices: 21 us -> 16.2 us  [body(): send = lambda chunk, perm: lax.ppermute(chunk, 'seq', perm)]
    all_to_all x0 -> x1, starting transfers between devices: none -> 4.68 us  [body(): lax.all_to_all(jnp.broadcast_to(own[None], (n_seq,) + own.shape), 'seq',...]
    pallas_call x2, Pallas kernels: 39 us -> 35.4 us  [the longest x1 19.5 us: attention_backward(): pl.pallas_call(backward_kernel, grid=(steps + 1,), in_specs=[pl.BlockSpec...]
    ppermute x3, waiting for transfers between devices: 0.46 us -> 2.35 us  [body(): lax.ppermute(turns[dy], 'head', head_perm(dy, 0))]
    ppermute x15, waiting for transfers between devices: 4.61 us -> 2.72 us  [body(): send = lambda chunk, perm: lax.ppermute(chunk, 'seq', perm)]
    unnamed x16 -> x22, local copies, waits for them, and re-layouts: 3.02 us -> 1.33 us
  transfers between devices with their start and end apart: 24 -> 25, of which waited for: 4 -> 6; matrix products, arithmetic and copies ran while one was open for 3% -> 4% of each run, Pallas kernels for 41% -> 40%
where the time goes in v3:
time: 155 us
  Pallas kernels  71.6 us (46%)
  starting transfers between devices  41.2 us (27%)
  waiting for transfers between devices  31 us (20%)
  other arithmetic  5.49 us (4%)
  local copies, waits for them, and re-layouts  3.52 us (2%)
  between operations  1.67 us (1%)
    pallas_call x1, Pallas kernels, attention_backward(): pl.pallas_call(backward_kernel, grid=(steps + 1,), in_specs=[pl.BlockSpec...  19.5 us
    pallas_call x2, Pallas kernels, head_products(): pl.pallas_call(products_kernel, in_specs=[scalar] * 4 + [anywhere] * 8 +...  18.6 us
    pallas_call x2, Pallas kernels, upstream(): pl.pallas_call(upstream_kernel, grid=(parts,), in_specs=[scalar] * 4 + [a...  17.7 us
    all_to_all x1, waiting for transfers between devices, body(): lax.all_to_all(jnp.broadcast_to(own[None], (n_seq,) + own.shape), 'seq',...  16.5 us
    ppermute x15, starting transfers between devices, body(): send = lambda chunk, perm: lax.ppermute(chunk, 'seq', perm)  16.2 us
    pallas_call x1, Pallas kernels, attention_forward(): pl.pallas_call(forward_kernel, grid=(steps + 1,), in_specs=[pl.BlockSpec(...  15.9 us
    all_to_all x1, starting transfers between devices, body(): lax.all_to_all(kv_grad.reshape(n_seq, prompt_rows, 2 * DIM), 'seq', 0, 0)  9.78 us
    ppermute x3, waiting for transfers between devices, body(): lax.ppermute(first[dy], 'head', head_perm(dy, 0))  6.22 us
  transfers between devices with their start and end apart: 25, of which 6 were waited for; matrix products, arithmetic and copies ran while one was open for 4% of the time, Pallas kernels for 40%

profile of v3, /device:TPU:1, one launch (start us, length us, event | category | flops | bytes accessed | tf_op | source)
XLA Modules:
  0.0 154.5 jit_solution(2011782920009447442)
XLA Ops:
  0.6 0.0 copy-start.7
  0.6 4.7 %collective-permute-start = (bf16[320,1024]{1,0:T(8,128)(2,1)}, bf16[320,1024]{1,0:T(8,128)(2,1)S(1)}, u32[]{:S(2)}, u32[]{:S(2)}) collective-permute-start(bf16[320,1024]{1,0:T(8,128)(2,1)} %bitcast.24), channel_id=1, source_target_pairs={{0,16},{8,56},{16,32},{24,8},{32,48},{40,24},{48,0},{56,40},{64,80... | collective-permute-start | bytes 1966088 | tf_op jit(solution)/shard_map/ppermute | solution.py:485
  5.3 0.0 collective-permute-start.1
  5.3 2.7 %collective-permute-start.2 = (bf16[320,1024]{1,0:T(8,128)(2,1)}, bf16[320,1024]{1,0:T(8,128)(2,1)S(1)}, u32[]{:S(2)}, u32[]{:S(2)}) collective-permute-start(bf16[320,1024]{1,0:T(8,128)(2,1)} %bitcast.26), channel_id=1, source_target_pairs={{0,64},{8,72},{16,80},{24,88},{32,96},{40,104},{48,112},{56,120},{... | collective-permute-start | bytes 1966088 | tf_op jit(solution)/shard_map/ppermute | solution.py:485
  8.0 0.7 pad_maximum_fusion.1
  8.8 0.8 broadcast_in_dim.2
  9.6 4.7 %all-to-all-start = ((bf16[16,64,256]{2,1,0:T(8,128)(2,1)}), bf16[16,64,256]{2,1,0:T(8,128)(2,1)S(1)}, u32[]{:S(2)}, u32[]{:S(2)}) async-start(bf16[16,64,256]{2,1,0:T(8,128)(2,1)} %broadcast_in_dim.2), calls=%async_computation | async-start | bytes 1048576 | tf_op jit(solution)/shard_map/all_to_all | solution.py:483
  14.3 0.3 collective-permute-start.5
  14.6 16.5 %all-to-all-done = bf16[16,64,256]{2,1,0:T(8,128)(2,1)S(1)} async-done(((bf16[16,64,256]{2,1,0:T(8,128)(2,1)}), bf16[16,64,256]{2,1,0:T(8,128)(2,1)S(1)}, u32[]{:S(2)}, u32[]{:S(2)}) %all-to-all-start) | async-done | bytes 524320 | tf_op jit(solution)/shard_map/all_to_all | solution.py:483
  31.1 0.0 collective-permute-done.refs_1_
  31.1 0.0 collective-permute-done.1.refs_2_
  31.1 0.0 collective-permute-done.2.refs_0_
  31.1 0.0 copy-start.2
  31.1 0.5 collective-permute-start.3
  31.6 0.8 collective-permute-start.6
  32.4 0.6 collective-permute-start.7
  33.0 2.3 %collective-permute-start.4 = (bf16[320,1024]{1,0:T(8,128)(2,1)S(1)}, bf16[320,1024]{1,0:T(8,128)(2,1)S(1)}, u32[]{:S(2)}, u32[]{:S(2)}) collective-permute-start(bf16[320,1024]{1,0:T(8,128)(2,1)S(1)} %collective-permute-done.2.refs_0_), channel_id=1, source_target_pairs={{0,16},{8,56},{16,32},{24,8},{32,48},{40,24},{48,0},{56,40},{64,80... | collective-permute-start | bytes 1966088 | tf_op jit(solution)/shard_map/ppermute | solution.py:485
  35.9 15.9 %attention_forward.1 = (bf16[8,1536,512]{2,1,0:T(8,128)(2,1)}, bf16[1024,512]{1,0:T(8,128)(2,1)}, bf16[512,1024]{1,0:T(8,128)(2,1)}, bf16[64,1024]{1,0:T(8,128)(...) custom-call(s32[1]{0:T(128)} %bitcast.9.index_ref, s32[1]{0:T(128)S(6)} %copy.30.length_ref, bf16[512,1024]{1,0:T(8,128)(2,1)} %query_ref.3, ...), custom_call_target="tpu_custom_call" | custom-call | flops 3221225472 | bytes 18874368 | tf_op jit(solution)/shard_map/attention_forward/pallas_call | solution.py:137
  51.8 0.0 collective-permute-done.5.refs_4_
  51.8 0.0 collective-permute-done.3.refs_3_
  51.9 0.0 collective-permute-done.7.refs_6_
  51.9 0.0 collective-permute-done.4.refs_1_
  51.9 0.0 copy-start.3
  51.9 0.1 collective-permute-start.8
  52.1 0.6 collective-permute-start.10
  52.7 1.0 collective-permute-start.9
  53.6 0.6 pad_add_fusion.order_ref
  54.2 2.1 %collective-permute-start.11 = (bf16[320,1024]{1,0:T(8,128)(2,1)S(1)}, bf16[320,1024]{1,0:T(8,128)(2,1)S(1)}, u32[]{:S(2)}, u32[]{:S(2)}) collective-permute-start(bf16[320,1024]{1,0:T(8,128)(2,1)S(1)} %collective-permute-done.2.refs_0_), channel_id=1, source_target_pairs={{0,8},{8,0},{16,24},{24,16},{32,40},{40,32},{48,56},{56,48},{64,72... | collective-permute-start | bytes 1966088 | tf_op jit(solution)/shard_map/ppermute | solution.py:485
  56.3 0.0 collective-permute-start.12
  56.3 8.6 %upstream.2.refs_10_ = f32[576,1024]{1,0:T(8,128)} custom-call(s32[4]{0:T(128)} %pad_add_fusion.order_ref, s32[1]{0:T(128)} %bitcast.4.core_ref, s32[1]{0:T(128)} %bitcast.10.half_ref, s32[1]{0:T(128)S(6)} %copy.30.length_ref, bf16[320,1024]{1,0:T(8,128)(2,1)} %bitcast.27, bf16[320,1024]{1,0:T(8,128)(2,1)} %copy-done.8, bf16[320,1024]{1,0:T(8,128)(2,1)} %copy-done.9, ...), custom_call_target="tpu_custom_call" | custom-call | flops 3019898880 | bytes 9437184 | tf_op jit(solution)/shard_map/upstream/pallas_call | solution.py:433
  64.9 9.3 %head_products.2 = (bf16[4,288,640]{2,1,0:T(8,128)(2,1)}, bf16[4,288,640]{2,1,0:T(8,128)(2,1)}, bf16[2,288,640]{2,1,0:T(8,128)(2,1)}, bf16[2,288,640]{2,1,0:T(8,...) custom-call(s32[4]{0:T(128)} %pad_add_fusion.order_ref, s32[1]{0:T(128)} %bitcast.4.core_ref, ...), custom_call_target="tpu_custom_call" | custom-call | flops 3019898880 | bytes 9437184 | tf_op jit(solution)/shard_map/head_products/pallas_call | solution.py:371
  74.3 0.0 collective-permute-done.10.refs_3_
  74.3 0.0 collective-permute-done.9.refs_2_
  74.3 0.6 collective-permute-start.13
  74.9 0.1 collective-permute-start.14
  75.0 0.0 collective-permute-done.11.refs_4_
  75.0 0.0 collective-permute-done.12.refs_5_
  75.0 1.8 %collective-permute-done.13.refs_6_ = bf16[320,1024]{1,0:T(8,128)(2,1)} collective-permute-done((bf16[320,1024]{1,0:T(8,128)(2,1)S(1)}, bf16[320,1024]{1,0:T(8,128)(2,1)}, u32[]{:S(2)}, u32[]{:S(2)}) %collective-permute-start.13) | collective-permute-done | bytes 655392 | tf_op jit(solution)/shard_map/ppermute | solution.py:485
  76.7 0.9 collective-permute-done.14.refs_7_
  77.7 9.2 %head_products.3 = (bf16[4,288,640]{2,1,0:T(8,128)(2,1)}, bf16[4,288,640]{2,1,0:T(8,128)(2,1)}, bf16[2,288,640]{2,1,0:T(8,128)(2,1)}, bf16[2,288,640]{2,1,0:T(8,...) custom-call(s32[4]{0:T(128)} %pad_add_fusion.order_ref, ...), custom_call_target="tpu_custom_call", output_to_operand_aliasing={{0}: (14, {}), {1}: (15, {}), {2}: (16, {}), {3}: (17, {}),... | custom-call | flops 3019898880 | bytes 9437184 | tf_op jit(solution)/shard_map/head_products/pallas_call | solution.py:371
  86.9 1.3 collective-permute-start.15
  88.2 1.3 collective-permute-start.16
  89.5 2.6 %collective-permute-start.17 = (bf16[2,288,640]{2,1,0:T(8,128)(2,1)}, bf16[2,288,640]{2,1,0:T(8,128)(2,1)}, u32[]{:S(2)}, u32[]{:S(2)}) collective-permute-start(bf16[2,288,640]{2,1,0:T(8,128)(2,1)} %get-tuple-element.91), channel_id=1, source_target_pairs={{0,4},{1,5},{2,6},{3,7},{4,0},{5,1},{6,2},{7,3},{8,12},{9,13},{10,... | collective-permute-start | bytes 2211848 | tf_op jit(solution)/shard_map/ppermute | solution.py:504
  92.1 1.0 collective-permute-start.18
  93.2 9.1 %upstream.3 = (bf16[64,1024]{1,0:T(8,128)(2,1)}, bf16[512,1024]{1,0:T(8,128)(2,1)}) custom-call(s32[4]{0:T(128)} %pad_add_fusion.order_ref, s32[1]{0:T(128)} %bitcast.4.core_ref, s32[1]{0:T(128)} %bitcast.6.half_ref, s32[1]{0:T(128)S(6)} %copy.30.length_ref, bf16[320,1024]{1,0:T(8,128)(2,1)} %copy-done.2, bf16[320,1024]{1,0:T(8,128)(2,1)} %copy-done.3, ...), custom_call_target="tpu_custom_call" | custom-call | flops 3019898880 | bytes 9437184 | tf_op jit(solution)/shard_map/upstream/pallas_call | solution.py:433
  102.3 19.5 %attention_backward.1 = (bf16[512,1024]{1,0:T(8,128)(2,1)}, bf16[64,1024]{1,0:T(8,128)(2,1)}, bf16[1024,256]{1,0:T(8,128)(2,1)}, bf16[512,128]{1,0:T(8,128)(2,1)}, bf16[512,128]{1,0:T(8,128)(2,1)}) custom-call(bf16[8,1536,512]{2,1,0:T(8,128)(2,1)} %get-tuple-element.93.weight_ref, bf16[1024,512]{1,0:T(8,128)(2,1)} %get-tuple-element.94.prompt_weight_ref, ...), custom_call_target="tpu_custom_call" | custom-call | flops 6442450944 | bytes 18874368 | tf_op jit(solution)/shard_map/attention_backward/pallas_call | solution.py:256
  121.8 2.3 %collective-permute-done.17 = bf16[2,288,640]{2,1,0:T(8,128)(2,1)} collective-permute-done((bf16[2,288,640]{2,1,0:T(8,128)(2,1)}, bf16[2,288,640]{2,1,0:T(8,128)(2,1)}, u32[]{:S(2)}, u32[]{:S(2)}) %collective-permute-start.17) | collective-permute-done | bytes 737312 | tf_op jit(solution)/shard_map/ppermute | solution.py:504
  124.1 1.7 %add_convert_fusion = bf16[2,288,640]{2,1,0:T(8,128)(2,1)S(1)} fusion(bf16[2,288,640]{2,1,0:T(8,128)(2,1)} %collective-permute-done.18, bf16[2,288,640]{2,1,0:T(8,128)(2,1)} %collective-permute-done.17, bf16[2,288,640]{2,1,0:T(8,128)(2,1)S(1)} %collective-permute-done.16, bf16[2,288,640]{2,1,0:T(8,128)(2,1)S(1)} %copy-done.1), kind=kLoop, calls=%fused_computation | loop fusion | flops 2949120 | bytes 3686400 | tf_op jit(solution)/shard_map/convert_element_type | solution.py:511
  125.9 0.1 slice_bitcast_fusion
  125.9 1.3 copy-done
  127.2 1.2 fusion.3
  128.4 1.1 collective-permute-start.19
  129.5 2.9 %collective-permute-start.20 = (bf16[288,640]{1,0:T(8,128)(2,1)}, bf16[288,640]{1,0:T(8,128)(2,1)S(1)}, u32[]{:S(2)}, u32[]{:S(2)}) collective-permute-start(bf16[288,640]{1,0:T(8,128)(2,1)} %get-tuple-element.103), channel_id=1, source_target_pairs={{0,4},{1,5},{2,6},{3,7},{4,0},{5,1},{6,2},{7,3},{8,12},{9,13},{10,... | collective-permute-start | bytes 1105928 | tf_op jit(solution)/shard_map/ppermute | solution.py:513
  132.4 0.0 collective-permute-start.21
  132.5 0.3 collective-permute-start.22
  132.8 9.8 %all-to-all-start.1 = ((bf16[16,64,256]{2,1,0:T(8,128)(2,1)}), bf16[16,64,256]{2,1,0:T(8,128)(2,1)S(1)}, u32[]{:S(2)}, u32[]{:S(2)}) async-start(bf16[16,64,256]{2,1,0:T(8,128)(2,1)} %bitcast.17), calls=%async_computation.1 | async-start | bytes 1048576 | tf_op jit(solution)/shard_map/all_to_all | solution.py:517
  142.5 6.2 %collective-permute-done.20 = bf16[288,640]{1,0:T(8,128)(2,1)S(1)} collective-permute-done((bf16[288,640]{1,0:T(8,128)(2,1)}, bf16[288,640]{1,0:T(8,128)(2,1)S(1)}, u32[]{:S(2)}, u32[]{:S(2)}) %collective-permute-start.20) | collective-permute-done | bytes 368672 | tf_op jit(solution)/shard_map/ppermute | solution.py:513
  148.8 0.2 add_convert_fusion.2
  149.0 0.6 slice.62
  149.6 0.1 add_convert_fusion.1
  149.7 0.9 pad_maximum_fusion
  150.6 3.2 %all-to-all-done.1 = bf16[16,64,256]{2,1,0:T(8,128)(2,1)S(1)} async-done(((bf16[16,64,256]{2,1,0:T(8,128)(2,1)}), bf16[16,64,256]{2,1,0:T(8,128)(2,1)S(1)}, u32[]{:S(2)}, u32[]{:S(2)}) %all-to-all-start.1) | async-done | bytes 524320 | tf_op jit(solution)/shard_map/all_to_all | solution.py:517
  153.8 0.1 reduce_sum.12
  153.9 0.6 fusion.4
  (27 shorter events, 0.1 us)
Async XLA Ops:
  0.6 13.7 %copy-start.7 = (bf16[1024,320]{0,1:T(8,128)(2,1)S(1)}, bf16[1024,320]{0,1:T(8,128)(2,1)}, u32[]{:S(2)}) copy-start(bf16[1024,320]{0,1:T(8,128)(2,1)} %param.17) | copy-start | bytes 1966084
  0.6 30.4 %collective-permute-start = (bf16[320,1024]{1,0:T(8,128)(2,1)}, bf16[320,1024]{1,0:T(8,128)(2,1)S(1)}, u32[]{:S(2)}, u32[]{:S(2)}) collective-permute-start(bf16[320,1024]{1,0:T(8,128)(2,1)} %bitcast.24), channel_id=1, source_target_pairs={{0,16},{8,56},{16,32},{24,8},{32,48},{40,24},{48,0},{56,40},{64,80... | collective-permute-start | bytes 1966088 | tf_op jit(solution)/shard_map/ppermute | solution.py:485
  5.3 25.8 %collective-permute-start.1 = (bf16[320,1024]{1,0:T(8,128)(2,1)}, bf16[320,1024]{1,0:T(8,128)(2,1)S(1)}, u32[]{:S(2)}, u32[]{:S(2)}) collective-permute-start(bf16[320,1024]{1,0:T(8,128)(2,1)} %bitcast.25), channel_id=1, source_target_pairs={{0,48},{8,24},{16,0},{24,40},{32,16},{40,56},{48,32},{56,8},{64,11... | collective-permute-start | bytes 1966088 | tf_op jit(solution)/shard_map/ppermute | solution.py:485
  5.3 25.8 %collective-permute-start.2 = (bf16[320,1024]{1,0:T(8,128)(2,1)}, bf16[320,1024]{1,0:T(8,128)(2,1)S(1)}, u32[]{:S(2)}, u32[]{:S(2)}) collective-permute-start(bf16[320,1024]{1,0:T(8,128)(2,1)} %bitcast.26), channel_id=1, source_target_pairs={{0,64},{8,72},{16,80},{24,88},{32,96},{40,104},{48,112},{56,120},{... | collective-permute-start | bytes 1966088 | tf_op jit(solution)/shard_map/ppermute | solution.py:485
  9.6 21.4 %all-to-all-start = ((bf16[16,64,256]{2,1,0:T(8,128)(2,1)}), bf16[16,64,256]{2,1,0:T(8,128)(2,1)S(1)}, u32[]{:S(2)}, u32[]{:S(2)}) async-start(bf16[16,64,256]{2,1,0:T(8,128)(2,1)} %broadcast_in_dim.2), calls=%async_computation | async-start | bytes 1048576 | tf_op jit(solution)/shard_map/all_to_all | solution.py:483
  14.3 37.5 %collective-permute-start.5 = (bf16[320,1024]{1,0:T(8,128)(2,1)S(1)}, bf16[320,1024]{1,0:T(8,128)(2,1)}, u32[]{:S(2)}, u32[]{:S(2)}) collective-permute-start(bf16[320,1024]{1,0:T(8,128)(2,1)S(1)} %bitcast.29), channel_id=1, source_target_pairs={{0,8},{8,0},{16,24},{24,16},{32,40},{40,32},{48,56},{56,48},{64,72... | collective-permute-start | bytes 1966088 | tf_op jit(solution)/shard_map/ppermute | solution.py:485
  31.1 1.3 copy-start.10
  31.1 20.7 %copy-start.8 = (bf16[320,1024]{1,0:T(8,128)(2,1)}, bf16[320,1024]{1,0:T(8,128)(2,1)S(1)}, u32[]{:S(2)}) copy-start(bf16[320,1024]{1,0:T(8,128)(2,1)S(1)} %collective-permute-done.refs_1_) | copy-start | bytes 1966084
  31.1 20.7 %copy-start.9 = (bf16[320,1024]{1,0:T(8,128)(2,1)}, bf16[320,1024]{1,0:T(8,128)(2,1)S(1)}, u32[]{:S(2)}) copy-start(bf16[320,1024]{1,0:T(8,128)(2,1)S(1)} %collective-permute-done.1.refs_2_) | copy-start | bytes 1966084
  31.1 23.1 %copy-start.2 = (bf16[320,1024]{1,0:T(8,128)(2,1)}, bf16[320,1024]{1,0:T(8,128)(2,1)S(1)}, u32[]{:S(2)}) copy-start(bf16[320,1024]{1,0:T(8,128)(2,1)S(1)} %collective-permute-done.2.refs_0_) | copy-start | bytes 1966084
  31.1 20.7 %collective-permute-start.3 = (bf16[320,1024]{1,0:T(8,128)(2,1)S(1)}, bf16[320,1024]{1,0:T(8,128)(2,1)}, u32[]{:S(2)}, u32[]{:S(2)}) collective-permute-start(bf16[320,1024]{1,0:T(8,128)(2,1)S(1)} %collective-permute-done.refs_1_), channel_id=1, source_target_pairs={{0,16},{8,56},{16,32},{24,8},{32,48},{40,24},{48,0},{56,40},{64,80... | collective-permute-start | bytes 1966088 | tf_op jit(solution)/shard_map/ppermute | solution.py:485
  31.6 20.3 %collective-permute-start.6 = (bf16[320,1024]{1,0:T(8,128)(2,1)S(1)}, bf16[320,1024]{1,0:T(8,128)(2,1)}, u32[]{:S(2)}, u32[]{:S(2)}) collective-permute-start(bf16[320,1024]{1,0:T(8,128)(2,1)S(1)} %collective-permute-done.refs_1_), channel_id=1, source_target_pairs={{0,8},{8,0},{16,24},{24,16},{32,40},{40,32},{48,56},{56,48},{64,72... | collective-permute-start | bytes 1966088 | tf_op jit(solution)/shard_map/ppermute | solution.py:485
  32.4 19.5 %collective-permute-start.7 = (bf16[320,1024]{1,0:T(8,128)(2,1)S(1)}, bf16[320,1024]{1,0:T(8,128)(2,1)}, u32[]{:S(2)}, u32[]{:S(2)}) collective-permute-start(bf16[320,1024]{1,0:T(8,128)(2,1)S(1)} %collective-permute-done.1.refs_2_), channel_id=1, source_target_pairs={{0,8},{8,0},{16,24},{24,16},{32,40},{40,32},{48,56},{56,48},{64,72... | collective-permute-start | bytes 1966088 | tf_op jit(solution)/shard_map/ppermute | solution.py:485
  33.0 18.9 %collective-permute-start.4 = (bf16[320,1024]{1,0:T(8,128)(2,1)S(1)}, bf16[320,1024]{1,0:T(8,128)(2,1)S(1)}, u32[]{:S(2)}, u32[]{:S(2)}) collective-permute-start(bf16[320,1024]{1,0:T(8,128)(2,1)S(1)} %collective-permute-done.2.refs_0_), channel_id=1, source_target_pairs={{0,16},{8,56},{16,32},{24,8},{32,48},{40,24},{48,0},{56,40},{64,80... | collective-permute-start | bytes 1966088 | tf_op jit(solution)/shard_map/ppermute | solution.py:485
  51.9 13.1 %copy-start.3 = (bf16[320,1024]{1,0:T(8,128)(2,1)}, bf16[320,1024]{1,0:T(8,128)(2,1)S(1)}, u32[]{:S(2)}) copy-start(bf16[320,1024]{1,0:T(8,128)(2,1)S(1)} %collective-permute-done.4.refs_1_) | copy-start | bytes 1966084
  51.9 4.4 %collective-permute-start.8 = (bf16[320,1024]{1,0:T(8,128)(2,1)}, bf16[320,1024]{1,0:T(8,128)(2,1)}, u32[]{:S(2)}, u32[]{:S(2)}) collective-permute-start(bf16[320,1024]{1,0:T(8,128)(2,1)} %collective-permute-done.3.refs_3_), channel_id=1, source_target_pairs={{0,8},{8,0},{16,24},{24,16},{32,40},{40,32},{48,56},{56,48},{64,72... | collective-permute-start | bytes 1966088 | tf_op jit(solution)/shard_map/ppermute | solution.py:485
  52.1 22.2 %collective-permute-start.10 = (bf16[320,1024]{1,0:T(8,128)(2,1)S(1)}, bf16[320,1024]{1,0:T(8,128)(2,1)S(1)}, u32[]{:S(2)}, u32[]{:S(2)}) collective-permute-start(bf16[320,1024]{1,0:T(8,128)(2,1)S(1)} %collective-permute-done.4.refs_1_), channel_id=1, source_target_pairs={{0,16},{8,56},{16,32},{24,8},{32,48},{40,24},{48,0},{56,40},{64,80... | collective-permute-start | bytes 1966088 | tf_op jit(solution)/shard_map/ppermute | solution.py:485
  52.7 21.6 %collective-permute-start.9 = (bf16[320,1024]{1,0:T(8,128)(2,1)S(1)}, bf16[320,1024]{1,0:T(8,128)(2,1)S(1)}, u32[]{:S(2)}, u32[]{:S(2)}) collective-permute-start(bf16[320,1024]{1,0:T(8,128)(2,1)S(1)} %collective-permute-done.2.refs_0_), channel_id=1, source_target_pairs={{0,48},{8,24},{16,0},{24,40},{32,16},{40,56},{48,32},{56,8},{64,11... | collective-permute-start | bytes 1966088 | tf_op jit(solution)/shard_map/ppermute | solution.py:485
  54.2 20.7 %collective-permute-start.11 = (bf16[320,1024]{1,0:T(8,128)(2,1)S(1)}, bf16[320,1024]{1,0:T(8,128)(2,1)S(1)}, u32[]{:S(2)}, u32[]{:S(2)}) collective-permute-start(bf16[320,1024]{1,0:T(8,128)(2,1)S(1)} %collective-permute-done.2.refs_0_), channel_id=1, source_target_pairs={{0,8},{8,0},{16,24},{24,16},{32,40},{40,32},{48,56},{56,48},{64,72... | collective-permute-start | bytes 1966088 | tf_op jit(solution)/shard_map/ppermute | solution.py:485
  56.3 18.7 %collective-permute-start.12 = (bf16[320,1024]{1,0:T(8,128)(2,1)S(1)}, bf16[320,1024]{1,0:T(8,128)(2,1)}, u32[]{:S(2)}, u32[]{:S(2)}) collective-permute-start(bf16[320,1024]{1,0:T(8,128)(2,1)S(1)} %collective-permute-done.4.refs_1_), channel_id=1, source_target_pairs={{0,8},{8,0},{16,24},{24,16},{32,40},{40,32},{48,56},{56,48},{64,72... | collective-permute-start | bytes 1966088 | tf_op jit(solution)/shard_map/ppermute | solution.py:485
  74.3 3.4 %copy-start.4 = (bf16[320,1024]{1,0:T(8,128)(2,1)}, bf16[320,1024]{1,0:T(8,128)(2,1)S(1)}, u32[]{:S(2)}) copy-start(bf16[320,1024]{1,0:T(8,128)(2,1)S(1)} %collective-permute-done.10.refs_3_) | copy-start | bytes 1966084
  74.3 3.4 %copy-start.5 = (bf16[320,1024]{1,0:T(8,128)(2,1)}, bf16[320,1024]{1,0:T(8,128)(2,1)S(1)}, u32[]{:S(2)}) copy-start(bf16[320,1024]{1,0:T(8,128)(2,1)S(1)} %collective-permute-done.9.refs_2_) | copy-start | bytes 1966084
  74.3 2.4 %collective-permute-start.13 = (bf16[320,1024]{1,0:T(8,128)(2,1)S(1)}, bf16[320,1024]{1,0:T(8,128)(2,1)}, u32[]{:S(2)}, u32[]{:S(2)}) collective-permute-start(bf16[320,1024]{1,0:T(8,128)(2,1)S(1)} %collective-permute-done.9.refs_2_), channel_id=1, source_target_pairs={{0,8},{8,0},{16,24},{24,16},{32,40},{40,32},{48,56},{56,48},{64,72... | collective-permute-start | bytes 1966088 | tf_op jit(solution)/shard_map/ppermute | solution.py:485
  74.9 2.8 %collective-permute-start.14 = (bf16[320,1024]{1,0:T(8,128)(2,1)S(1)}, bf16[320,1024]{1,0:T(8,128)(2,1)}, u32[]{:S(2)}, u32[]{:S(2)}) collective-permute-start(bf16[320,1024]{1,0:T(8,128)(2,1)S(1)} %collective-permute-done.10.refs_3_), channel_id=1, source_target_pairs={{0,8},{8,0},{16,24},{24,16},{32,40},{40,32},{48,56},{56,48},{64,72... | collective-permute-start | bytes 1966088 | tf_op jit(solution)/shard_map/ppermute | solution.py:485
  75.0 2.7 %copy-start.6 = (bf16[320,1024]{1,0:T(8,128)(2,1)}, bf16[320,1024]{1,0:T(8,128)(2,1)S(1)}, u32[]{:S(2)}) copy-start(bf16[320,1024]{1,0:T(8,128)(2,1)S(1)} %collective-permute-done.11.refs_4_) | copy-start | bytes 1966084
  86.9 39.0 %collective-permute-start.15 = (bf16[4,288,640]{2,1,0:T(8,128)(2,1)}, bf16[4,288,640]{2,1,0:T(8,128)(2,1)S(1)}, u32[]{:S(2)}, u32[]{:S(2)}) collective-permute-start(bf16[4,288,640]{2,1,0:T(8,128)(2,1)} %get-tuple-element.88), channel_id=1, source_target_pairs={{0,1},{1,0},{2,3},{3,2},{4,5},{5,4},{6,7},{7,6},{8,9},{9,8},{10,11... | collective-permute-start | bytes 4423688 | tf_op jit(solution)/shard_map/ppermute | solution.py:503
  88.2 33.6 %collective-permute-start.16 = (bf16[2,288,640]{2,1,0:T(8,128)(2,1)}, bf16[2,288,640]{2,1,0:T(8,128)(2,1)S(1)}, u32[]{:S(2)}, u32[]{:S(2)}) collective-permute-start(bf16[2,288,640]{2,1,0:T(8,128)(2,1)} %get-tuple-element.90), channel_id=1, source_target_pairs={{0,2},{1,3},{2,4},{3,5},{4,6},{5,7},{6,0},{7,1},{8,10},{9,11},{10,... | collective-permute-start | bytes 2211848 | tf_op jit(solution)/shard_map/ppermute | solution.py:504
  89.5 34.6 %collective-permute-start.17 = (bf16[2,288,640]{2,1,0:T(8,128)(2,1)}, bf16[2,288,640]{2,1,0:T(8,128)(2,1)}, u32[]{:S(2)}, u32[]{:S(2)}) collective-permute-start(bf16[2,288,640]{2,1,0:T(8,128)(2,1)} %get-tuple-element.91), channel_id=1, source_target_pairs={{0,4},{1,5},{2,6},{3,7},{4,0},{5,1},{6,2},{7,3},{8,12},{9,13},{10,... | collective-permute-start | bytes 2211848 | tf_op jit(solution)/shard_map/ppermute | solution.py:504
  92.1 32.0 %collective-permute-start.18 = (bf16[2,288,640]{2,1,0:T(8,128)(2,1)}, bf16[2,288,640]{2,1,0:T(8,128)(2,1)}, u32[]{:S(2)}, u32[]{:S(2)}) collective-permute-start(bf16[2,288,640]{2,1,0:T(8,128)(2,1)} %get-tuple-element.92), channel_id=1, source_target_pairs={{0,6},{1,7},{2,0},{3,1},{4,2},{5,3},{6,4},{7,5},{8,14},{9,15},{10,... | collective-permute-start | bytes 2211848 | tf_op jit(solution)/shard_map/ppermute | solution.py:504
  102.2 21.9 %copy-start.1 = (bf16[2,288,640]{2,1,0:T(8,128)(2,1)S(1)}, bf16[2,288,640]{2,1,0:T(8,128)(2,1)}, u32[]{:S(2)}) copy-start(bf16[2,288,640]{2,1,0:T(8,128)(2,1)} %get-tuple-element.89) | copy-start | bytes 2211844
  125.8 1.4 copy-start
  128.4 14.1 %collective-permute-start.19 = (bf16[288,640]{1,0:T(8,128)(2,1)}, bf16[288,640]{1,0:T(8,128)(2,1)S(1)}, u32[]{:S(2)}, u32[]{:S(2)}) collective-permute-start(bf16[288,640]{1,0:T(8,128)(2,1)} %get-tuple-element.102), channel_id=1, source_target_pairs={{0,2},{1,3},{2,4},{3,5},{4,6},{5,7},{6,0},{7,1},{8,10},{9,11},{10,... | collective-permute-start | bytes 1105928 | tf_op jit(solution)/shard_map/ppermute | solution.py:513
  129.5 19.2 %collective-permute-start.20 = (bf16[288,640]{1,0:T(8,128)(2,1)}, bf16[288,640]{1,0:T(8,128)(2,1)S(1)}, u32[]{:S(2)}, u32[]{:S(2)}) collective-permute-start(bf16[288,640]{1,0:T(8,128)(2,1)} %get-tuple-element.103), channel_id=1, source_target_pairs={{0,4},{1,5},{2,6},{3,7},{4,0},{5,1},{6,2},{7,3},{8,12},{9,13},{10,... | collective-permute-start | bytes 1105928 | tf_op jit(solution)/shard_map/ppermute | solution.py:513
  132.4 16.3 %collective-permute-start.21 = (bf16[288,640]{1,0:T(8,128)(2,1)S(1)}, bf16[288,640]{1,0:T(8,128)(2,1)S(1)}, u32[]{:S(2)}, u32[]{:S(2)}) collective-permute-start(bf16[288,640]{1,0:T(8,128)(2,1)S(1)} %get-tuple-element.104), channel_id=1, source_target_pairs={{0,6},{1,7},{2,0},{3,1},{4,2},{5,3},{6,4},{7,5},{8,14},{9,15},{10,... | collective-permute-start | bytes 1105928 | tf_op jit(solution)/shard_map/ppermute | solution.py:513
  132.5 17.1 %collective-permute-start.22 = (bf16[288,640]{1,0:T(8,128)(2,1)S(1)}, bf16[288,640]{1,0:T(8,128)(2,1)S(1)}, u32[]{:S(2)}, u32[]{:S(2)}) collective-permute-start(bf16[288,640]{1,0:T(8,128)(2,1)S(1)} %get-tuple-element.106), channel_id=1, source_target_pairs={{0,1},{1,0},{2,3},{3,2},{4,5},{5,4},{6,7},{7,6},{8,9},{9,8},{10,11... | collective-permute-start | bytes 1105928 | tf_op jit(solution)/shard_map/ppermute | solution.py:514
  132.8 21.1 %all-to-all-start.1 = ((bf16[16,64,256]{2,1,0:T(8,128)(2,1)}), bf16[16,64,256]{2,1,0:T(8,128)(2,1)S(1)}, u32[]{:S(2)}, u32[]{:S(2)}) async-start(bf16[16,64,256]{2,1,0:T(8,128)(2,1)} %bitcast.17), calls=%async_computation.1 | async-start | bytes 1048576 | tf_op jit(solution)/shard_map/all_to_all | solution.py:517

commit v4 on v3

--- a/solution.py
+++ b/solution.py
@@ -1,3 +1,5 @@
+import functools
+
 import jax
 import jax.numpy as jnp
 from jax import lax
@@ -299,153 +301,175 @@
     )(weights, prompt_weights, reply_query, reply_up, reply_att, prompt_query, prompt_up, prompt_att, inverse, prompt_inverse, kv, kv, reply_key, reply_value)
 
 
-def half_copies(chunks, order_ref, core_ref, gathered, sems):
-    size = chunks[0].shape[0]
-    core = core_ref[0]
+def absorb_kernel(project, back, resume, order_ref, core_ref, head_ref, half_ref, length_ref, *refs):
+    refs = list(refs)
+    take = lambda count: [refs.pop(0) for _ in range(count)]
+    chunks = take(8)
+    sides = []
+    if project:
+        sides.append(take(2))
+    if back:
+        sides.append(take(2))
+    (earlier,) = take(1) if back and resume else (None,)
+    if project and resume:
+        take(6)
+    outs = take(6) if project else None
+    ups = take(2 if resume else 1) if back else None
+    gathered, sems = take(2)
+    if project:
+        rows, held, row_sems, out_sems = take(4)
+    if back:
+        grads, grad_sems = take(2)
+        total, total_sem = take(2) if resume else (ups[0], None)
+    size, core = chunks[0].shape[0], core_ref[0]
+    width = 2 * size
+
     copies = []
+    if project:
+        prompt_ref, reply_ref = sides[0]
+        count = prompt_ref.shape[0]
+        row_copies = [
+            pltpu.make_async_copy(prompt_ref, rows.at[pl.ds(0, count), :], row_sems.at[0]),
+            pltpu.make_async_copy(reply_ref, rows.at[pl.ds(count, reply_ref.shape[0]), :], row_sems.at[1]),
+        ]
+        copies += row_copies
+    if back:
+        prompt_ref, reply_ref = sides[-1]
+        count = prompt_ref.shape[0]
+        columns = pl.ds(pl.multiple_of(half_ref[0] * (4 * width), 4 * width), 4 * width)
+        grad_copies = [
+            pltpu.make_async_copy(prompt_ref.at[:, columns], grads.at[pl.ds(0, count), :], grad_sems.at[0]),
+            pltpu.make_async_copy(reply_ref.at[:, columns], grads.at[pl.ds(count, reply_ref.shape[0]), :], grad_sems.at[1]),
+        ]
+        if resume:
+            grad_copies.append(pltpu.make_async_copy(earlier, total, total_sem.at[0]))
+        if not project:
+            copies += grad_copies
+    pair_copies = []
     for slot in range(4):
-        for side in range(2):
-            place = order_ref[slot if side == 0 else SWAPPED[slot]]
-            row = place * (2 * size) + (core if side == 0 else 1 - core) * size
-            copies.append(
-                pltpu.make_async_copy(
-                    chunks[side * 4 + slot],
-                    gathered.at[pl.ds(pl.multiple_of(row, size), size), :],
-                    sems.at[place, side],
-                )
-            )
-    return copies
-
-
-def products_kernel(order_ref, core_ref, head_ref, half_ref, *refs):
-    chunks = refs[:8]
-    prompt_ref, reply_ref = refs[8:10]
-    outs, (gathered, rows, held, sems, out_sems) = refs[-11:-5], refs[-5:]
-    size = chunks[0].shape[0]
-    for copy in half_copies(chunks, order_ref, core_ref, gathered, sems):
+        start = order_ref[slot] * width
+        pair = []
+        for side, chunk in enumerate((chunks[slot], chunks[4 + SWAPPED[slot]])):
+            row = pl.multiple_of(start + (core if side == 0 else 1 - core) * size, size)
+            pair.append(pltpu.make_async_copy(chunk, gathered.at[pl.ds(row, size), :], sems.at[slot, side]))
+        pair_copies.append(pair)
+        copies += pair
+    if back and project:
+        copies += grad_copies
+    for copy in copies:
         copy.start()
-    count = prompt_ref.shape[0]
-    half = rows.shape[0] // 2
-    rows[:count, :] = prompt_ref[...]
-    rows[count:, :] = reply_ref[...]
-    across, along = head_ref[0] % 2, head_ref[0] // 2
-
-    def flush(slot, dy, dx):
-        upper = [
-            pltpu.make_async_copy(held.at[slot, pl.ds(0, half), :], outs[side].at[dy], out_sems.at[slot, 0]) for side in range(2)
-        ]
-        lower = [
-            pltpu.make_async_copy(held.at[slot, pl.ds(half, half), :], outs[2 + turn].at[dx], out_sems.at[slot, 1]) for turn in range(4)
-        ]
-        return upper, lower
-
-    for place in range(4):
-        slot = place % 2
-        if place >= 2:
-            upper, lower = flush(slot, 0, 0)
-            upper[0].wait()
-            lower[0].wait()
-        for side in range(2):
-            pltpu.make_async_copy(chunks[side * 4], gathered.at[pl.ds(0, size), :], sems.at[place, side]).wait()
-        block = gathered[2 * size * place : 2 * size * (place + 1), :]
-        held[slot] = dot_nt(rows[...], block).astype(BF)
-        target = half_ref[0] * 4 + place
-        dy, dx = (target // 2 - along + 4) % 4, (target % 2 - across + 2) % 2
-        upper, lower = flush(slot, dy, dx)
-        for side in range(2):
-            pl.when(dx == side)(upper[side].start)
-        for turn in range(4):
-            pl.when(dy == turn)(lower[turn].start)
-    for slot in range(2):
-        upper, lower = flush(slot, 0, 0)
-        upper[0].wait()
-        lower[0].wait()
-
-
-def head_products(order, core, head, half, chunks, prompt_att, reply_att, earlier):
-    total = prompt_att.shape[0] + reply_att.shape[0]
+
+    if project:
+        for copy in row_copies:
+            copy.wait()
+        half = rows.shape[0] // 2
+        across, along = head_ref[0] % 2, head_ref[0] // 2
+
+        def upper(slot, side, dy):
+            return pltpu.make_async_copy(held.at[slot, pl.ds(0, half), :], outs[side].at[dy], out_sems.at[slot, 0])
+
+        def lower(slot, turn, dx):
+            return pltpu.make_async_copy(held.at[slot, pl.ds(half, half), :], outs[2 + turn].at[dx], out_sems.at[slot, 1])
+
+        def settle(slot):
+            upper(slot, 0, 0).wait()
+            lower(slot, 0, 0).wait()
+
+        for slot in range(4):
+            place, buffer = order_ref[slot], slot % 2
+            if slot >= 2:
+                settle(buffer)
+            for copy in pair_copies[slot]:
+                copy.wait()
+            block = gathered[pl.ds(pl.multiple_of(place * width, width), width), :]
+            held[buffer] = dot_nt(rows[...], block).astype(BF)
+            target = half_ref[0] * 4 + place
+            dy, dx = (target // 2 - along + 4) % 4, (target % 2 - across + 2) % 2
+            for side in range(2):
+
+                @pl.when(dx == side)
+                def _():
+                    upper(buffer, side, dy).start()
+
+            for turn in range(4):
+
+                @pl.when(dy == turn)
+                def _():
+                    lower(buffer, turn, dx).start()
+
+    if back:
+        for copy in grad_copies:
+            copy.wait()
+        for slot in range(4):
+            if not project:
+                for copy in pair_copies[slot]:
+                    copy.wait()
+            block = pl.ds(pl.multiple_of(order_ref[slot] * width, width), width)
+            part = dot_nn(grads[:, block], gathered[block, :])
+            if slot == 0 and not resume:
+                total[...] = part
+            else:
+                total[...] += part
+        if resume:
+            count = ups[0].shape[0]
+            ups[0][...] = total[:count, :].astype(BF)
+            live = lax.broadcasted_iota(jnp.int32, ups[1].shape, 0) < length_ref[0]
+            ups[1][...] = jnp.where(live, total[count:, :], 0.0).astype(BF)
+
+    if project:
+        settle(0)
+        settle(1)
+
+
+def absorb(scalars, chunks, att, grads, earlier=None, products=None):
+    resume = earlier is not None or products is not None
+    project, back = att is not None, grads is not None
     size, depth = chunks[0].shape
     width = 2 * size
+    prompt_rows, reply_rows = (att or grads)[0].shape[0], (att or grads)[1].shape[0]
+    total = prompt_rows + reply_rows
     anywhere = pl.BlockSpec(memory_space=pl.ANY)
+    local = pl.BlockSpec(memory_space=pltpu.VMEM)
     scalar = pl.BlockSpec(memory_space=pltpu.SMEM)
-    return pl.pallas_call(
-        products_kernel,
-        in_specs=[scalar] * 4 + [anywhere] * 8 + [pl.BlockSpec(memory_space=pltpu.VMEM)] * 2 + [anywhere] * len(earlier),
-        out_specs=[anywhere] * 6,
-        out_shape=[jax.ShapeDtypeStruct((4, total // 2, width), BF)] * 2 + [jax.ShapeDtypeStruct((2, total // 2, width), BF)] * 4,
-        input_output_aliases={14 + place: place for place in range(len(earlier))},
-        scratch_shapes=[
-            pltpu.VMEM((8 * size, depth), BF),
+    operands = [*chunks, *(att or ()), *(grads or ())]
+    if back and resume:
+        operands.append(earlier)
+    aliases = {}
+    out_specs, out_shape = [], []
+    scratch = [pltpu.VMEM((8 * size, depth), BF), pltpu.SemaphoreType.DMA((4, 2))]
+    if project:
+        if resume:
+            aliases = {len(scalars) + len(operands) + place: place for place in range(6)}
+            operands += products
+        out_specs += [anywhere] * 6
+        out_shape += [jax.ShapeDtypeStruct((4, total // 2, width), BF)] * 2 + [jax.ShapeDtypeStruct((2, total // 2, width), BF)] * 4
+        scratch += [
             pltpu.VMEM((total, depth), BF),
             pltpu.VMEM((2, total, width), BF),
-            pltpu.SemaphoreType.DMA((4, 2)),
+            pltpu.SemaphoreType.DMA((2,)),
             pltpu.SemaphoreType.DMA((2, 2)),
-        ],
-        compiler_params=pltpu.CompilerParams(vmem_limit_bytes=VMEM_LIMIT),
-        cost_estimate=pl.CostEstimate(flops=2 * total * depth * 8 * size, bytes_accessed=9 * 2**20, transcendentals=0),
-        name="head_products",
-    )(order, core, head, half, *chunks, prompt_att, reply_att, *earlier)
-
-
-def upstream_kernel(order_ref, core_ref, half_ref, length_ref, *refs):
-    chunks = refs[:8]
-    prompt_ref, reply_ref = refs[8:10]
-    last = len(refs) == 17
-    earlier, outs, (gathered, rows, sems, row_sems) = (refs[10:11], refs[11:13], refs[13:]) if last else ((), refs[10:11], refs[11:])
-    step = pl.program_id(0)
-    count = prompt_ref.shape[0]
-
-    @pl.when(step == 0)
-    def _():
-        columns = pl.ds(pl.multiple_of(half_ref[0] * rows.shape[1], rows.shape[1]), rows.shape[1])
-        copies = half_copies(chunks, order_ref, core_ref, gathered, sems)
-        copies.append(pltpu.make_async_copy(prompt_ref.at[:, columns], rows.at[pl.ds(0, count), :], row_sems.at[0]))
-        copies.append(pltpu.make_async_copy(reply_ref.at[:, columns], rows.at[pl.ds(count, rows.shape[0] - count), :], row_sems.at[1]))
-        for copy in copies:
-            copy.start()
-        for copy in copies:
-            copy.wait()
-
-    width = outs[0].shape[1]
-    total = dot_nn(rows[...], gathered[:, pl.ds(pl.multiple_of(step * width, width), width)])
-    if not last:
-        outs[0][...] = total
-    else:
-        total = total + earlier[0][...]
-        outs[0][...] = total[:count].astype(BF)
-        live = lax.broadcasted_iota(jnp.int32, (total.shape[0] - count, width), 0) < length_ref[0]
-        outs[1][...] = jnp.where(live, total[count:], 0.0).astype(BF)
-
-
-def upstream(order, core, half, lengths, chunks, prompt_grad, reply_grad, earlier):
-    size, depth = chunks[0].shape
-    prompt_rows, reply_rows = prompt_grad.shape[0], reply_grad.shape[0]
-    total = prompt_rows + reply_rows
-    parts = 2
-    anywhere = pl.BlockSpec(memory_space=pl.ANY)
-    scalar = pl.BlockSpec(memory_space=pltpu.SMEM)
-    column = lambda rows: pl.BlockSpec((rows, depth // parts), lambda k: (0, k))
-    if earlier is None:
-        out_specs, out_shape = [column(total)], [jax.ShapeDtypeStruct((total, depth), F32)]
-    else:
-        out_specs = [column(prompt_rows), column(reply_rows)]
-        out_shape = [jax.ShapeDtypeStruct((prompt_rows, depth), BF), jax.ShapeDtypeStruct((reply_rows, depth), BF)]
+        ]
+    if back:
+        scratch += [pltpu.VMEM((total, 8 * size), BF), pltpu.SemaphoreType.DMA((2,))]
+        if resume:
+            out_specs += [local] * 2
+            out_shape += [jax.ShapeDtypeStruct((prompt_rows, depth), BF), jax.ShapeDtypeStruct((reply_rows, depth), BF)]
+            scratch += [pltpu.VMEM((total, depth), F32), pltpu.SemaphoreType.DMA((1,))]
+        else:
+            out_specs.append(local)
+            out_shape.append(jax.ShapeDtypeStruct((total, depth), F32))
+    count = int(project) + int(back)
     return pl.pallas_call(
-        upstream_kernel,
-        grid=(parts,),
-        in_specs=[scalar] * 4 + [anywhere] * 10 + ([] if earlier is None else [column(total)]),
+        functools.partial(absorb_kernel, project, back, resume),
+        in_specs=[scalar] * len(scalars) + [anywhere] * len(operands),
         out_specs=out_specs,
         out_shape=out_shape,
-        scratch_shapes=[
-            pltpu.VMEM((8 * size, depth), BF),
-            pltpu.VMEM((total, 8 * size), BF),
-            pltpu.SemaphoreType.DMA((4, 2)),
-            pltpu.SemaphoreType.DMA((2,)),
-        ],
+        input_output_aliases=aliases,
+        scratch_shapes=scratch,
         compiler_params=pltpu.CompilerParams(vmem_limit_bytes=VMEM_LIMIT),
-        cost_estimate=pl.CostEstimate(flops=2 * total * depth * 8 * size, bytes_accessed=9 * 2**20, transcendentals=0),
-        name="upstream",
-    )(order, core, half, lengths, *chunks, prompt_grad, reply_grad, *([] if earlier is None else [earlier]))
+        cost_estimate=pl.CostEstimate(flops=2 * total * depth * 8 * size * count, bytes_accessed=9 * 2**20, transcendentals=0),
+        name="absorb_both" if count == 2 else "absorb_products" if project else "absorb_upstream",
+    )(*scalars, *operands)
 
 
 SWAPPED = (0, 2, 1, 3)
@@ -494,15 +518,16 @@
     near_chunks = [mine, along, against, far, *near_twins, send(far, SIBLING)]
     peer_against, peer_far = send(peer, AGAINST), send(peer_along, ALONG)
     peer_twins = [send(chunk, SIBLING) for chunk in (peer, peer_along)]
-    (partial,) = upstream(order, core, near, lengths, near_chunks, prompt_grad, reply_grad, None)
-    products = head_products(order, core, head, near, near_chunks, prompt_att, reply_att, ())
+    att, grads = (prompt_att, reply_att), (prompt_grad, reply_grad)
+    *products, partial = absorb((order, core, head, near, lengths), near_chunks, att, grads)
     partial, products, peer_against, peer_far = lax.optimization_barrier((partial, products, peer_against, peer_far))
     peer_twins = peer_twins + [send(chunk, SIBLING) for chunk in (peer_against, peer_far)]
     far_chunks = [peer, peer_along, peer_against, peer_far, *peer_twins]
-    kept, sent, *turns = head_products(order, core, head, other, far_chunks, prompt_att, reply_att, products)
+    far_scalars = (order, core, head, other, lengths)
+    kept, sent, *turns = absorb(far_scalars, far_chunks, att, None, None, products)
     came = lax.ppermute(sent, "head", head_perm(0, 1))
     turned = [lax.ppermute(turns[dy], "head", head_perm(dy, 0)) for dy in (1, 2, 3)]
-    prompt_up, reply_up = upstream(order, core, other, lengths, far_chunks, prompt_grad, reply_grad, partial)
+    prompt_up, reply_up = absorb(far_scalars, far_chunks, None, grads, partial)
     query_grad, prompt_query_grad, kv_grad, reply_key_grad, reply_value_grad = attention_backward(
         weights, prompt_weights, inverse, prompt_inverse, reply_query, reply_up, reply_att, prompt_query, prompt_up, prompt_att, kv, reply_key, reply_value
     )

time: 155 us -> 150 us (0.968)
  Pallas kernels: 71.6 us -> 69.2 us
  starting transfers between devices: 41.2 us -> 39.1 us
  waiting for transfers between devices: 31 us -> 29.4 us
    all_to_all x1, waiting for transfers between devices: 3.21 us -> 0.01 us  [body(): lax.all_to_all(kv_grad.reshape(n_seq, prompt_rows, 2 * DIM), 'seq', 0, 0)]
    ppermute x3, waiting for transfers between devices: 6.22 us -> 8.76 us  [body(): lax.ppermute(first[dy], 'head', head_perm(dy, 0))]
    all_to_all x1, starting transfers between devices: 9.78 us -> 7.24 us  [body(): lax.all_to_all(kv_grad.reshape(n_seq, prompt_rows, 2 * DIM), 'seq', 0, 0)]
    pallas_call x4 -> x3, Pallas kernels: 36.2 us -> 33.7 us  [absorb(): pl.pallas_call(functools.partial(absorb_kernel, project, back, resume), i...]
  transfers between devices with their start and end apart: 25 -> 25, of which waited for: 6 -> 5; matrix products, arithmetic and copies ran while one was open for 4% -> 5% of each run, Pallas kernels for 40% -> 40%
where the time goes in v4:
time: 150 us; the launch traced here: 149 us
  Pallas kernels  69.2 us (46%)
  starting transfers between devices  39.1 us (26%)
  waiting for transfers between devices  29.4 us (20%)
  other arithmetic  6.48 us (4%)
  local copies, waits for them, and re-layouts  3.52 us (2%)
  between operations  1.54 us (1%)
    pallas_call x3, Pallas kernels, absorb(): pl.pallas_call(functools.partial(absorb_kernel, project, back, resume), i...  33.7 us
    pallas_call x1, Pallas kernels, attention_backward(): pl.pallas_call(backward_kernel, grid=(steps + 1,), in_specs=[pl.BlockSpec...  19.5 us
    ppermute x15, starting transfers between devices, body(): send = lambda chunk, perm: lax.ppermute(chunk, 'seq', perm)  16.5 us
    all_to_all x1, waiting for transfers between devices, body(): lax.all_to_all(jnp.broadcast_to(own[None], (n_seq,) + own.shape), 'seq',...  16.5 us
    pallas_call x1, Pallas kernels, attention_forward(): pl.pallas_call(forward_kernel, grid=(steps + 1,), in_specs=[pl.BlockSpec(...  15.9 us
    ppermute x3, waiting for transfers between devices, body(): lax.ppermute(first[dy], 'head', head_perm(dy, 0))  8.76 us
    all_to_all x1, starting transfers between devices, body(): lax.all_to_all(kv_grad.reshape(n_seq, prompt_rows, 2 * DIM), 'seq', 0, 0)  7.24 us
    ppermute x3, starting transfers between devices, body(): lax.ppermute(turns[dy], 'head', head_perm(dy, 0))  5.08 us
  transfers between devices with their start and end apart: 25, of which 5 were waited for; matrix products, arithmetic and copies ran while one was open for 5% of the time, Pallas kernels for 40%

profile of v4, /device:TPU:1, one launch (start us, length us, event | category | flops | bytes accessed | tf_op | source)
XLA Modules:
  0.0 149.3 jit_solution(4174253184569899056)
XLA Ops:
  0.6 0.0 copy-start.8
  0.6 4.7 %collective-permute-start = (bf16[320,1024]{1,0:T(8,128)(2,1)}, bf16[320,1024]{1,0:T(8,128)(2,1)S(1)}, u32[]{:S(2)}, u32[]{:S(2)}) collective-permute-start(bf16[320,1024]{1,0:T(8,128)(2,1)} %bitcast.28), channel_id=1, source_target_pairs={{0,16},{8,56},{16,32},{24,8},{32,48},{40,24},{48,0},{56,40},{64,80... | collective-permute-start | bytes 1966088 | tf_op jit(solution)/shard_map/ppermute | solution.py:509
  5.3 0.0 collective-permute-start.1
  5.3 2.7 %collective-permute-start.2 = (bf16[320,1024]{1,0:T(8,128)(2,1)}, bf16[320,1024]{1,0:T(8,128)(2,1)S(1)}, u32[]{:S(2)}, u32[]{:S(2)}) collective-permute-start(bf16[320,1024]{1,0:T(8,128)(2,1)} %bitcast.30), channel_id=1, source_target_pairs={{0,64},{8,72},{16,80},{24,88},{32,96},{40,104},{48,112},{56,120},{... | collective-permute-start | bytes 1966088 | tf_op jit(solution)/shard_map/ppermute | solution.py:509
  8.0 0.7 pad_maximum_fusion.1
  8.8 0.8 broadcast_in_dim.2
  9.6 4.7 %all-to-all-start = ((bf16[16,64,256]{2,1,0:T(8,128)(2,1)}), bf16[16,64,256]{2,1,0:T(8,128)(2,1)S(1)}, u32[]{:S(2)}, u32[]{:S(2)}) async-start(bf16[16,64,256]{2,1,0:T(8,128)(2,1)} %broadcast_in_dim.2), calls=%async_computation | async-start | bytes 1048576 | tf_op jit(solution)/shard_map/all_to_all | solution.py:507
  14.3 0.3 collective-permute-start.5
  14.6 16.5 %all-to-all-done = bf16[16,64,256]{2,1,0:T(8,128)(2,1)S(1)} async-done(((bf16[16,64,256]{2,1,0:T(8,128)(2,1)}), bf16[16,64,256]{2,1,0:T(8,128)(2,1)S(1)}, u32[]{:S(2)}, u32[]{:S(2)}) %all-to-all-start) | async-done | bytes 524320 | tf_op jit(solution)/shard_map/all_to_all | solution.py:507
  31.1 0.0 collective-permute-done.refs_1_
  31.1 0.0 collective-permute-done.1.refs_2_
  31.1 0.0 collective-permute-done.2.refs_0_
  31.1 0.0 copy-start.2
  31.1 0.5 collective-permute-start.3
  31.6 0.8 collective-permute-start.6
  32.4 2.9 %collective-permute-start.4 = (bf16[320,1024]{1,0:T(8,128)(2,1)S(1)}, bf16[320,1024]{1,0:T(8,128)(2,1)S(1)}, u32[]{:S(2)}, u32[]{:S(2)}) collective-permute-start(bf16[320,1024]{1,0:T(8,128)(2,1)S(1)} %collective-permute-done.2.refs_0_), channel_id=1, source_target_pairs={{0,16},{8,56},{16,32},{24,8},{32,48},{40,24},{48,0},{56,40},{64,80... | collective-permute-start | bytes 1966088 | tf_op jit(solution)/shard_map/ppermute | solution.py:509
  35.2 0.0 collective-permute-start.7
  35.9 15.9 %attention_forward.1 = (bf16[8,1536,512]{2,1,0:T(8,128)(2,1)}, bf16[1024,512]{1,0:T(8,128)(2,1)}, bf16[512,1024]{1,0:T(8,128)(2,1)}, bf16[64,1024]{1,0:T(8,128)(...) custom-call(s32[1]{0:T(128)} %bitcast.9.index_ref, s32[1]{0:T(128)S(6)} %copy.30.length_ref, bf16[512,1024]{1,0:T(8,128)(2,1)} %query_ref.3, ...), custom_call_target="tpu_custom_call" | custom-call | flops 3221225472 | bytes 18874368 | tf_op jit(solution)/shard_map/attention_forward/pallas_call | solution.py:139
  51.8 0.0 collective-permute-done.5.refs_4_
  51.8 0.0 collective-permute-done.3.refs_3_
  51.8 0.0 collective-permute-done.6.refs_5_
  51.9 0.0 collective-permute-done.4.refs_1_
  51.9 0.0 copy-start.3
  51.9 0.6 collective-permute-start.8
  52.5 0.0 collective-permute-start.10
  52.5 1.4 collective-permute-start.9
  53.9 0.6 pad_add_fusion.order_ref
  54.5 2.0 %collective-permute-start.11 = (bf16[320,1024]{1,0:T(8,128)(2,1)S(1)}, bf16[320,1024]{1,0:T(8,128)(2,1)S(1)}, u32[]{:S(2)}, u32[]{:S(2)}) collective-permute-start(bf16[320,1024]{1,0:T(8,128)(2,1)S(1)} %collective-permute-done.2.refs_0_), channel_id=1, source_target_pairs={{0,8},{8,0},{16,24},{24,16},{32,40},{40,32},{48,56},{56,48},{64,72... | collective-permute-start | bytes 1966088 | tf_op jit(solution)/shard_map/ppermute | solution.py:509
  56.5 0.0 collective-permute-start.12
  56.5 0.0 collective-permute-done.8.refs_7_
  56.5 14.5 %absorb_both.1 = (bf16[4,288,640]{2,1,0:T(8,128)(2,1)}, bf16[4,288,640]{2,1,0:T(8,128)(2,1)}, bf16[2,288,640]{2,1,0:T(8,128)(2,1)}, bf16[2,288,640]{2,1,0:T(8,12...) custom-call(s32[4]{0:T(128)} %pad_add_fusion.order_ref, ...), custom_call_target="tpu_custom_call" | custom-call | flops 6039797760 | bytes 9437184 | tf_op jit(solution)/shard_map/absorb_both/pallas_call | solution.py:462
  71.0 0.0 collective-permute-done.10.refs_3_
  71.0 0.0 collective-permute-done.9.refs_2_
  71.0 0.6 collective-permute-start.13
  71.6 0.1 collective-permute-start.14
  71.7 1.8 %collective-permute-done.13.refs_6_ = bf16[320,1024]{1,0:T(8,128)(2,1)} collective-permute-done((bf16[320,1024]{1,0:T(8,128)(2,1)S(1)}, bf16[320,1024]{1,0:T(8,128)(2,1)}, u32[]{:S(2)}, u32[]{:S(2)}) %collective-permute-start.13) | collective-permute-done | bytes 655392 | tf_op jit(solution)/shard_map/ppermute | solution.py:509
  73.5 0.9 collective-permute-done.14.refs_7_
  74.4 9.4 %absorb_products.1 = (bf16[4,288,640]{2,1,0:T(8,128)(2,1)}, bf16[4,288,640]{2,1,0:T(8,128)(2,1)}, bf16[2,288,640]{2,1,0:T(8,128)(2,1)}, bf16[2,288,640]{2,1,0:T(...) custom-call(s32[4]{0:T(128)} %pad_add_fusion.order_ref, ...), custom_call_target="tpu_custom_call", output_to_operand_aliasing={{0}: (15, {}), {1}: (16, {}), {2}: (17, {}), {3}: (18, {}),... | custom-call | flops 3019898880 | bytes 9437184 | tf_op jit(solution)/shard_map/absorb_products/pallas_call | solution.py:462
  83.8 1.3 collective-permute-start.15
  85.1 1.4 collective-permute-start.16
  86.5 2.6 %collective-permute-start.17 = (bf16[2,288,640]{2,1,0:T(8,128)(2,1)}, bf16[2,288,640]{2,1,0:T(8,128)(2,1)}, u32[]{:S(2)}, u32[]{:S(2)}) collective-permute-start(bf16[2,288,640]{2,1,0:T(8,128)(2,1)} %get-tuple-element.93), channel_id=1, source_target_pairs={{0,4},{1,5},{2,6},{3,7},{4,0},{5,1},{6,2},{7,3},{8,12},{9,13},{10,... | collective-permute-start | bytes 2211848 | tf_op jit(solution)/shard_map/ppermute | solution.py:529
  89.1 1.1 collective-permute-start.18
  90.2 9.9 %absorb_upstream.1 = (bf16[64,1024]{1,0:T(8,128)(2,1)}, bf16[512,1024]{1,0:T(8,128)(2,1)}) custom-call(s32[4]{0:T(128)} %pad_add_fusion.order_ref, s32[1]{0:T(128)} %bitcast.4.core_ref, s32[1]{0:T(128)} %bitcast.5.head_ref, s32[1]{0:T(128)} %bitcast.6.half_ref, s32[1]{0:T(128)S(6)} %copy.30.length_ref, bf16[320,1024]{1,0:T(8,128)(2,1)} %copy-done.2, ...), custom_call_target="tpu_custom_call" | custom-call | flops 3019898880 | bytes 9437184 | tf_op jit(solution)/shard_map/absorb_upstream/pallas_call | solution.py:462
  100.1 19.5 %attention_backward.1 = (bf16[512,1024]{1,0:T(8,128)(2,1)}, bf16[64,1024]{1,0:T(8,128)(2,1)}, bf16[1024,256]{1,0:T(8,128)(2,1)}, bf16[512,128]{1,0:T(8,128)(2,1)}, bf16[512,128]{1,0:T(8,128)(2,1)}) custom-call(bf16[8,1536,512]{2,1,0:T(8,128)(2,1)} %get-tuple-element.95.weight_ref, bf16[1024,512]{1,0:T(8,128)(2,1)} %get-tuple-element.96.prompt_weight_ref, ...), custom_call_target="tpu_custom_call" | custom-call | flops 6442450944 | bytes 18874368 | tf_op jit(solution)/shard_map/attention_backward/pallas_call | solution.py:258
  119.6 0.0 collective-permute-done.16
  119.6 1.5 collective-permute-done.17
  121.1 1.7 %add_convert_fusion = bf16[2,288,640]{2,1,0:T(8,128)(2,1)S(1)} fusion(bf16[2,288,640]{2,1,0:T(8,128)(2,1)} %collective-permute-done.18, bf16[2,288,640]{2,1,0:T(8,128)(2,1)} %collective-permute-done.17, bf16[2,288,640]{2,1,0:T(8,128)(2,1)S(1)} %collective-permute-done.16, bf16[2,288,640]{2,1,0:T(8,128)(2,1)S(1)} %copy-done.1), kind=kLoop, calls=%fused_computation | loop fusion | flops 2949120 | bytes 3686400 | tf_op jit(solution)/shard_map/convert_element_type | solution.py:536
  122.8 0.1 slice_bitcast_fusion
  122.9 1.3 copy-done
  124.2 1.2 fusion.3
  125.4 1.0 collective-permute-start.19
  126.4 3.0 %collective-permute-start.20 = (bf16[288,640]{1,0:T(8,128)(2,1)}, bf16[288,640]{1,0:T(8,128)(2,1)S(1)}, u32[]{:S(2)}, u32[]{:S(2)}) collective-permute-start(bf16[288,640]{1,0:T(8,128)(2,1)} %get-tuple-element.105), channel_id=1, source_target_pairs={{0,4},{1,5},{2,6},{3,7},{4,0},{5,1},{6,2},{7,3},{8,12},{9,13},{10,... | collective-permute-start | bytes 1105928 | tf_op jit(solution)/shard_map/ppermute | solution.py:538
  129.4 0.1 collective-permute-start.21
  129.5 0.2 collective-permute-start.22
  129.7 7.2 %all-to-all-start.1 = ((bf16[16,64,256]{2,1,0:T(8,128)(2,1)}), bf16[16,64,256]{2,1,0:T(8,128)(2,1)S(1)}, u32[]{:S(2)}, u32[]{:S(2)}) async-start(bf16[16,64,256]{2,1,0:T(8,128)(2,1)} %bitcast.17), calls=%async_computation.1 | async-start | bytes 1048576 | tf_op jit(solution)/shard_map/all_to_all | solution.py:542
  137.0 8.8 %collective-permute-done.20 = bf16[288,640]{1,0:T(8,128)(2,1)S(1)} collective-permute-done((bf16[288,640]{1,0:T(8,128)(2,1)}, bf16[288,640]{1,0:T(8,128)(2,1)S(1)}, u32[]{:S(2)}, u32[]{:S(2)}) %collective-permute-start.20) | collective-permute-done | bytes 368672 | tf_op jit(solution)/shard_map/ppermute | solution.py:538
  145.7 0.0 collective-permute-done.21
  145.7 0.2 add_convert_fusion.2
  145.9 0.6 slice.62
  146.6 1.1 add_convert_fusion.1
  147.7 0.9 pad_maximum_fusion
  148.6 0.0 all-to-all-done.1
  148.6 0.1 reduce_sum.12
  148.6 0.6 fusion.4
  (24 shorter events, 0.1 us)
Async XLA Ops:
  0.6 13.7 %copy-start.8 = (bf16[1024,320]{0,1:T(8,128)(2,1)S(1)}, bf16[1024,320]{0,1:T(8,128)(2,1)}, u32[]{:S(2)}) copy-start(bf16[1024,320]{0,1:T(8,128)(2,1)} %param.17) | copy-start | bytes 1966084
  0.6 30.4 %collective-permute-start = (bf16[320,1024]{1,0:T(8,128)(2,1)}, bf16[320,1024]{1,0:T(8,128)(2,1)S(1)}, u32[]{:S(2)}, u32[]{:S(2)}) collective-permute-start(bf16[320,1024]{1,0:T(8,128)(2,1)} %bitcast.28), channel_id=1, source_target_pairs={{0,16},{8,56},{16,32},{24,8},{32,48},{40,24},{48,0},{56,40},{64,80... | collective-permute-start | bytes 1966088 | tf_op jit(solution)/shard_map/ppermute | solution.py:509
  5.3 25.8 %collective-permute-start.1 = (bf16[320,1024]{1,0:T(8,128)(2,1)}, bf16[320,1024]{1,0:T(8,128)(2,1)}, u32[]{:S(2)}, u32[]{:S(2)}) collective-permute-start(bf16[320,1024]{1,0:T(8,128)(2,1)} %bitcast.29), channel_id=1, source_target_pairs={{0,48},{8,24},{16,0},{24,40},{32,16},{40,56},{48,32},{56,8},{64,11... | collective-permute-start | bytes 1966088 | tf_op jit(solution)/shard_map/ppermute | solution.py:509
  5.3 25.8 %collective-permute-start.2 = (bf16[320,1024]{1,0:T(8,128)(2,1)}, bf16[320,1024]{1,0:T(8,128)(2,1)S(1)}, u32[]{:S(2)}, u32[]{:S(2)}) collective-permute-start(bf16[320,1024]{1,0:T(8,128)(2,1)} %bitcast.30), channel_id=1, source_target_pairs={{0,64},{8,72},{16,80},{24,88},{32,96},{40,104},{48,112},{56,120},{... | collective-permute-start | bytes 1966088 | tf_op jit(solution)/shard_map/ppermute | solution.py:509
  9.6 21.4 %all-to-all-start = ((bf16[16,64,256]{2,1,0:T(8,128)(2,1)}), bf16[16,64,256]{2,1,0:T(8,128)(2,1)S(1)}, u32[]{:S(2)}, u32[]{:S(2)}) async-start(bf16[16,64,256]{2,1,0:T(8,128)(2,1)} %broadcast_in_dim.2), calls=%async_computation | async-start | bytes 1048576 | tf_op jit(solution)/shard_map/all_to_all | solution.py:507
  14.3 37.5 %collective-permute-start.5 = (bf16[320,1024]{1,0:T(8,128)(2,1)S(1)}, bf16[320,1024]{1,0:T(8,128)(2,1)}, u32[]{:S(2)}, u32[]{:S(2)}) collective-permute-start(bf16[320,1024]{1,0:T(8,128)(2,1)S(1)} %bitcast.32), channel_id=1, source_target_pairs={{0,8},{8,0},{16,24},{24,16},{32,40},{40,32},{48,56},{56,48},{64,72... | collective-permute-start | bytes 1966088 | tf_op jit(solution)/shard_map/ppermute | solution.py:509
  31.1 4.8 %copy-start.7 = (bf16[16,64,256]{2,1,0:T(8,128)(2,1)}, bf16[16,64,256]{2,1,0:T(8,128)(2,1)S(1)}, u32[]{:S(2)}) copy-start(bf16[16,64,256]{2,1,0:T(8,128)(2,1)S(1)} %all-to-all-done) | copy-start | bytes 1572868
  31.1 20.7 %copy-start.9 = (bf16[320,1024]{1,0:T(8,128)(2,1)}, bf16[320,1024]{1,0:T(8,128)(2,1)S(1)}, u32[]{:S(2)}) copy-start(bf16[320,1024]{1,0:T(8,128)(2,1)S(1)} %collective-permute-done.refs_1_) | copy-start | bytes 1966084
  31.1 23.4 %copy-start.2 = (bf16[320,1024]{1,0:T(8,128)(2,1)}, bf16[320,1024]{1,0:T(8,128)(2,1)S(1)}, u32[]{:S(2)}) copy-start(bf16[320,1024]{1,0:T(8,128)(2,1)S(1)} %collective-permute-done.2.refs_0_) | copy-start | bytes 1966084
  31.1 20.7 %collective-permute-start.3 = (bf16[320,1024]{1,0:T(8,128)(2,1)S(1)}, bf16[320,1024]{1,0:T(8,128)(2,1)}, u32[]{:S(2)}, u32[]{:S(2)}) collective-permute-start(bf16[320,1024]{1,0:T(8,128)(2,1)S(1)} %collective-permute-done.refs_1_), channel_id=1, source_target_pairs={{0,16},{8,56},{16,32},{24,8},{32,48},{40,24},{48,0},{56,40},{64,80... | collective-permute-start | bytes 1966088 | tf_op jit(solution)/shard_map/ppermute | solution.py:509
  31.6 20.3 %collective-permute-start.6 = (bf16[320,1024]{1,0:T(8,128)(2,1)S(1)}, bf16[320,1024]{1,0:T(8,128)(2,1)}, u32[]{:S(2)}, u32[]{:S(2)}) collective-permute-start(bf16[320,1024]{1,0:T(8,128)(2,1)S(1)} %collective-permute-done.refs_1_), channel_id=1, source_target_pairs={{0,8},{8,0},{16,24},{24,16},{32,40},{40,32},{48,56},{56,48},{64,72... | collective-permute-start | bytes 1966088 | tf_op jit(solution)/shard_map/ppermute | solution.py:509
  32.4 19.5 %collective-permute-start.4 = (bf16[320,1024]{1,0:T(8,128)(2,1)S(1)}, bf16[320,1024]{1,0:T(8,128)(2,1)S(1)}, u32[]{:S(2)}, u32[]{:S(2)}) collective-permute-start(bf16[320,1024]{1,0:T(8,128)(2,1)S(1)} %collective-permute-done.2.refs_0_), channel_id=1, source_target_pairs={{0,16},{8,56},{16,32},{24,8},{32,48},{40,24},{48,0},{56,40},{64,80... | collective-permute-start | bytes 1966088 | tf_op jit(solution)/shard_map/ppermute | solution.py:509
  35.2 16.6 %collective-permute-start.7 = (bf16[320,1024]{1,0:T(8,128)(2,1)}, bf16[320,1024]{1,0:T(8,128)(2,1)}, u32[]{:S(2)}, u32[]{:S(2)}) collective-permute-start(bf16[320,1024]{1,0:T(8,128)(2,1)} %collective-permute-done.1.refs_2_), channel_id=1, source_target_pairs={{0,8},{8,0},{16,24},{24,16},{32,40},{40,32},{48,56},{56,48},{64,72... | collective-permute-start | bytes 1966088 | tf_op jit(solution)/shard_map/ppermute | solution.py:509
  51.9 19.1 %copy-start.3 = (bf16[320,1024]{1,0:T(8,128)(2,1)}, bf16[320,1024]{1,0:T(8,128)(2,1)S(1)}, u32[]{:S(2)}) copy-start(bf16[320,1024]{1,0:T(8,128)(2,1)S(1)} %collective-permute-done.4.refs_1_) | copy-start | bytes 1966084
  51.9 4.6 %collective-permute-start.8 = (bf16[320,1024]{1,0:T(8,128)(2,1)}, bf16[320,1024]{1,0:T(8,128)(2,1)}, u32[]{:S(2)}, u32[]{:S(2)}) collective-permute-start(bf16[320,1024]{1,0:T(8,128)(2,1)} %collective-permute-done.3.refs_3_), channel_id=1, source_target_pairs={{0,8},{8,0},{16,24},{24,16},{32,40},{40,32},{48,56},{56,48},{64,72... | collective-permute-start | bytes 1966088 | tf_op jit(solution)/shard_map/ppermute | solution.py:509
  52.5 18.5 %collective-permute-start.10 = (bf16[320,1024]{1,0:T(8,128)(2,1)S(1)}, bf16[320,1024]{1,0:T(8,128)(2,1)S(1)}, u32[]{:S(2)}, u32[]{:S(2)}) collective-permute-start(bf16[320,1024]{1,0:T(8,128)(2,1)S(1)} %collective-permute-done.4.refs_1_), channel_id=1, source_target_pairs={{0,16},{8,56},{16,32},{24,8},{32,48},{40,24},{48,0},{56,40},{64,80... | collective-permute-start | bytes 1966088 | tf_op jit(solution)/shard_map/ppermute | solution.py:509
  52.5 18.5 %collective-permute-start.9 = (bf16[320,1024]{1,0:T(8,128)(2,1)S(1)}, bf16[320,1024]{1,0:T(8,128)(2,1)S(1)}, u32[]{:S(2)}, u32[]{:S(2)}) collective-permute-start(bf16[320,1024]{1,0:T(8,128)(2,1)S(1)} %collective-permute-done.2.refs_0_), channel_id=1, source_target_pairs={{0,48},{8,24},{16,0},{24,40},{32,16},{40,56},{48,32},{56,8},{64,11... | collective-permute-start | bytes 1966088 | tf_op jit(solution)/shard_map/ppermute | solution.py:509
  54.5 17.2 %collective-permute-start.11 = (bf16[320,1024]{1,0:T(8,128)(2,1)S(1)}, bf16[320,1024]{1,0:T(8,128)(2,1)S(1)}, u32[]{:S(2)}, u32[]{:S(2)}) collective-permute-start(bf16[320,1024]{1,0:T(8,128)(2,1)S(1)} %collective-permute-done.2.refs_0_), channel_id=1, source_target_pairs={{0,8},{8,0},{16,24},{24,16},{32,40},{40,32},{48,56},{56,48},{64,72... | collective-permute-start | bytes 1966088 | tf_op jit(solution)/shard_map/ppermute | solution.py:509
  56.5 15.2 %collective-permute-start.12 = (bf16[320,1024]{1,0:T(8,128)(2,1)S(1)}, bf16[320,1024]{1,0:T(8,128)(2,1)}, u32[]{:S(2)}, u32[]{:S(2)}) collective-permute-start(bf16[320,1024]{1,0:T(8,128)(2,1)S(1)} %collective-permute-done.4.refs_1_), channel_id=1, source_target_pairs={{0,8},{8,0},{16,24},{24,16},{32,40},{40,32},{48,56},{56,48},{64,72... | collective-permute-start | bytes 1966088 | tf_op jit(solution)/shard_map/ppermute | solution.py:509
  71.0 3.4 %copy-start.4 = (bf16[320,1024]{1,0:T(8,128)(2,1)}, bf16[320,1024]{1,0:T(8,128)(2,1)S(1)}, u32[]{:S(2)}) copy-start(bf16[320,1024]{1,0:T(8,128)(2,1)S(1)} %collective-permute-done.10.refs_3_) | copy-start | bytes 1966084
  71.0 3.4 %copy-start.5 = (bf16[320,1024]{1,0:T(8,128)(2,1)}, bf16[320,1024]{1,0:T(8,128)(2,1)S(1)}, u32[]{:S(2)}) copy-start(bf16[320,1024]{1,0:T(8,128)(2,1)S(1)} %collective-permute-done.9.refs_2_) | copy-start | bytes 1966084
  71.0 2.4 %collective-permute-start.13 = (bf16[320,1024]{1,0:T(8,128)(2,1)S(1)}, bf16[320,1024]{1,0:T(8,128)(2,1)}, u32[]{:S(2)}, u32[]{:S(2)}) collective-permute-start(bf16[320,1024]{1,0:T(8,128)(2,1)S(1)} %collective-permute-done.9.refs_2_), channel_id=1, source_target_pairs={{0,8},{8,0},{16,24},{24,16},{32,40},{40,32},{48,56},{56,48},{64,72... | collective-permute-start | bytes 1966088 | tf_op jit(solution)/shard_map/ppermute | solution.py:509
  71.6 2.8 %collective-permute-start.14 = (bf16[320,1024]{1,0:T(8,128)(2,1)S(1)}, bf16[320,1024]{1,0:T(8,128)(2,1)}, u32[]{:S(2)}, u32[]{:S(2)}) collective-permute-start(bf16[320,1024]{1,0:T(8,128)(2,1)S(1)} %collective-permute-done.10.refs_3_), channel_id=1, source_target_pairs={{0,8},{8,0},{16,24},{24,16},{32,40},{40,32},{48,56},{56,48},{64,72... | collective-permute-start | bytes 1966088 | tf_op jit(solution)/shard_map/ppermute | solution.py:509
  71.7 2.7 %copy-start.6 = (bf16[320,1024]{1,0:T(8,128)(2,1)}, bf16[320,1024]{1,0:T(8,128)(2,1)S(1)}, u32[]{:S(2)}) copy-start(bf16[320,1024]{1,0:T(8,128)(2,1)S(1)} %collective-permute-done.11.refs_4_) | copy-start | bytes 1966084
  83.8 39.1 %collective-permute-start.15 = (bf16[4,288,640]{2,1,0:T(8,128)(2,1)}, bf16[4,288,640]{2,1,0:T(8,128)(2,1)S(1)}, u32[]{:S(2)}, u32[]{:S(2)}) collective-permute-start(bf16[4,288,640]{2,1,0:T(8,128)(2,1)} %get-tuple-element.90), channel_id=1, source_target_pairs={{0,1},{1,0},{2,3},{3,2},{4,5},{5,4},{6,7},{7,6},{8,9},{9,8},{10,11... | collective-permute-start | bytes 4423688 | tf_op jit(solution)/shard_map/ppermute | solution.py:528
  85.1 34.5 %collective-permute-start.16 = (bf16[2,288,640]{2,1,0:T(8,128)(2,1)}, bf16[2,288,640]{2,1,0:T(8,128)(2,1)S(1)}, u32[]{:S(2)}, u32[]{:S(2)}) collective-permute-start(bf16[2,288,640]{2,1,0:T(8,128)(2,1)} %get-tuple-element.92), channel_id=1, source_target_pairs={{0,2},{1,3},{2,4},{3,5},{4,6},{5,7},{6,0},{7,1},{8,10},{9,11},{10,... | collective-permute-start | bytes 2211848 | tf_op jit(solution)/shard_map/ppermute | solution.py:529
  86.5 34.6 %collective-permute-start.17 = (bf16[2,288,640]{2,1,0:T(8,128)(2,1)}, bf16[2,288,640]{2,1,0:T(8,128)(2,1)}, u32[]{:S(2)}, u32[]{:S(2)}) collective-permute-start(bf16[2,288,640]{2,1,0:T(8,128)(2,1)} %get-tuple-element.93), channel_id=1, source_target_pairs={{0,4},{1,5},{2,6},{3,7},{4,0},{5,1},{6,2},{7,3},{8,12},{9,13},{10,... | collective-permute-start | bytes 2211848 | tf_op jit(solution)/shard_map/ppermute | solution.py:529
  89.1 32.0 %collective-permute-start.18 = (bf16[2,288,640]{2,1,0:T(8,128)(2,1)}, bf16[2,288,640]{2,1,0:T(8,128)(2,1)}, u32[]{:S(2)}, u32[]{:S(2)}) collective-permute-start(bf16[2,288,640]{2,1,0:T(8,128)(2,1)} %get-tuple-element.94), channel_id=1, source_target_pairs={{0,6},{1,7},{2,0},{3,1},{4,2},{5,3},{6,4},{7,5},{8,14},{9,15},{10,... | collective-permute-start | bytes 2211848 | tf_op jit(solution)/shard_map/ppermute | solution.py:529
  100.1 21.0 %copy-start.1 = (bf16[2,288,640]{2,1,0:T(8,128)(2,1)S(1)}, bf16[2,288,640]{2,1,0:T(8,128)(2,1)}, u32[]{:S(2)}) copy-start(bf16[2,288,640]{2,1,0:T(8,128)(2,1)} %get-tuple-element.91) | copy-start | bytes 2211844
  122.8 1.4 copy-start
  125.4 11.6 %collective-permute-start.19 = (bf16[288,640]{1,0:T(8,128)(2,1)}, bf16[288,640]{1,0:T(8,128)(2,1)S(1)}, u32[]{:S(2)}, u32[]{:S(2)}) collective-permute-start(bf16[288,640]{1,0:T(8,128)(2,1)} %get-tuple-element.104), channel_id=1, source_target_pairs={{0,2},{1,3},{2,4},{3,5},{4,6},{5,7},{6,0},{7,1},{8,10},{9,11},{10,... | collective-permute-start | bytes 1105928 | tf_op jit(solution)/shard_map/ppermute | solution.py:538
  126.4 19.3 %collective-permute-start.20 = (bf16[288,640]{1,0:T(8,128)(2,1)}, bf16[288,640]{1,0:T(8,128)(2,1)S(1)}, u32[]{:S(2)}, u32[]{:S(2)}) collective-permute-start(bf16[288,640]{1,0:T(8,128)(2,1)} %get-tuple-element.105), channel_id=1, source_target_pairs={{0,4},{1,5},{2,6},{3,7},{4,0},{5,1},{6,2},{7,3},{8,12},{9,13},{10,... | collective-permute-start | bytes 1105928 | tf_op jit(solution)/shard_map/ppermute | solution.py:538
  129.4 16.3 %collective-permute-start.21 = (bf16[288,640]{1,0:T(8,128)(2,1)S(1)}, bf16[288,640]{1,0:T(8,128)(2,1)S(1)}, u32[]{:S(2)}, u32[]{:S(2)}) collective-permute-start(bf16[288,640]{1,0:T(8,128)(2,1)S(1)} %get-tuple-element.106), channel_id=1, source_target_pairs={{0,6},{1,7},{2,0},{3,1},{4,2},{5,3},{6,4},{7,5},{8,14},{9,15},{10,... | collective-permute-start | bytes 1105928 | tf_op jit(solution)/shard_map/ppermute | solution.py:538
  129.5 17.1 %collective-permute-start.22 = (bf16[288,640]{1,0:T(8,128)(2,1)S(1)}, bf16[288,640]{1,0:T(8,128)(2,1)}, u32[]{:S(2)}, u32[]{:S(2)}) collective-permute-start(bf16[288,640]{1,0:T(8,128)(2,1)S(1)} %get-tuple-element.108), channel_id=1, source_target_pairs={{0,1},{1,0},{2,3},{3,2},{4,5},{5,4},{6,7},{7,6},{8,9},{9,8},{10,11... | collective-permute-start | bytes 1105928 | tf_op jit(solution)/shard_map/ppermute | solution.py:539
  129.7 18.9 %all-to-all-start.1 = ((bf16[16,64,256]{2,1,0:T(8,128)(2,1)}), bf16[16,64,256]{2,1,0:T(8,128)(2,1)S(1)}, u32[]{:S(2)}, u32[]{:S(2)}) async-start(bf16[16,64,256]{2,1,0:T(8,128)(2,1)} %bitcast.17), calls=%async_computation.1 | async-start | bytes 1048576 | tf_op jit(solution)/shard_map/all_to_all | solution.py:542

commit v5 on v4

--- a/solution.py
+++ b/solution.py
@@ -211,17 +211,29 @@
 
     @pl.when(step < heads)
     def _():
+        items = []
         for slot in range(PER):
             lanes = slice(slot * DIM, (slot + 1) * DIM)
             query, grad = query_ref[:, lanes], (grad_ref[:, lanes].astype(F32) * inverse_ref[:, lanes]).astype(BF)
-            delta = row_delta(grad, out_ref[:, lanes])
-            for start in range(0, prompt, 512):
-                key_block(slot, weight_ref[slot, start : start + 512, :], value_ref[start : start + 512, :], grad, query, delta, start, 512, 0)
-            key_block(slot, weight_ref[slot, prompt : prompt + half, :], reply_value_ref[:half], grad, query, delta, prompt, half, 0)
-            key_block(
-                slot, weight_ref[slot, prompt + half :, half:], reply_value_ref[half:], grad[half:], query[half:], delta[:, half:],
-                prompt + half, half, half,
-            )
+            items.append((slot, query, grad, row_delta(grad, out_ref[:, lanes])))
+        whole = [(value_ref, start, start, 512) for start in range(0, prompt, 512)] + [(reply_value_ref, 0, prompt, half)]
+        for low, blocks in ((0, whole), (half, [(reply_value_ref, half, prompt + half, half)])):
+            queries = jnp.concatenate([query[low:] for _, query, _, _ in items], 0)
+            grads = jnp.concatenate([grad[low:] for _, _, grad, _ in items], 0)
+            for source, base, start, size in blocks:
+                value = source[base : base + size, :]
+                block = slice(start, start + size)
+                parts, weights = [], []
+                for slot, _, grad, delta in items:
+                    weight = weight_ref[slot, block, low:]
+                    part = (weight.astype(F32) * (dot_nt(value, grad[low:]) - delta[:, low:])).astype(BF)
+                    score_grad[slot, block, low:] = part
+                    parts.append(part)
+                    weights.append(weight)
+                key_grad[block, :] += dot_nn(jnp.concatenate(parts, 1), queries)
+                value_grad[block, :] += dot_nn(jnp.concatenate(weights, 1), grads)
+        for slot in range(PER):
+            lanes = slice(slot * DIM, (slot + 1) * DIM)
             query_grad_ref[:, lanes] = (dot_nn(key_t[...], score_grad[slot]).T * SCALE).astype(BF)
 
     @pl.when(step == heads)

time: 150 us -> 150 us (level)
  transfers between devices with their start and end apart: 25 -> 25, of which waited for: 5 -> 5; matrix products, arithmetic and copies ran while one was open for 5% -> 5% of each run, Pallas kernels for 40% -> 39%
where the time goes in v5:
time: 150 us; the launch traced here: 149 us
  Pallas kernels  68 us (45%)
  starting transfers between devices  39.1 us (26%)
  waiting for transfers between devices  30.6 us (20%)
  other arithmetic  6.48 us (4%)
  local copies, waits for them, and re-layouts  3.52 us (2%)
  between operations  1.54 us (1%)
    pallas_call x3, Pallas kernels, absorb(): pl.pallas_call(functools.partial(absorb_kernel, project, back, resume), i...  33.7 us
    pallas_call x1, Pallas kernels, attention_backward(): pl.pallas_call(backward_kernel, grid=(steps + 1,), in_specs=[pl.BlockSpec...  18.4 us
    ppermute x15, starting transfers between devices, body(): send = lambda chunk, perm: lax.ppermute(chunk, 'seq', perm)  16.5 us
    all_to_all x1, waiting for transfers between devices, body(): lax.all_to_all(jnp.broadcast_to(own[None], (n_seq,) + own.shape), 'seq',...  16.5 us
    pallas_call x1, Pallas kernels, attention_forward(): pl.pallas_call(forward_kernel, grid=(steps + 1,), in_specs=[pl.BlockSpec(...  15.9 us
    ppermute x3, waiting for transfers between devices, body(): lax.ppermute(first[dy], 'head', head_perm(dy, 0))  8.76 us
    all_to_all x1, starting transfers between devices, body(): lax.all_to_all(kv_grad.reshape(n_seq, prompt_rows, 2 * DIM), 'seq', 0, 0)  7.24 us
    ppermute x3, starting transfers between devices, body(): lax.ppermute(turns[dy], 'head', head_perm(dy, 0))  5.08 us
  transfers between devices with their start and end apart: 25, of which 5 were waited for; matrix products, arithmetic and copies ran while one was open for 5% of the time, Pallas kernels for 39%

profile of v5, /device:TPU:1, one launch (start us, length us, event | category | flops | bytes accessed | tf_op | source)
XLA Modules:
  0.0 149.3 jit_solution(10334563586469463445)
XLA Ops:
  0.6 0.0 copy-start.8
  0.6 4.7 %collective-permute-start = (bf16[320,1024]{1,0:T(8,128)(2,1)}, bf16[320,1024]{1,0:T(8,128)(2,1)S(1)}, u32[]{:S(2)}, u32[]{:S(2)}) collective-permute-start(bf16[320,1024]{1,0:T(8,128)(2,1)} %bitcast.28), channel_id=1, source_target_pairs={{0,16},{8,56},{16,32},{24,8},{32,48},{40,24},{48,0},{56,40},{64,80... | collective-permute-start | bytes 1966088 | tf_op jit(solution)/shard_map/ppermute | solution.py:521
  5.3 0.0 collective-permute-start.1
  5.3 2.7 %collective-permute-start.2 = (bf16[320,1024]{1,0:T(8,128)(2,1)}, bf16[320,1024]{1,0:T(8,128)(2,1)S(1)}, u32[]{:S(2)}, u32[]{:S(2)}) collective-permute-start(bf16[320,1024]{1,0:T(8,128)(2,1)} %bitcast.30), channel_id=1, source_target_pairs={{0,64},{8,72},{16,80},{24,88},{32,96},{40,104},{48,112},{56,120},{... | collective-permute-start | bytes 1966088 | tf_op jit(solution)/shard_map/ppermute | solution.py:521
  8.0 0.7 pad_maximum_fusion.1
  8.8 0.8 broadcast_in_dim.2
  9.6 4.7 %all-to-all-start = ((bf16[16,64,256]{2,1,0:T(8,128)(2,1)}), bf16[16,64,256]{2,1,0:T(8,128)(2,1)S(1)}, u32[]{:S(2)}, u32[]{:S(2)}) async-start(bf16[16,64,256]{2,1,0:T(8,128)(2,1)} %broadcast_in_dim.2), calls=%async_computation | async-start | bytes 1048576 | tf_op jit(solution)/shard_map/all_to_all | solution.py:519
  14.3 0.3 collective-permute-start.5
  14.6 16.5 %all-to-all-done = bf16[16,64,256]{2,1,0:T(8,128)(2,1)S(1)} async-done(((bf16[16,64,256]{2,1,0:T(8,128)(2,1)}), bf16[16,64,256]{2,1,0:T(8,128)(2,1)S(1)}, u32[]{:S(2)}, u32[]{:S(2)}) %all-to-all-start) | async-done | bytes 524320 | tf_op jit(solution)/shard_map/all_to_all | solution.py:519
  31.1 0.0 collective-permute-done.refs_1_
  31.1 0.0 collective-permute-done.1.refs_2_
  31.1 0.0 collective-permute-done.2.refs_0_
  31.1 0.0 copy-start.2
  31.1 0.5 collective-permute-start.3
  31.6 0.8 collective-permute-start.6
  32.4 2.9 %collective-permute-start.4 = (bf16[320,1024]{1,0:T(8,128)(2,1)S(1)}, bf16[320,1024]{1,0:T(8,128)(2,1)S(1)}, u32[]{:S(2)}, u32[]{:S(2)}) collective-permute-start(bf16[320,1024]{1,0:T(8,128)(2,1)S(1)} %collective-permute-done.2.refs_0_), channel_id=1, source_target_pairs={{0,16},{8,56},{16,32},{24,8},{32,48},{40,24},{48,0},{56,40},{64,80... | collective-permute-start | bytes 1966088 | tf_op jit(solution)/shard_map/ppermute | solution.py:521
  35.2 0.0 collective-permute-start.7
  35.9 15.9 %attention_forward.1 = (bf16[8,1536,512]{2,1,0:T(8,128)(2,1)}, bf16[1024,512]{1,0:T(8,128)(2,1)}, bf16[512,1024]{1,0:T(8,128)(2,1)}, bf16[64,1024]{1,0:T(8,128)(...) custom-call(s32[1]{0:T(128)} %bitcast.9.index_ref, s32[1]{0:T(128)S(6)} %copy.30.length_ref, bf16[512,1024]{1,0:T(8,128)(2,1)} %query_ref.3, ...), custom_call_target="tpu_custom_call" | custom-call | flops 3221225472 | bytes 18874368 | tf_op jit(solution)/shard_map/attention_forward/pallas_call | solution.py:139
  51.8 0.0 collective-permute-done.5.refs_4_
  51.8 0.0 collective-permute-done.3.refs_3_
  51.9 0.0 collective-permute-done.4.refs_1_
  51.9 0.0 copy-start.3
  51.9 0.6 collective-permute-start.8
  52.5 0.0 collective-permute-start.10
  52.5 1.5 collective-permute-start.9
  54.0 0.6 pad_add_fusion.order_ref
  54.5 2.0 %collective-permute-start.11 = (bf16[320,1024]{1,0:T(8,128)(2,1)S(1)}, bf16[320,1024]{1,0:T(8,128)(2,1)S(1)}, u32[]{:S(2)}, u32[]{:S(2)}) collective-permute-start(bf16[320,1024]{1,0:T(8,128)(2,1)S(1)} %collective-permute-done.2.refs_0_), channel_id=1, source_target_pairs={{0,8},{8,0},{16,24},{24,16},{32,40},{40,32},{48,56},{56,48},{64,72... | collective-permute-start | bytes 1966088 | tf_op jit(solution)/shard_map/ppermute | solution.py:521
  56.5 0.0 collective-permute-start.12
  56.5 0.0 collective-permute-done.8.refs_7_
  56.5 14.5 %absorb_both.1 = (bf16[4,288,640]{2,1,0:T(8,128)(2,1)}, bf16[4,288,640]{2,1,0:T(8,128)(2,1)}, bf16[2,288,640]{2,1,0:T(8,128)(2,1)}, bf16[2,288,640]{2,1,0:T(8,12...) custom-call(s32[4]{0:T(128)} %pad_add_fusion.order_ref, ...), custom_call_target="tpu_custom_call" | custom-call | flops 6039797760 | bytes 9437184 | tf_op jit(solution)/shard_map/absorb_both/pallas_call | solution.py:474
  71.0 0.0 collective-permute-done.10.refs_3_
  71.0 0.0 collective-permute-done.9.refs_2_
  71.1 0.6 collective-permute-start.13
  71.6 0.1 collective-permute-start.14
  71.7 0.0 collective-permute-done.12.refs_5_
  71.7 1.8 %collective-permute-done.13.refs_6_ = bf16[320,1024]{1,0:T(8,128)(2,1)} collective-permute-done((bf16[320,1024]{1,0:T(8,128)(2,1)S(1)}, bf16[320,1024]{1,0:T(8,128)(2,1)}, u32[]{:S(2)}, u32[]{:S(2)}) %collective-permute-start.13) | collective-permute-done | bytes 655392 | tf_op jit(solution)/shard_map/ppermute | solution.py:521
  73.5 0.9 collective-permute-done.14.refs_7_
  74.4 9.4 %absorb_products.1 = (bf16[4,288,640]{2,1,0:T(8,128)(2,1)}, bf16[4,288,640]{2,1,0:T(8,128)(2,1)}, bf16[2,288,640]{2,1,0:T(8,128)(2,1)}, bf16[2,288,640]{2,1,0:T(...) custom-call(s32[4]{0:T(128)} %pad_add_fusion.order_ref, ...), custom_call_target="tpu_custom_call", output_to_operand_aliasing={{0}: (15, {}), {1}: (16, {}), {2}: (17, {}), {3}: (18, {}),... | custom-call | flops 3019898880 | bytes 9437184 | tf_op jit(solution)/shard_map/absorb_products/pallas_call | solution.py:474
  83.8 1.3 collective-permute-start.15
  85.1 1.4 collective-permute-start.16
  86.5 2.6 %collective-permute-start.17 = (bf16[2,288,640]{2,1,0:T(8,128)(2,1)}, bf16[2,288,640]{2,1,0:T(8,128)(2,1)}, u32[]{:S(2)}, u32[]{:S(2)}) collective-permute-start(bf16[2,288,640]{2,1,0:T(8,128)(2,1)} %get-tuple-element.93), channel_id=1, source_target_pairs={{0,4},{1,5},{2,6},{3,7},{4,0},{5,1},{6,2},{7,3},{8,12},{9,13},{10,... | collective-permute-start | bytes 2211848 | tf_op jit(solution)/shard_map/ppermute | solution.py:541
  89.1 1.1 collective-permute-start.18
  90.2 9.9 %absorb_upstream.1 = (bf16[64,1024]{1,0:T(8,128)(2,1)}, bf16[512,1024]{1,0:T(8,128)(2,1)}) custom-call(s32[4]{0:T(128)} %pad_add_fusion.order_ref, s32[1]{0:T(128)} %bitcast.4.core_ref, s32[1]{0:T(128)} %bitcast.5.head_ref, s32[1]{0:T(128)} %bitcast.6.half_ref, s32[1]{0:T(128)S(6)} %copy.30.length_ref, bf16[320,1024]{1,0:T(8,128)(2,1)} %copy-done.2, ...), custom_call_target="tpu_custom_call" | custom-call | flops 3019898880 | bytes 9437184 | tf_op jit(solution)/shard_map/absorb_upstream/pallas_call | solution.py:474
  100.1 18.4 %attention_backward.1 = (bf16[512,1024]{1,0:T(8,128)(2,1)}, bf16[64,1024]{1,0:T(8,128)(2,1)}, bf16[1024,256]{1,0:T(8,128)(2,1)}, bf16[512,128]{1,0:T(8,128)(2,1)}, bf16[512,128]{1,0:T(8,128)(2,1)}) custom-call(bf16[8,1536,512]{2,1,0:T(8,128)(2,1)} %get-tuple-element.95.weight_ref, bf16[1024,512]{1,0:T(8,128)(2,1)} %get-tuple-element.96.prompt_weight_ref, ...), custom_call_target="tpu_custom_call" | custom-call | flops 6442450944 | bytes 18874368 | tf_op jit(solution)/shard_map/attention_backward/pallas_call | solution.py:270
  118.4 0.0 collective-permute-done.16
  118.5 2.6 %collective-permute-done.17 = bf16[2,288,640]{2,1,0:T(8,128)(2,1)} collective-permute-done((bf16[2,288,640]{2,1,0:T(8,128)(2,1)}, bf16[2,288,640]{2,1,0:T(8,128)(2,1)}, u32[]{:S(2)}, u32[]{:S(2)}) %collective-permute-start.17) | collective-permute-done | bytes 737312 | tf_op jit(solution)/shard_map/ppermute | solution.py:541
  121.1 1.7 %add_convert_fusion = bf16[2,288,640]{2,1,0:T(8,128)(2,1)S(1)} fusion(bf16[2,288,640]{2,1,0:T(8,128)(2,1)} %collective-permute-done.18, bf16[2,288,640]{2,1,0:T(8,128)(2,1)} %collective-permute-done.17, bf16[2,288,640]{2,1,0:T(8,128)(2,1)S(1)} %collective-permute-done.16, bf16[2,288,640]{2,1,0:T(8,128)(2,1)S(1)} %copy-done.1), kind=kLoop, calls=%fused_computation | loop fusion | flops 2949120 | bytes 3686400 | tf_op jit(solution)/shard_map/convert_element_type | solution.py:548
  122.8 0.1 slice_bitcast_fusion
  122.9 1.3 copy-done
  124.2 1.2 fusion.3
  125.4 1.0 collective-permute-start.19
  126.4 3.0 %collective-permute-start.20 = (bf16[288,640]{1,0:T(8,128)(2,1)}, bf16[288,640]{1,0:T(8,128)(2,1)S(1)}, u32[]{:S(2)}, u32[]{:S(2)}) collective-permute-start(bf16[288,640]{1,0:T(8,128)(2,1)} %get-tuple-element.105), channel_id=1, source_target_pairs={{0,4},{1,5},{2,6},{3,7},{4,0},{5,1},{6,2},{7,3},{8,12},{9,13},{10,... | collective-permute-start | bytes 1105928 | tf_op jit(solution)/shard_map/ppermute | solution.py:550
  129.4 0.1 collective-permute-start.21
  129.5 0.2 collective-permute-start.22
  129.7 7.2 %all-to-all-start.1 = ((bf16[16,64,256]{2,1,0:T(8,128)(2,1)}), bf16[16,64,256]{2,1,0:T(8,128)(2,1)S(1)}, u32[]{:S(2)}, u32[]{:S(2)}) async-start(bf16[16,64,256]{2,1,0:T(8,128)(2,1)} %bitcast.17), calls=%async_computation.1 | async-start | bytes 1048576 | tf_op jit(solution)/shard_map/all_to_all | solution.py:554
  137.0 8.8 %collective-permute-done.20 = bf16[288,640]{1,0:T(8,128)(2,1)S(1)} collective-permute-done((bf16[288,640]{1,0:T(8,128)(2,1)}, bf16[288,640]{1,0:T(8,128)(2,1)S(1)}, u32[]{:S(2)}, u32[]{:S(2)}) %collective-permute-start.20) | collective-permute-done | bytes 368672 | tf_op jit(solution)/shard_map/ppermute | solution.py:550
  145.7 0.0 collective-permute-done.21
  145.7 0.2 add_convert_fusion.2
  145.9 0.6 slice.62
  146.6 1.1 add_convert_fusion.1
  147.7 0.9 pad_maximum_fusion
  148.6 0.0 all-to-all-done.1
  148.6 0.1 reduce_sum.12
  148.6 0.6 fusion.4
  (24 shorter events, 0.1 us)
Async XLA Ops:
  0.6 13.7 %copy-start.8 = (bf16[1024,320]{0,1:T(8,128)(2,1)S(1)}, bf16[1024,320]{0,1:T(8,128)(2,1)}, u32[]{:S(2)}) copy-start(bf16[1024,320]{0,1:T(8,128)(2,1)} %param.17) | copy-start | bytes 1966084
  0.6 30.4 %collective-permute-start = (bf16[320,1024]{1,0:T(8,128)(2,1)}, bf16[320,1024]{1,0:T(8,128)(2,1)S(1)}, u32[]{:S(2)}, u32[]{:S(2)}) collective-permute-start(bf16[320,1024]{1,0:T(8,128)(2,1)} %bitcast.28), channel_id=1, source_target_pairs={{0,16},{8,56},{16,32},{24,8},{32,48},{40,24},{48,0},{56,40},{64,80... | collective-permute-start | bytes 1966088 | tf_op jit(solution)/shard_map/ppermute | solution.py:521
  5.3 25.8 %collective-permute-start.1 = (bf16[320,1024]{1,0:T(8,128)(2,1)}, bf16[320,1024]{1,0:T(8,128)(2,1)}, u32[]{:S(2)}, u32[]{:S(2)}) collective-permute-start(bf16[320,1024]{1,0:T(8,128)(2,1)} %bitcast.29), channel_id=1, source_target_pairs={{0,48},{8,24},{16,0},{24,40},{32,16},{40,56},{48,32},{56,8},{64,11... | collective-permute-start | bytes 1966088 | tf_op jit(solution)/shard_map/ppermute | solution.py:521
  5.3 25.8 %collective-permute-start.2 = (bf16[320,1024]{1,0:T(8,128)(2,1)}, bf16[320,1024]{1,0:T(8,128)(2,1)S(1)}, u32[]{:S(2)}, u32[]{:S(2)}) collective-permute-start(bf16[320,1024]{1,0:T(8,128)(2,1)} %bitcast.30), channel_id=1, source_target_pairs={{0,64},{8,72},{16,80},{24,88},{32,96},{40,104},{48,112},{56,120},{... | collective-permute-start | bytes 1966088 | tf_op jit(solution)/shard_map/ppermute | solution.py:521
  9.6 21.4 %all-to-all-start = ((bf16[16,64,256]{2,1,0:T(8,128)(2,1)}), bf16[16,64,256]{2,1,0:T(8,128)(2,1)S(1)}, u32[]{:S(2)}, u32[]{:S(2)}) async-start(bf16[16,64,256]{2,1,0:T(8,128)(2,1)} %broadcast_in_dim.2), calls=%async_computation | async-start | bytes 1048576 | tf_op jit(solution)/shard_map/all_to_all | solution.py:519
  14.3 37.5 %collective-permute-start.5 = (bf16[320,1024]{1,0:T(8,128)(2,1)S(1)}, bf16[320,1024]{1,0:T(8,128)(2,1)}, u32[]{:S(2)}, u32[]{:S(2)}) collective-permute-start(bf16[320,1024]{1,0:T(8,128)(2,1)S(1)} %bitcast.32), channel_id=1, source_target_pairs={{0,8},{8,0},{16,24},{24,16},{32,40},{40,32},{48,56},{56,48},{64,72... | collective-permute-start | bytes 1966088 | tf_op jit(solution)/shard_map/ppermute | solution.py:521
  31.1 4.8 %copy-start.7 = (bf16[16,64,256]{2,1,0:T(8,128)(2,1)}, bf16[16,64,256]{2,1,0:T(8,128)(2,1)S(1)}, u32[]{:S(2)}) copy-start(bf16[16,64,256]{2,1,0:T(8,128)(2,1)S(1)} %all-to-all-done) | copy-start | bytes 1572868
  31.1 20.7 %copy-start.9 = (bf16[320,1024]{1,0:T(8,128)(2,1)}, bf16[320,1024]{1,0:T(8,128)(2,1)S(1)}, u32[]{:S(2)}) copy-start(bf16[320,1024]{1,0:T(8,128)(2,1)S(1)} %collective-permute-done.refs_1_) | copy-start | bytes 1966084
  31.1 23.4 %copy-start.2 = (bf16[320,1024]{1,0:T(8,128)(2,1)}, bf16[320,1024]{1,0:T(8,128)(2,1)S(1)}, u32[]{:S(2)}) copy-start(bf16[320,1024]{1,0:T(8,128)(2,1)S(1)} %collective-permute-done.2.refs_0_) | copy-start | bytes 1966084
  31.1 20.7 %collective-permute-start.3 = (bf16[320,1024]{1,0:T(8,128)(2,1)S(1)}, bf16[320,1024]{1,0:T(8,128)(2,1)}, u32[]{:S(2)}, u32[]{:S(2)}) collective-permute-start(bf16[320,1024]{1,0:T(8,128)(2,1)S(1)} %collective-permute-done.refs_1_), channel_id=1, source_target_pairs={{0,16},{8,56},{16,32},{24,8},{32,48},{40,24},{48,0},{56,40},{64,80... | collective-permute-start | bytes 1966088 | tf_op jit(solution)/shard_map/ppermute | solution.py:521
  31.6 20.3 %collective-permute-start.6 = (bf16[320,1024]{1,0:T(8,128)(2,1)S(1)}, bf16[320,1024]{1,0:T(8,128)(2,1)}, u32[]{:S(2)}, u32[]{:S(2)}) collective-permute-start(bf16[320,1024]{1,0:T(8,128)(2,1)S(1)} %collective-permute-done.refs_1_), channel_id=1, source_target_pairs={{0,8},{8,0},{16,24},{24,16},{32,40},{40,32},{48,56},{56,48},{64,72... | collective-permute-start | bytes 1966088 | tf_op jit(solution)/shard_map/ppermute | solution.py:521
  32.4 19.5 %collective-permute-start.4 = (bf16[320,1024]{1,0:T(8,128)(2,1)S(1)}, bf16[320,1024]{1,0:T(8,128)(2,1)S(1)}, u32[]{:S(2)}, u32[]{:S(2)}) collective-permute-start(bf16[320,1024]{1,0:T(8,128)(2,1)S(1)} %collective-permute-done.2.refs_0_), channel_id=1, source_target_pairs={{0,16},{8,56},{16,32},{24,8},{32,48},{40,24},{48,0},{56,40},{64,80... | collective-permute-start | bytes 1966088 | tf_op jit(solution)/shard_map/ppermute | solution.py:521
  35.2 16.6 %collective-permute-start.7 = (bf16[320,1024]{1,0:T(8,128)(2,1)}, bf16[320,1024]{1,0:T(8,128)(2,1)}, u32[]{:S(2)}, u32[]{:S(2)}) collective-permute-start(bf16[320,1024]{1,0:T(8,128)(2,1)} %collective-permute-done.1.refs_2_), channel_id=1, source_target_pairs={{0,8},{8,0},{16,24},{24,16},{32,40},{40,32},{48,56},{56,48},{64,72... | collective-permute-start | bytes 1966088 | tf_op jit(solution)/shard_map/ppermute | solution.py:521
  51.9 19.1 %copy-start.3 = (bf16[320,1024]{1,0:T(8,128)(2,1)}, bf16[320,1024]{1,0:T(8,128)(2,1)S(1)}, u32[]{:S(2)}) copy-start(bf16[320,1024]{1,0:T(8,128)(2,1)S(1)} %collective-permute-done.4.refs_1_) | copy-start | bytes 1966084
  51.9 4.6 %collective-permute-start.8 = (bf16[320,1024]{1,0:T(8,128)(2,1)}, bf16[320,1024]{1,0:T(8,128)(2,1)}, u32[]{:S(2)}, u32[]{:S(2)}) collective-permute-start(bf16[320,1024]{1,0:T(8,128)(2,1)} %collective-permute-done.3.refs_3_), channel_id=1, source_target_pairs={{0,8},{8,0},{16,24},{24,16},{32,40},{40,32},{48,56},{56,48},{64,72... | collective-permute-start | bytes 1966088 | tf_op jit(solution)/shard_map/ppermute | solution.py:521
  52.5 18.5 %collective-permute-start.10 = (bf16[320,1024]{1,0:T(8,128)(2,1)S(1)}, bf16[320,1024]{1,0:T(8,128)(2,1)S(1)}, u32[]{:S(2)}, u32[]{:S(2)}) collective-permute-start(bf16[320,1024]{1,0:T(8,128)(2,1)S(1)} %collective-permute-done.4.refs_1_), channel_id=1, source_target_pairs={{0,16},{8,56},{16,32},{24,8},{32,48},{40,24},{48,0},{56,40},{64,80... | collective-permute-start | bytes 1966088 | tf_op jit(solution)/shard_map/ppermute | solution.py:521
  52.5 18.5 %collective-permute-start.9 = (bf16[320,1024]{1,0:T(8,128)(2,1)S(1)}, bf16[320,1024]{1,0:T(8,128)(2,1)S(1)}, u32[]{:S(2)}, u32[]{:S(2)}) collective-permute-start(bf16[320,1024]{1,0:T(8,128)(2,1)S(1)} %collective-permute-done.2.refs_0_), channel_id=1, source_target_pairs={{0,48},{8,24},{16,0},{24,40},{32,16},{40,56},{48,32},{56,8},{64,11... | collective-permute-start | bytes 1966088 | tf_op jit(solution)/shard_map/ppermute | solution.py:521
  54.5 17.2 %collective-permute-start.11 = (bf16[320,1024]{1,0:T(8,128)(2,1)S(1)}, bf16[320,1024]{1,0:T(8,128)(2,1)S(1)}, u32[]{:S(2)}, u32[]{:S(2)}) collective-permute-start(bf16[320,1024]{1,0:T(8,128)(2,1)S(1)} %collective-permute-done.2.refs_0_), channel_id=1, source_target_pairs={{0,8},{8,0},{16,24},{24,16},{32,40},{40,32},{48,56},{56,48},{64,72... | collective-permute-start | bytes 1966088 | tf_op jit(solution)/shard_map/ppermute | solution.py:521
  56.5 15.2 %collective-permute-start.12 = (bf16[320,1024]{1,0:T(8,128)(2,1)S(1)}, bf16[320,1024]{1,0:T(8,128)(2,1)}, u32[]{:S(2)}, u32[]{:S(2)}) collective-permute-start(bf16[320,1024]{1,0:T(8,128)(2,1)S(1)} %collective-permute-done.4.refs_1_), channel_id=1, source_target_pairs={{0,8},{8,0},{16,24},{24,16},{32,40},{40,32},{48,56},{56,48},{64,72... | collective-permute-start | bytes 1966088 | tf_op jit(solution)/shard_map/ppermute | solution.py:521
  71.0 3.4 %copy-start.4 = (bf16[320,1024]{1,0:T(8,128)(2,1)}, bf16[320,1024]{1,0:T(8,128)(2,1)S(1)}, u32[]{:S(2)}) copy-start(bf16[320,1024]{1,0:T(8,128)(2,1)S(1)} %collective-permute-done.10.refs_3_) | copy-start | bytes 1966084
  71.0 3.4 %copy-start.5 = (bf16[320,1024]{1,0:T(8,128)(2,1)}, bf16[320,1024]{1,0:T(8,128)(2,1)S(1)}, u32[]{:S(2)}) copy-start(bf16[320,1024]{1,0:T(8,128)(2,1)S(1)} %collective-permute-done.9.refs_2_) | copy-start | bytes 1966084
  71.1 2.4 %collective-permute-start.13 = (bf16[320,1024]{1,0:T(8,128)(2,1)S(1)}, bf16[320,1024]{1,0:T(8,128)(2,1)}, u32[]{:S(2)}, u32[]{:S(2)}) collective-permute-start(bf16[320,1024]{1,0:T(8,128)(2,1)S(1)} %collective-permute-done.9.refs_2_), channel_id=1, source_target_pairs={{0,8},{8,0},{16,24},{24,16},{32,40},{40,32},{48,56},{56,48},{64,72... | collective-permute-start | bytes 1966088 | tf_op jit(solution)/shard_map/ppermute | solution.py:521
  71.6 2.8 %collective-permute-start.14 = (bf16[320,1024]{1,0:T(8,128)(2,1)S(1)}, bf16[320,1024]{1,0:T(8,128)(2,1)}, u32[]{:S(2)}, u32[]{:S(2)}) collective-permute-start(bf16[320,1024]{1,0:T(8,128)(2,1)S(1)} %collective-permute-done.10.refs_3_), channel_id=1, source_target_pairs={{0,8},{8,0},{16,24},{24,16},{32,40},{40,32},{48,56},{56,48},{64,72... | collective-permute-start | bytes 1966088 | tf_op jit(solution)/shard_map/ppermute | solution.py:521
  71.7 2.7 %copy-start.6 = (bf16[320,1024]{1,0:T(8,128)(2,1)}, bf16[320,1024]{1,0:T(8,128)(2,1)S(1)}, u32[]{:S(2)}) copy-start(bf16[320,1024]{1,0:T(8,128)(2,1)S(1)} %collective-permute-done.11.refs_4_) | copy-start | bytes 1966084
  83.8 39.0 %collective-permute-start.15 = (bf16[4,288,640]{2,1,0:T(8,128)(2,1)}, bf16[4,288,640]{2,1,0:T(8,128)(2,1)S(1)}, u32[]{:S(2)}, u32[]{:S(2)}) collective-permute-start(bf16[4,288,640]{2,1,0:T(8,128)(2,1)} %get-tuple-element.90), channel_id=1, source_target_pairs={{0,1},{1,0},{2,3},{3,2},{4,5},{5,4},{6,7},{7,6},{8,9},{9,8},{10,11... | collective-permute-start | bytes 4423688 | tf_op jit(solution)/shard_map/ppermute | solution.py:540
  85.1 33.3 %collective-permute-start.16 = (bf16[2,288,640]{2,1,0:T(8,128)(2,1)}, bf16[2,288,640]{2,1,0:T(8,128)(2,1)S(1)}, u32[]{:S(2)}, u32[]{:S(2)}) collective-permute-start(bf16[2,288,640]{2,1,0:T(8,128)(2,1)} %get-tuple-element.92), channel_id=1, source_target_pairs={{0,2},{1,3},{2,4},{3,5},{4,6},{5,7},{6,0},{7,1},{8,10},{9,11},{10,... | collective-permute-start | bytes 2211848 | tf_op jit(solution)/shard_map/ppermute | solution.py:541
  86.5 34.6 %collective-permute-start.17 = (bf16[2,288,640]{2,1,0:T(8,128)(2,1)}, bf16[2,288,640]{2,1,0:T(8,128)(2,1)}, u32[]{:S(2)}, u32[]{:S(2)}) collective-permute-start(bf16[2,288,640]{2,1,0:T(8,128)(2,1)} %get-tuple-element.93), channel_id=1, source_target_pairs={{0,4},{1,5},{2,6},{3,7},{4,0},{5,1},{6,2},{7,3},{8,12},{9,13},{10,... | collective-permute-start | bytes 2211848 | tf_op jit(solution)/shard_map/ppermute | solution.py:541
  89.1 32.0 %collective-permute-start.18 = (bf16[2,288,640]{2,1,0:T(8,128)(2,1)}, bf16[2,288,640]{2,1,0:T(8,128)(2,1)}, u32[]{:S(2)}, u32[]{:S(2)}) collective-permute-start(bf16[2,288,640]{2,1,0:T(8,128)(2,1)} %get-tuple-element.94), channel_id=1, source_target_pairs={{0,6},{1,7},{2,0},{3,1},{4,2},{5,3},{6,4},{7,5},{8,14},{9,15},{10,... | collective-permute-start | bytes 2211848 | tf_op jit(solution)/shard_map/ppermute | solution.py:541
  100.1 21.0 %copy-start.1 = (bf16[2,288,640]{2,1,0:T(8,128)(2,1)S(1)}, bf16[2,288,640]{2,1,0:T(8,128)(2,1)}, u32[]{:S(2)}) copy-start(bf16[2,288,640]{2,1,0:T(8,128)(2,1)} %get-tuple-element.91) | copy-start | bytes 2211844
  122.8 1.4 copy-start
  125.4 11.6 %collective-permute-start.19 = (bf16[288,640]{1,0:T(8,128)(2,1)}, bf16[288,640]{1,0:T(8,128)(2,1)S(1)}, u32[]{:S(2)}, u32[]{:S(2)}) collective-permute-start(bf16[288,640]{1,0:T(8,128)(2,1)} %get-tuple-element.104), channel_id=1, source_target_pairs={{0,2},{1,3},{2,4},{3,5},{4,6},{5,7},{6,0},{7,1},{8,10},{9,11},{10,... | collective-permute-start | bytes 1105928 | tf_op jit(solution)/shard_map/ppermute | solution.py:550
  126.4 19.3 %collective-permute-start.20 = (bf16[288,640]{1,0:T(8,128)(2,1)}, bf16[288,640]{1,0:T(8,128)(2,1)S(1)}, u32[]{:S(2)}, u32[]{:S(2)}) collective-permute-start(bf16[288,640]{1,0:T(8,128)(2,1)} %get-tuple-element.105), channel_id=1, source_target_pairs={{0,4},{1,5},{2,6},{3,7},{4,0},{5,1},{6,2},{7,3},{8,12},{9,13},{10,... | collective-permute-start | bytes 1105928 | tf_op jit(solution)/shard_map/ppermute | solution.py:550
  129.4 16.3 %collective-permute-start.21 = (bf16[288,640]{1,0:T(8,128)(2,1)S(1)}, bf16[288,640]{1,0:T(8,128)(2,1)S(1)}, u32[]{:S(2)}, u32[]{:S(2)}) collective-permute-start(bf16[288,640]{1,0:T(8,128)(2,1)S(1)} %get-tuple-element.106), channel_id=1, source_target_pairs={{0,6},{1,7},{2,0},{3,1},{4,2},{5,3},{6,4},{7,5},{8,14},{9,15},{10,... | collective-permute-start | bytes 1105928 | tf_op jit(solution)/shard_map/ppermute | solution.py:550
  129.5 17.1 %collective-permute-start.22 = (bf16[288,640]{1,0:T(8,128)(2,1)S(1)}, bf16[288,640]{1,0:T(8,128)(2,1)}, u32[]{:S(2)}, u32[]{:S(2)}) collective-permute-start(bf16[288,640]{1,0:T(8,128)(2,1)S(1)} %get-tuple-element.108), channel_id=1, source_target_pairs={{0,1},{1,0},{2,3},{3,2},{4,5},{5,4},{6,7},{7,6},{8,9},{9,8},{10,11... | collective-permute-start | bytes 1105928 | tf_op jit(solution)/shard_map/ppermute | solution.py:551
  129.7 18.9 %all-to-all-start.1 = ((bf16[16,64,256]{2,1,0:T(8,128)(2,1)}), bf16[16,64,256]{2,1,0:T(8,128)(2,1)S(1)}, u32[]{:S(2)}, u32[]{:S(2)}) async-start(bf16[16,64,256]{2,1,0:T(8,128)(2,1)} %bitcast.17), calls=%async_computation.1 | async-start | bytes 1048576 | tf_op jit(solution)/shard_map/all_to_all | solution.py:554

commit v6 on v5

--- a/solution.py
+++ b/solution.py
@@ -544,9 +544,9 @@
         weights, prompt_weights, inverse, prompt_inverse, reply_query, reply_up, reply_att, prompt_query, prompt_up, prompt_att, kv, reply_key, reply_value
     )
     first = [(kept[dy].astype(F32) + came[dy].astype(F32)).astype(BF) for dy in range(4)]
-    second = turns[0].astype(F32) + turned[0].astype(F32) + turned[1].astype(F32) + turned[2].astype(F32)
+    first, kv_grad, own_turn = lax.optimization_barrier((first, kv_grad, turns[0]))
+    second = own_turn.astype(F32) + turned[0].astype(F32) + turned[1].astype(F32) + turned[2].astype(F32)
     second = second.astype(BF)
-    first, second, kv_grad = lax.optimization_barrier((first, (second[0], second[1]), kv_grad))
     first = [first[0]] + [lax.ppermute(first[dy], "head", head_perm(dy, 0)) for dy in (1, 2, 3)]
     second = second[0].astype(F32) + lax.ppermute(second[1], "head", head_perm(0, 1)).astype(F32)
     first = first[0].astype(F32) + first[1].astype(F32) + first[2].astype(F32) + first[3].astype(F32)

time: 150 us -> 147 us (0.980)
  waiting for transfers between devices: 30.6 us -> 28.6 us
    all_to_all x1, waiting for transfers between devices: 0.01 us -> 4.5 us  [body(): lax.all_to_all(kv_grad.reshape(n_seq, prompt_rows, 2 * DIM), 'seq', 0, 0)]
    ppermute x3, waiting for transfers between devices: 8.76 us -> 4.93 us  [body(): lax.ppermute(first[dy], 'head', head_perm(dy, 0))]
    ppermute x3, waiting for transfers between devices: 2.63 us -> 0.01 us  [body(): lax.ppermute(turns[dy], 'head', head_perm(dy, 0))]
  transfers between devices with their start and end apart: 25 -> 25, of which waited for: 5 -> 6; matrix products, arithmetic and copies ran while one was open for 5% -> 5% of each run, Pallas kernels for 39% -> 40%
where the time goes in v6:
time: 147 us; the launch traced here: 146 us
  Pallas kernels  68.1 us (46%)
  starting transfers between devices  39.2 us (27%)
  waiting for transfers between devices  28.6 us (19%)
  other arithmetic  5.7 us (4%)
  local copies, waits for them, and re-layouts  2.95 us (2%)
  between operations  1.54 us (1%)
    pallas_call x3, Pallas kernels, absorb(): pl.pallas_call(functools.partial(absorb_kernel, project, back, resume), i...  33.7 us
    pallas_call x1, Pallas kernels, attention_backward(): pl.pallas_call(backward_kernel, grid=(steps + 1,), in_specs=[pl.BlockSpec...  18.4 us
    ppermute x15, starting transfers between devices, body(): send = lambda chunk, perm: lax.ppermute(chunk, 'seq', perm)  16.5 us
    all_to_all x1, waiting for transfers between devices, body(): lax.all_to_all(jnp.broadcast_to(own[None], (n_seq,) + own.shape), 'seq',...  16.5 us
    pallas_call x1, Pallas kernels, attention_forward(): pl.pallas_call(forward_kernel, grid=(steps + 1,), in_specs=[pl.BlockSpec(...  15.9 us
    all_to_all x1, starting transfers between devices, body(): lax.all_to_all(kv_grad.reshape(n_seq, prompt_rows, 2 * DIM), 'seq', 0, 0)  6.24 us
    ppermute x3, starting transfers between devices, body(): lax.ppermute(turns[dy], 'head', head_perm(dy, 0))  5 us
    ppermute x3, waiting for transfers between devices, body(): lax.ppermute(first[dy], 'head', head_perm(dy, 0))  4.93 us
  transfers between devices with their start and end apart: 25, of which 6 were waited for; matrix products, arithmetic and copies ran while one was open for 5% of the time, Pallas kernels for 40%

profile of v6, /device:TPU:1, one launch (start us, length us, event | category | flops | bytes accessed | tf_op | source)
XLA Modules:
  0.0 146.1 jit_solution(13298685474046130583)
XLA Ops:
  0.6 0.0 copy-start.8
  0.6 4.7 %collective-permute-start = (bf16[320,1024]{1,0:T(8,128)(2,1)}, bf16[320,1024]{1,0:T(8,128)(2,1)S(1)}, u32[]{:S(2)}, u32[]{:S(2)}) collective-permute-start(bf16[320,1024]{1,0:T(8,128)(2,1)} %bitcast.31), channel_id=1, source_target_pairs={{0,16},{8,56},{16,32},{24,8},{32,48},{40,24},{48,0},{56,40},{64,80... | collective-permute-start | bytes 1966088 | tf_op jit(solution)/shard_map/ppermute | solution.py:521
  5.3 0.0 collective-permute-start.1
  5.3 2.7 %collective-permute-start.2 = (bf16[320,1024]{1,0:T(8,128)(2,1)}, bf16[320,1024]{1,0:T(8,128)(2,1)S(1)}, u32[]{:S(2)}, u32[]{:S(2)}) collective-permute-start(bf16[320,1024]{1,0:T(8,128)(2,1)} %bitcast.33), channel_id=1, source_target_pairs={{0,64},{8,72},{16,80},{24,88},{32,96},{40,104},{48,112},{56,120},{... | collective-permute-start | bytes 1966088 | tf_op jit(solution)/shard_map/ppermute | solution.py:521
  8.0 0.7 pad_maximum_fusion.1
  8.8 0.8 broadcast_in_dim.2
  9.6 4.7 %all-to-all-start = ((bf16[16,64,256]{2,1,0:T(8,128)(2,1)}), bf16[16,64,256]{2,1,0:T(8,128)(2,1)S(1)}, u32[]{:S(2)}, u32[]{:S(2)}) async-start(bf16[16,64,256]{2,1,0:T(8,128)(2,1)} %broadcast_in_dim.2), calls=%async_computation | async-start | bytes 1048576 | tf_op jit(solution)/shard_map/all_to_all | solution.py:519
  14.3 0.3 collective-permute-start.5
  14.6 16.5 %all-to-all-done = bf16[16,64,256]{2,1,0:T(8,128)(2,1)S(1)} async-done(((bf16[16,64,256]{2,1,0:T(8,128)(2,1)}), bf16[16,64,256]{2,1,0:T(8,128)(2,1)S(1)}, u32[]{:S(2)}, u32[]{:S(2)}) %all-to-all-start) | async-done | bytes 524320 | tf_op jit(solution)/shard_map/all_to_all | solution.py:519
  31.1 0.0 collective-permute-done.refs_1_
  31.1 0.0 collective-permute-done.1.refs_2_
  31.1 0.0 collective-permute-done.2.refs_0_
  31.1 0.0 copy-start.2
  31.1 0.5 collective-permute-start.3
  31.6 0.8 collective-permute-start.6
  32.4 2.9 %collective-permute-start.4 = (bf16[320,1024]{1,0:T(8,128)(2,1)S(1)}, bf16[320,1024]{1,0:T(8,128)(2,1)S(1)}, u32[]{:S(2)}, u32[]{:S(2)}) collective-permute-start(bf16[320,1024]{1,0:T(8,128)(2,1)S(1)} %collective-permute-done.2.refs_0_), channel_id=1, source_target_pairs={{0,16},{8,56},{16,32},{24,8},{32,48},{40,24},{48,0},{56,40},{64,80... | collective-permute-start | bytes 1966088 | tf_op jit(solution)/shard_map/ppermute | solution.py:521
  35.2 0.0 collective-permute-start.7
  35.9 15.9 %attention_forward.1 = (bf16[8,1536,512]{2,1,0:T(8,128)(2,1)}, bf16[1024,512]{1,0:T(8,128)(2,1)}, bf16[512,1024]{1,0:T(8,128)(2,1)}, bf16[64,1024]{1,0:T(8,128)(...) custom-call(s32[1]{0:T(128)} %bitcast.9.index_ref, s32[1]{0:T(128)S(6)} %copy.30.length_ref, bf16[512,1024]{1,0:T(8,128)(2,1)} %query_ref.3, ...), custom_call_target="tpu_custom_call" | custom-call | flops 3221225472 | bytes 18874368 | tf_op jit(solution)/shard_map/attention_forward/pallas_call | solution.py:139
  51.9 0.0 collective-permute-done.5.refs_4_
  51.9 0.0 collective-permute-done.3.refs_3_
  51.9 0.0 collective-permute-done.6.refs_5_
  51.9 0.0 collective-permute-done.4.refs_1_
  51.9 0.0 copy-start.3
  51.9 0.0 collective-permute-done.7.refs_6_
  51.9 0.6 collective-permute-start.8
  52.5 0.0 collective-permute-start.10
  52.5 1.5 collective-permute-start.9
  54.0 0.6 pad_add_fusion.order_ref
  54.6 2.0 %collective-permute-start.11 = (bf16[320,1024]{1,0:T(8,128)(2,1)S(1)}, bf16[320,1024]{1,0:T(8,128)(2,1)S(1)}, u32[]{:S(2)}, u32[]{:S(2)}) collective-permute-start(bf16[320,1024]{1,0:T(8,128)(2,1)S(1)} %collective-permute-done.2.refs_0_), channel_id=1, source_target_pairs={{0,8},{8,0},{16,24},{24,16},{32,40},{40,32},{48,56},{56,48},{64,72... | collective-permute-start | bytes 1966088 | tf_op jit(solution)/shard_map/ppermute | solution.py:521
  56.5 0.0 collective-permute-start.12
  56.5 0.0 collective-permute-done.8.refs_7_
  56.5 14.5 %absorb_both.1 = (bf16[4,288,640]{2,1,0:T(8,128)(2,1)}, bf16[4,288,640]{2,1,0:T(8,128)(2,1)}, bf16[2,288,640]{2,1,0:T(8,128)(2,1)}, bf16[2,288,640]{2,1,0:T(8,12...) custom-call(s32[4]{0:T(128)} %pad_add_fusion.order_ref, ...), custom_call_target="tpu_custom_call" | custom-call | flops 6039797760 | bytes 9437184 | tf_op jit(solution)/shard_map/absorb_both/pallas_call | solution.py:474
  71.0 0.0 collective-permute-done.10.refs_3_
  71.1 0.0 collective-permute-done.9.refs_2_
  71.1 0.6 collective-permute-start.13
  71.7 0.1 collective-permute-start.14
  71.8 0.0 collective-permute-done.11.refs_4_
  71.8 1.8 %collective-permute-done.13.refs_6_ = bf16[320,1024]{1,0:T(8,128)(2,1)} collective-permute-done((bf16[320,1024]{1,0:T(8,128)(2,1)S(1)}, bf16[320,1024]{1,0:T(8,128)(2,1)}, u32[]{:S(2)}, u32[]{:S(2)}) %collective-permute-start.13) | collective-permute-done | bytes 655392 | tf_op jit(solution)/shard_map/ppermute | solution.py:521
  73.5 0.9 collective-permute-done.14.refs_7_
  74.5 9.4 %absorb_products.1 = (bf16[4,288,640]{2,1,0:T(8,128)(2,1)}, bf16[4,288,640]{2,1,0:T(8,128)(2,1)}, bf16[2,288,640]{2,1,0:T(8,128)(2,1)}, bf16[2,288,640]{2,1,0:T(...) custom-call(s32[4]{0:T(128)} %pad_add_fusion.order_ref, ...), custom_call_target="tpu_custom_call", output_to_operand_aliasing={{0}: (15, {}), {1}: (16, {}), {2}: (17, {}), {3}: (18, {}),... | custom-call | flops 3019898880 | bytes 9437184 | tf_op jit(solution)/shard_map/absorb_products/pallas_call | solution.py:474
  83.9 1.3 collective-permute-start.15
  85.2 1.3 collective-permute-start.19
  86.5 2.6 %collective-permute-start.20 = (bf16[2,288,640]{2,1,0:T(8,128)(2,1)}, bf16[2,288,640]{2,1,0:T(8,128)(2,1)}, u32[]{:S(2)}, u32[]{:S(2)}) collective-permute-start(bf16[2,288,640]{2,1,0:T(8,128)(2,1)} %get-tuple-element.105), channel_id=1, source_target_pairs={{0,4},{1,5},{2,6},{3,7},{4,0},{5,1},{6,2},{7,3},{8,12},{9,13},{10,... | collective-permute-start | bytes 2211848 | tf_op jit(solution)/shard_map/ppermute | solution.py:541
  89.1 1.1 collective-permute-start.21
  90.2 9.9 %absorb_upstream.1 = (bf16[64,1024]{1,0:T(8,128)(2,1)}, bf16[512,1024]{1,0:T(8,128)(2,1)}) custom-call(s32[4]{0:T(128)} %pad_add_fusion.order_ref, s32[1]{0:T(128)} %bitcast.4.core_ref, s32[1]{0:T(128)} %bitcast.5.head_ref, s32[1]{0:T(128)} %bitcast.6.half_ref, s32[1]{0:T(128)S(6)} %copy.30.length_ref, bf16[320,1024]{1,0:T(8,128)(2,1)} %copy-done.2, ...), custom_call_target="tpu_custom_call" | custom-call | flops 3019898880 | bytes 9437184 | tf_op jit(solution)/shard_map/absorb_upstream/pallas_call | solution.py:474
  100.0 18.4 %attention_backward.1 = (bf16[512,1024]{1,0:T(8,128)(2,1)}, bf16[64,1024]{1,0:T(8,128)(2,1)}, bf16[1024,256]{1,0:T(8,128)(2,1)}, bf16[512,128]{1,0:T(8,128)(2,1)}, bf16[512,128]{1,0:T(8,128)(2,1)}) custom-call(bf16[8,1536,512]{2,1,0:T(8,128)(2,1)} %get-tuple-element.90.weight_ref, bf16[1024,512]{1,0:T(8,128)(2,1)} %get-tuple-element.91.prompt_weight_ref, ...), custom_call_target="tpu_custom_call" | custom-call | flops 6442450944 | bytes 18874368 | tf_op jit(solution)/shard_map/attention_backward/pallas_call | solution.py:270
  118.5 1.2 fusion.4
  119.7 0.6 collective-permute-start.16
  120.3 2.6 %collective-permute-start.17 = (bf16[288,640]{1,0:T(8,128)(2,1)}, bf16[288,640]{1,0:T(8,128)(2,1)S(1)}, u32[]{:S(2)}, u32[]{:S(2)}) collective-permute-start(bf16[288,640]{1,0:T(8,128)(2,1)} %get-tuple-element.101), channel_id=1, source_target_pairs={{0,4},{1,5},{2,6},{3,7},{4,0},{5,1},{6,2},{7,3},{8,12},{9,13},{10,... | collective-permute-start | bytes 1105928 | tf_op jit(solution)/shard_map/ppermute | solution.py:550
  122.9 1.1 collective-permute-start.18
  123.9 0.0 collective-permute-done.20
  123.9 1.9 %add_convert_fusion = bf16[2,288,640]{2,1,0:T(8,128)(2,1)S(1)} fusion(bf16[2,288,640]{2,1,0:T(8,128)(2,1)} %collective-permute-done.21, bf16[2,288,640]{2,1,0:T(8,128)(2,1)} %collective-permute-done.20, bf16[2,288,640]{2,1,0:T(8,128)(2,1)} %collective-permute-done.19, bf16[2,288,640]{2,1,0:T(8,128)(2,1)S(1)} %copy-done.1), kind=kLoop, calls=%fused_computation | loop fusion | flops 2949120 | bytes 3686400 | tf_op jit(solution)/shard_map/convert_element_type | solution.py:549
  125.9 0.8 slice_bitcast_fusion
  126.6 1.2 collective-permute-start.22
  127.9 6.2 %all-to-all-start.1 = ((bf16[16,64,256]{2,1,0:T(8,128)(2,1)}), bf16[16,64,256]{2,1,0:T(8,128)(2,1)S(1)}, u32[]{:S(2)}, u32[]{:S(2)}) async-start(bf16[16,64,256]{2,1,0:T(8,128)(2,1)} %bitcast.17), calls=%async_computation.1 | async-start | bytes 1048576 | tf_op jit(solution)/shard_map/all_to_all | solution.py:554
  134.1 4.3 %collective-permute-done.17 = bf16[288,640]{1,0:T(8,128)(2,1)S(1)} collective-permute-done((bf16[288,640]{1,0:T(8,128)(2,1)}, bf16[288,640]{1,0:T(8,128)(2,1)S(1)}, u32[]{:S(2)}, u32[]{:S(2)}) %collective-permute-start.17) | collective-permute-done | bytes 368672 | tf_op jit(solution)/shard_map/ppermute | solution.py:550
  138.4 0.6 collective-permute-done.18
  139.1 0.2 add_convert_fusion.1
  139.3 0.6 slice.60
  139.9 0.1 fusion
  140.0 0.9 pad_maximum_fusion
  140.9 4.5 %all-to-all-done.1 = bf16[16,64,256]{2,1,0:T(8,128)(2,1)S(1)} async-done(((bf16[16,64,256]{2,1,0:T(8,128)(2,1)}), bf16[16,64,256]{2,1,0:T(8,128)(2,1)S(1)}, u32[]{:S(2)}, u32[]{:S(2)}) %all-to-all-start.1) | async-done | bytes 524320 | tf_op jit(solution)/shard_map/all_to_all | solution.py:554
  145.4 0.1 reduce_sum.12
  145.5 0.6 fusion.5
  (24 shorter events, 0.1 us)
Async XLA Ops:
  0.6 13.7 %copy-start.8 = (bf16[1024,320]{0,1:T(8,128)(2,1)S(1)}, bf16[1024,320]{0,1:T(8,128)(2,1)}, u32[]{:S(2)}) copy-start(bf16[1024,320]{0,1:T(8,128)(2,1)} %param.17) | copy-start | bytes 1966084
  0.6 30.4 %collective-permute-start = (bf16[320,1024]{1,0:T(8,128)(2,1)}, bf16[320,1024]{1,0:T(8,128)(2,1)S(1)}, u32[]{:S(2)}, u32[]{:S(2)}) collective-permute-start(bf16[320,1024]{1,0:T(8,128)(2,1)} %bitcast.31), channel_id=1, source_target_pairs={{0,16},{8,56},{16,32},{24,8},{32,48},{40,24},{48,0},{56,40},{64,80... | collective-permute-start | bytes 1966088 | tf_op jit(solution)/shard_map/ppermute | solution.py:521
  5.3 25.8 %collective-permute-start.1 = (bf16[320,1024]{1,0:T(8,128)(2,1)}, bf16[320,1024]{1,0:T(8,128)(2,1)}, u32[]{:S(2)}, u32[]{:S(2)}) collective-permute-start(bf16[320,1024]{1,0:T(8,128)(2,1)} %bitcast.32), channel_id=1, source_target_pairs={{0,48},{8,24},{16,0},{24,40},{32,16},{40,56},{48,32},{56,8},{64,11... | collective-permute-start | bytes 1966088 | tf_op jit(solution)/shard_map/ppermute | solution.py:521
  5.3 25.8 %collective-permute-start.2 = (bf16[320,1024]{1,0:T(8,128)(2,1)}, bf16[320,1024]{1,0:T(8,128)(2,1)S(1)}, u32[]{:S(2)}, u32[]{:S(2)}) collective-permute-start(bf16[320,1024]{1,0:T(8,128)(2,1)} %bitcast.33), channel_id=1, source_target_pairs={{0,64},{8,72},{16,80},{24,88},{32,96},{40,104},{48,112},{56,120},{... | collective-permute-start | bytes 1966088 | tf_op jit(solution)/shard_map/ppermute | solution.py:521
  9.6 21.4 %all-to-all-start = ((bf16[16,64,256]{2,1,0:T(8,128)(2,1)}), bf16[16,64,256]{2,1,0:T(8,128)(2,1)S(1)}, u32[]{:S(2)}, u32[]{:S(2)}) async-start(bf16[16,64,256]{2,1,0:T(8,128)(2,1)} %broadcast_in_dim.2), calls=%async_computation | async-start | bytes 1048576 | tf_op jit(solution)/shard_map/all_to_all | solution.py:519
  14.3 37.5 %collective-permute-start.5 = (bf16[320,1024]{1,0:T(8,128)(2,1)S(1)}, bf16[320,1024]{1,0:T(8,128)(2,1)}, u32[]{:S(2)}, u32[]{:S(2)}) collective-permute-start(bf16[320,1024]{1,0:T(8,128)(2,1)S(1)} %bitcast.35), channel_id=1, source_target_pairs={{0,8},{8,0},{16,24},{24,16},{32,40},{40,32},{48,56},{56,48},{64,72... | collective-permute-start | bytes 1966088 | tf_op jit(solution)/shard_map/ppermute | solution.py:521
  31.1 4.8 %copy-start.7 = (bf16[16,64,256]{2,1,0:T(8,128)(2,1)}, bf16[16,64,256]{2,1,0:T(8,128)(2,1)S(1)}, u32[]{:S(2)}) copy-start(bf16[16,64,256]{2,1,0:T(8,128)(2,1)S(1)} %all-to-all-done) | copy-start | bytes 1572868
  31.1 20.8 %copy-start.9 = (bf16[320,1024]{1,0:T(8,128)(2,1)}, bf16[320,1024]{1,0:T(8,128)(2,1)S(1)}, u32[]{:S(2)}) copy-start(bf16[320,1024]{1,0:T(8,128)(2,1)S(1)} %collective-permute-done.refs_1_) | copy-start | bytes 1966084
  31.1 23.5 %copy-start.2 = (bf16[320,1024]{1,0:T(8,128)(2,1)}, bf16[320,1024]{1,0:T(8,128)(2,1)S(1)}, u32[]{:S(2)}) copy-start(bf16[320,1024]{1,0:T(8,128)(2,1)S(1)} %collective-permute-done.2.refs_0_) | copy-start | bytes 1966084
  31.1 20.8 %collective-permute-start.3 = (bf16[320,1024]{1,0:T(8,128)(2,1)S(1)}, bf16[320,1024]{1,0:T(8,128)(2,1)}, u32[]{:S(2)}, u32[]{:S(2)}) collective-permute-start(bf16[320,1024]{1,0:T(8,128)(2,1)S(1)} %collective-permute-done.refs_1_), channel_id=1, source_target_pairs={{0,16},{8,56},{16,32},{24,8},{32,48},{40,24},{48,0},{56,40},{64,80... | collective-permute-start | bytes 1966088 | tf_op jit(solution)/shard_map/ppermute | solution.py:521
  31.6 20.3 %collective-permute-start.6 = (bf16[320,1024]{1,0:T(8,128)(2,1)S(1)}, bf16[320,1024]{1,0:T(8,128)(2,1)}, u32[]{:S(2)}, u32[]{:S(2)}) collective-permute-start(bf16[320,1024]{1,0:T(8,128)(2,1)S(1)} %collective-permute-done.refs_1_), channel_id=1, source_target_pairs={{0,8},{8,0},{16,24},{24,16},{32,40},{40,32},{48,56},{56,48},{64,72... | collective-permute-start | bytes 1966088 | tf_op jit(solution)/shard_map/ppermute | solution.py:521
  32.4 19.5 %collective-permute-start.4 = (bf16[320,1024]{1,0:T(8,128)(2,1)S(1)}, bf16[320,1024]{1,0:T(8,128)(2,1)S(1)}, u32[]{:S(2)}, u32[]{:S(2)}) collective-permute-start(bf16[320,1024]{1,0:T(8,128)(2,1)S(1)} %collective-permute-done.2.refs_0_), channel_id=1, source_target_pairs={{0,16},{8,56},{16,32},{24,8},{32,48},{40,24},{48,0},{56,40},{64,80... | collective-permute-start | bytes 1966088 | tf_op jit(solution)/shard_map/ppermute | solution.py:521
  35.2 16.7 %collective-permute-start.7 = (bf16[320,1024]{1,0:T(8,128)(2,1)}, bf16[320,1024]{1,0:T(8,128)(2,1)}, u32[]{:S(2)}, u32[]{:S(2)}) collective-permute-start(bf16[320,1024]{1,0:T(8,128)(2,1)} %collective-permute-done.1.refs_2_), channel_id=1, source_target_pairs={{0,8},{8,0},{16,24},{24,16},{32,40},{40,32},{48,56},{56,48},{64,72... | collective-permute-start | bytes 1966088 | tf_op jit(solution)/shard_map/ppermute | solution.py:521
  51.9 19.1 %copy-start.3 = (bf16[320,1024]{1,0:T(8,128)(2,1)}, bf16[320,1024]{1,0:T(8,128)(2,1)S(1)}, u32[]{:S(2)}) copy-start(bf16[320,1024]{1,0:T(8,128)(2,1)S(1)} %collective-permute-done.4.refs_1_) | copy-start | bytes 1966084
  51.9 4.6 %collective-permute-start.8 = (bf16[320,1024]{1,0:T(8,128)(2,1)}, bf16[320,1024]{1,0:T(8,128)(2,1)}, u32[]{:S(2)}, u32[]{:S(2)}) collective-permute-start(bf16[320,1024]{1,0:T(8,128)(2,1)} %collective-permute-done.3.refs_3_), channel_id=1, source_target_pairs={{0,8},{8,0},{16,24},{24,16},{32,40},{40,32},{48,56},{56,48},{64,72... | collective-permute-start | bytes 1966088 | tf_op jit(solution)/shard_map/ppermute | solution.py:521
  52.5 18.5 %collective-permute-start.10 = (bf16[320,1024]{1,0:T(8,128)(2,1)S(1)}, bf16[320,1024]{1,0:T(8,128)(2,1)S(1)}, u32[]{:S(2)}, u32[]{:S(2)}) collective-permute-start(bf16[320,1024]{1,0:T(8,128)(2,1)S(1)} %collective-permute-done.4.refs_1_), channel_id=1, source_target_pairs={{0,16},{8,56},{16,32},{24,8},{32,48},{40,24},{48,0},{56,40},{64,80... | collective-permute-start | bytes 1966088 | tf_op jit(solution)/shard_map/ppermute | solution.py:521
  52.5 18.5 %collective-permute-start.9 = (bf16[320,1024]{1,0:T(8,128)(2,1)S(1)}, bf16[320,1024]{1,0:T(8,128)(2,1)S(1)}, u32[]{:S(2)}, u32[]{:S(2)}) collective-permute-start(bf16[320,1024]{1,0:T(8,128)(2,1)S(1)} %collective-permute-done.2.refs_0_), channel_id=1, source_target_pairs={{0,48},{8,24},{16,0},{24,40},{32,16},{40,56},{48,32},{56,8},{64,11... | collective-permute-start | bytes 1966088 | tf_op jit(solution)/shard_map/ppermute | solution.py:521
  54.6 17.2 %collective-permute-start.11 = (bf16[320,1024]{1,0:T(8,128)(2,1)S(1)}, bf16[320,1024]{1,0:T(8,128)(2,1)S(1)}, u32[]{:S(2)}, u32[]{:S(2)}) collective-permute-start(bf16[320,1024]{1,0:T(8,128)(2,1)S(1)} %collective-permute-done.2.refs_0_), channel_id=1, source_target_pairs={{0,8},{8,0},{16,24},{24,16},{32,40},{40,32},{48,56},{56,48},{64,72... | collective-permute-start | bytes 1966088 | tf_op jit(solution)/shard_map/ppermute | solution.py:521
  56.5 15.2 %collective-permute-start.12 = (bf16[320,1024]{1,0:T(8,128)(2,1)S(1)}, bf16[320,1024]{1,0:T(8,128)(2,1)}, u32[]{:S(2)}, u32[]{:S(2)}) collective-permute-start(bf16[320,1024]{1,0:T(8,128)(2,1)S(1)} %collective-permute-done.4.refs_1_), channel_id=1, source_target_pairs={{0,8},{8,0},{16,24},{24,16},{32,40},{40,32},{48,56},{56,48},{64,72... | collective-permute-start | bytes 1966088 | tf_op jit(solution)/shard_map/ppermute | solution.py:521
  71.1 3.4 %copy-start.4 = (bf16[320,1024]{1,0:T(8,128)(2,1)}, bf16[320,1024]{1,0:T(8,128)(2,1)S(1)}, u32[]{:S(2)}) copy-start(bf16[320,1024]{1,0:T(8,128)(2,1)S(1)} %collective-permute-done.10.refs_3_) | copy-start | bytes 1966084
  71.1 3.4 %copy-start.5 = (bf16[320,1024]{1,0:T(8,128)(2,1)}, bf16[320,1024]{1,0:T(8,128)(2,1)S(1)}, u32[]{:S(2)}) copy-start(bf16[320,1024]{1,0:T(8,128)(2,1)S(1)} %collective-permute-done.9.refs_2_) | copy-start | bytes 1966084
  71.1 2.4 %collective-permute-start.13 = (bf16[320,1024]{1,0:T(8,128)(2,1)S(1)}, bf16[320,1024]{1,0:T(8,128)(2,1)}, u32[]{:S(2)}, u32[]{:S(2)}) collective-permute-start(bf16[320,1024]{1,0:T(8,128)(2,1)S(1)} %collective-permute-done.9.refs_2_), channel_id=1, source_target_pairs={{0,8},{8,0},{16,24},{24,16},{32,40},{40,32},{48,56},{56,48},{64,72... | collective-permute-start | bytes 1966088 | tf_op jit(solution)/shard_map/ppermute | solution.py:521
  71.7 2.8 %collective-permute-start.14 = (bf16[320,1024]{1,0:T(8,128)(2,1)S(1)}, bf16[320,1024]{1,0:T(8,128)(2,1)}, u32[]{:S(2)}, u32[]{:S(2)}) collective-permute-start(bf16[320,1024]{1,0:T(8,128)(2,1)S(1)} %collective-permute-done.10.refs_3_), channel_id=1, source_target_pairs={{0,8},{8,0},{16,24},{24,16},{32,40},{40,32},{48,56},{56,48},{64,72... | collective-permute-start | bytes 1966088 | tf_op jit(solution)/shard_map/ppermute | solution.py:521
  71.8 2.7 %copy-start.6 = (bf16[320,1024]{1,0:T(8,128)(2,1)}, bf16[320,1024]{1,0:T(8,128)(2,1)S(1)}, u32[]{:S(2)}) copy-start(bf16[320,1024]{1,0:T(8,128)(2,1)S(1)} %collective-permute-done.11.refs_4_) | copy-start | bytes 1966084
  83.9 34.6 %collective-permute-start.15 = (bf16[4,288,640]{2,1,0:T(8,128)(2,1)}, bf16[4,288,640]{2,1,0:T(8,128)(2,1)S(1)}, u32[]{:S(2)}, u32[]{:S(2)}) collective-permute-start(bf16[4,288,640]{2,1,0:T(8,128)(2,1)} %get-tuple-element.89), channel_id=1, source_target_pairs={{0,1},{1,0},{2,3},{3,2},{4,5},{5,4},{6,7},{7,6},{8,9},{9,8},{10,11... | collective-permute-start | bytes 4423688 | tf_op jit(solution)/shard_map/ppermute | solution.py:540
  85.2 37.7 %collective-permute-start.19 = (bf16[2,288,640]{2,1,0:T(8,128)(2,1)}, bf16[2,288,640]{2,1,0:T(8,128)(2,1)}, u32[]{:S(2)}, u32[]{:S(2)}) collective-permute-start(bf16[2,288,640]{2,1,0:T(8,128)(2,1)} %get-tuple-element.104), channel_id=1, source_target_pairs={{0,2},{1,3},{2,4},{3,5},{4,6},{5,7},{6,0},{7,1},{8,10},{9,11},{10,... | collective-permute-start | bytes 2211848 | tf_op jit(solution)/shard_map/ppermute | solution.py:541
  86.5 37.5 %collective-permute-start.20 = (bf16[2,288,640]{2,1,0:T(8,128)(2,1)}, bf16[2,288,640]{2,1,0:T(8,128)(2,1)}, u32[]{:S(2)}, u32[]{:S(2)}) collective-permute-start(bf16[2,288,640]{2,1,0:T(8,128)(2,1)} %get-tuple-element.105), channel_id=1, source_target_pairs={{0,4},{1,5},{2,6},{3,7},{4,0},{5,1},{6,2},{7,3},{8,12},{9,13},{10,... | collective-permute-start | bytes 2211848 | tf_op jit(solution)/shard_map/ppermute | solution.py:541
  89.1 34.9 %collective-permute-start.21 = (bf16[2,288,640]{2,1,0:T(8,128)(2,1)}, bf16[2,288,640]{2,1,0:T(8,128)(2,1)}, u32[]{:S(2)}, u32[]{:S(2)}) collective-permute-start(bf16[2,288,640]{2,1,0:T(8,128)(2,1)} %get-tuple-element.106), channel_id=1, source_target_pairs={{0,6},{1,7},{2,0},{3,1},{4,2},{5,3},{6,4},{7,5},{8,14},{9,15},{10,... | collective-permute-start | bytes 2211848 | tf_op jit(solution)/shard_map/ppermute | solution.py:541
  100.0 18.4 %copy-start = (bf16[4,288,640]{2,1,0:T(8,128)(2,1)S(1)}, bf16[4,288,640]{2,1,0:T(8,128)(2,1)}, u32[]{:S(2)}) copy-start(bf16[4,288,640]{2,1,0:T(8,128)(2,1)} %get-tuple-element.88) | copy-start | bytes 4423684
  118.5 5.5 %copy-start.1 = (bf16[2,288,640]{2,1,0:T(8,128)(2,1)S(1)}, bf16[2,288,640]{2,1,0:T(8,128)(2,1)}, u32[]{:S(2)}) copy-start(bf16[2,288,640]{2,1,0:T(8,128)(2,1)} %get-tuple-element.103) | copy-start | bytes 2211844
  119.7 14.5 %collective-permute-start.16 = (bf16[288,640]{1,0:T(8,128)(2,1)}, bf16[288,640]{1,0:T(8,128)(2,1)S(1)}, u32[]{:S(2)}, u32[]{:S(2)}) collective-permute-start(bf16[288,640]{1,0:T(8,128)(2,1)} %get-tuple-element.100), channel_id=1, source_target_pairs={{0,2},{1,3},{2,4},{3,5},{4,6},{5,7},{6,0},{7,1},{8,10},{9,11},{10,... | collective-permute-start | bytes 1105928 | tf_op jit(solution)/shard_map/ppermute | solution.py:550
  120.3 18.2 %collective-permute-start.17 = (bf16[288,640]{1,0:T(8,128)(2,1)}, bf16[288,640]{1,0:T(8,128)(2,1)S(1)}, u32[]{:S(2)}, u32[]{:S(2)}) collective-permute-start(bf16[288,640]{1,0:T(8,128)(2,1)} %get-tuple-element.101), channel_id=1, source_target_pairs={{0,4},{1,5},{2,6},{3,7},{4,0},{5,1},{6,2},{7,3},{8,12},{9,13},{10,... | collective-permute-start | bytes 1105928 | tf_op jit(solution)/shard_map/ppermute | solution.py:550
  122.9 16.2 %collective-permute-start.18 = (bf16[288,640]{1,0:T(8,128)(2,1)S(1)}, bf16[288,640]{1,0:T(8,128)(2,1)S(1)}, u32[]{:S(2)}, u32[]{:S(2)}) collective-permute-start(bf16[288,640]{1,0:T(8,128)(2,1)S(1)} %get-tuple-element.102), channel_id=1, source_target_pairs={{0,6},{1,7},{2,0},{3,1},{4,2},{5,3},{6,4},{7,5},{8,14},{9,15},{10,... | collective-permute-start | bytes 1105928 | tf_op jit(solution)/shard_map/ppermute | solution.py:550
  126.6 13.3 %collective-permute-start.22 = (bf16[288,640]{1,0:T(8,128)(2,1)}, bf16[288,640]{1,0:T(8,128)(2,1)S(1)}, u32[]{:S(2)}, u32[]{:S(2)}) collective-permute-start(bf16[288,640]{1,0:T(8,128)(2,1)} %slice_bitcast_fusion), channel_id=1, source_target_pairs={{0,1},{1,0},{2,3},{3,2},{4,5},{5,4},{6,7},{7,6},{8,9},{9,8},{10,11... | collective-permute-start | bytes 1105928 | tf_op jit(solution)/shard_map/ppermute | solution.py:551
  127.9 17.5 %all-to-all-start.1 = ((bf16[16,64,256]{2,1,0:T(8,128)(2,1)}), bf16[16,64,256]{2,1,0:T(8,128)(2,1)S(1)}, u32[]{:S(2)}, u32[]{:S(2)}) async-start(bf16[16,64,256]{2,1,0:T(8,128)(2,1)} %bitcast.17), calls=%async_computation.1 | async-start | bytes 1048576 | tf_op jit(solution)/shard_map/all_to_all | solution.py:554
